TPU v7x, 32 devices: a whole 2x2x4 slice. The times are simulated.
32 devices in a mesh: runs: 2 (over x), gy: 16 (over z, y, core).
Axes of the slice: x: 2, y: 2, z: 4, core: 2. Of those that a mesh axis runs over, the one named last changes fastest.
Arguments:
- depth: float32 [1024, 1920], P(('runs', 'gy')), parts along dimension 0, may hold values from 0.02 to 3
- flux_east: float32 [1024, 1920], P(('runs', 'gy')), parts along dimension 0, may hold values from -2 to 2
- flux_south: float32 [1024, 1920], P(('runs', 'gy')), parts along dimension 0, may hold values from -2 to 2
- river_section: float32 [4096], P(('runs', 'gy')), parts along dimension 0, may hold values from 0 to 2
- bed_level: float32 [512, 1920], P('gy'), may hold values from -3 to 3
- rough_class: int32 [512, 1920], P('gy'), may hold values from 0 to 7
- manning_table: float32 [8], replicated, may hold values from 0.02 to 0.15
- bank_cell: int32 [4, 2048], P(None, 'gy'), may hold values from 0 to 983039, as said below
Outputs:
- depth_out: float32 [1024, 1920], P(('runs', 'gy')), parts along dimension 0
- east_out: float32 [1024, 1920], P(('runs', 'gy')), parts along dimension 0
- south_out: float32 [1024, 1920], P(('runs', 'gy')), parts along dimension 0
- section_out: float32 [4096], P(('runs', 'gy')), parts along dimension 0
There are 2 independent parts, one for each index of `runs`. A program takes and returns all parts, laid end to end along the dimension named above; an argument that names none is the same for every part. Nothing has to cross between parts.
Inputs may be any that keep to these rules, and one draw needn't show every extreme that they name: `bank_cell`: the 4 corridor cells of a node are consecutive flat indices row * 1920 + column within one map row. Node n is owned by gy index o = n // 128, and all its corridor cells lie in map rows from max((o - 1) * 32, 0) to min((o + 2) * 32, 512) - 1.
All inputs are finite; a program needn't handle non-finite values.
Results may differ from a plain program's by a relative error of at most 0.00013.
Values sent between devices are 32-bit elements; how exact they have to be, the bound alone decides.
No kernel may reach another device: no remote copies, remote signals or barrier semaphores. Data moves between devices by JAX's collectives and lax.ppermute only.
A program may use at most 64 MiB of HBM per device.

v0:
```python
import functools

import jax
import jax.numpy as jnp
from jax import lax
from jax.experimental import pallas as pl
from jax.experimental.pallas import tpu as pltpu
from jax.sharding import PartitionSpec as P

STEPS = 4

GRAV = 9.81
TSTEP = 8.0
CELL = 90.0
FLOOR = 0.05
BANK_COEF = 200.0
CELL_AREA = 8100.0
NODE_AREA = 20000.0

LANES = 128
HALO = 4
SLOPE = GRAV * TSTEP / CELL
SPREAD = TSTEP / CELL
FEED = TSTEP * BANK_COEF / CELL_AREA
DRAIN = TSTEP * BANK_COEF / NODE_AREA
VMEM_LIMIT = 32 * 1024 * 1024

VMEM_SPEC = pl.BlockSpec(memory_space=pltpu.VMEM)
HBM_SPEC = pl.BlockSpec(memory_space=pltpu.HBM)


def swapped(value, first):
    count = lax.axis_size("gy")
    pairs = []
    for low in range(first, count - 1, 2):
        pairs += [(low, low + 1), (low + 1, low)]
    return lax.ppermute(value, "gy", pairs)


def cols(chunk):
    return slice(chunk * LANES, (chunk + 1) * LANES)


def lanes_of(rows):
    return lax.broadcasted_iota(jnp.int32, (rows, LANES), 1)


def moved_left(value, following, by):
    return jnp.where(
        lanes_of(value.shape[0]) >= LANES - by,
        pltpu.roll(following, LANES - by, 1),
        pltpu.roll(value, LANES - by, 1),
    )


def moved_up(value):
    return pltpu.roll(value, value.shape[0] - 1, 0)


def split3(value):
    high = value.astype(jnp.bfloat16)
    rest = value - high.astype(jnp.float32)
    middle = rest.astype(jnp.bfloat16)
    low = (rest - middle.astype(jnp.float32)).astype(jnp.bfloat16)
    return high, middle, low


def one_hot(count, key):
    rows = lax.broadcasted_iota(jnp.int32, (count, key.shape[1]), 0)
    return jnp.where(rows == key, 1.0, 0.0)


def drag_of(mann_a, mann_b):
    pair = mann_a + mann_b
    return (0.25 * GRAV * TSTEP * SLOPE) * (pair * pair)


def looked_up(klass, entries):
    value = jnp.broadcast_to(entries[0], klass.shape)
    for k in range(1, len(entries)):
        value = jnp.where(klass == k, entries[k], value)
    return value


def face(flux, surf_a, surf_b, bed_max, drag):
    flow_depth = jnp.maximum(jnp.maximum(surf_a, surf_b) - bed_max, FLOOR)
    power = jnp.exp2((-7.0 / 3.0) * jnp.log2(flow_depth))
    driven = flux - flow_depth * (surf_b - surf_a)
    damping = 1.0 + drag * jnp.abs(flux) * power
    return driven * pl.reciprocal(damping, approx=True)


def window_sums(blocks, reach, forward):
    height = blocks[0].shape[0]
    count = len(blocks)
    spare = -(count * height) % 16
    whole = blocks + ([jnp.zeros((spare, LANES), jnp.float32)] if spare else [])
    whole = jnp.concatenate(whole, axis=0)
    high = whole.astype(jnp.bfloat16)
    low = (whole - high.astype(jnp.float32)).astype(jnp.bfloat16)
    source = lax.broadcasted_iota(jnp.int32, (2 * LANES, 2 * LANES), 0) % LANES
    target = lax.broadcasted_iota(jnp.int32, (2 * LANES, 2 * LANES), 1)
    spill = target >= LANES
    target = target % LANES
    if forward:
        ahead = source - target + jnp.where(spill, LANES, 0)
    else:
        ahead = target - source + jnp.where(spill, LANES, 0)
    band = jnp.where((ahead >= 0) & (ahead < reach), 1.0, 0.0).astype(jnp.bfloat16)
    sums = jnp.dot(
        jnp.concatenate([high, low], axis=1), band, preferred_element_type=jnp.float32
    )
    results = []
    for block in range(count):
        result = sums[block * height : (block + 1) * height, :LANES]
        beside = block + 1 if forward else block - 1
        if 0 <= beside < count:
            result = result + sums[beside * height : (beside + 1) * height, LANES:]
        results.append(result)
    return results


def east_walled(value, chunk, chunks):
    if chunk + 1 < chunks:
        return value
    return jnp.where(lanes_of(value.shape[0]) == LANES - 1, 0.0, value)


def located(cell, position, rows, ext, columns):
    base = ((position * rows - HALO) * columns + 1).astype(jnp.float32)
    offset = cell - base
    valid = (cell > 0.0) & (offset >= 0.0) & (offset < float(ext * columns))
    offset = jnp.where(valid, offset, 0.0)
    row = jnp.floor((offset + 0.5) * (1.0 / columns))
    column = (offset - row * float(columns)).astype(jnp.int32)
    row = row.astype(jnp.int32) - HALO
    row = jnp.where(row < 0, row + ext, row)
    chunk = column // LANES
    return valid, row, chunk, column - chunk * LANES


def scattered(section, key, lane, count):
    at_lane = one_hot(LANES, lane)
    parts = [at_lane] + [at_lane * part.astype(jnp.float32) for part in split3(section)]
    grid = lax.dot_general(
        one_hot(-(-count // 16) * 16, key).astype(jnp.bfloat16),
        jnp.concatenate(parts, axis=0).astype(jnp.bfloat16),
        (((1,), (1,)), ((), ())),
        preferred_element_type=jnp.float32,
    )
    number = grid[:, :LANES]
    total = (grid[:, LANES : 2 * LANES] + grid[:, 2 * LANES : 3 * LANES]) + grid[:, 3 * LANES :]
    return number, total


def border_rows(of_first, fields, south):
    outer = lax.broadcasted_iota(jnp.int32, (HALO, LANES), 0) == jnp.where(of_first, HALO - 1, 0)
    flux = jnp.where(of_first, south[:HALO], south[HALO:])
    return [
        jnp.where(outer, flux[slot : slot + 1], jnp.where(of_first, value[:HALO], value[HALO:]))
        for slot, value in enumerate(fields)
    ]


def pack_kernel(
    depth, bed, rough, east, south, section, cells, table_in, to_other, own, *refs
):
    held, held_rough, held_cells, table, sems = refs
    rows, columns = depth.shape
    chunks = columns // LANES
    even = lax.axis_index("gy") % 2 == 0
    start = pl.multiple_of(jnp.where(even, 0, rows - 8), 8)
    near = pl.ds(start, 8)
    copies = [
        pltpu.make_async_copy(source, target, sems.at[slot])
        for slot, (source, target) in enumerate(
            (
                (rough.at[near, :], held_rough),
                (bed.at[near, :], held.at[1]),
                (depth.at[near, :], held.at[0]),
                (east.at[near, :], held.at[2]),
                (south.at[near, :], held.at[3]),
                (section, own.at[pl.ds(0, 1), :]),
                (cells, held_cells),
                (table_in, table),
            )
        )
    ]
    for copy in copies:
        copy.start()
    for copy in copies:
        copy.wait()
    own[1:2, :] = (held_cells[0:1, :] + 1).astype(jnp.float32)
    entries = [
        jnp.broadcast_to(table[:, k : k + 1], (1, LANES)) for k in range(table.shape[1])
    ]
    manns = [looked_up(held_rough[:, cols(chunk)], entries) for chunk in range(chunks)]
    row = lax.broadcasted_iota(jnp.int32, (8, LANES), 0)
    beds = [held[1, :, cols(chunk)] for chunk in range(chunks)]
    surfs = [held[0, :, cols(chunk)] + beds[chunk] for chunk in range(chunks)]

    def moved(values):
        rolled = [pltpu.roll(value, LANES - 1, 1) for value in values]
        rolled.append(rolled[-1])
        edge = lanes_of(8) == LANES - 1
        return [jnp.where(edge, rolled[c + 1], rolled[c]) for c in range(chunks)]

    beds_left, surfs_left, manns_left = moved(beds), moved(surfs), moved(manns)
    for chunk in range(chunks):
        at = cols(chunk)
        m0, b0, s0 = manns[chunk], beds[chunk], surfs[chunk]
        bed_max = jnp.maximum(b0, beds_left[chunk])
        drag = drag_of(m0, manns_left[chunk])
        q0 = (1.0 / SLOPE) * held[2, :, at]
        new_east = face(q0, s0, surfs_left[chunk], bed_max, drag)
        new_east = east_walled(new_east, chunk, chunks)
        bed_max = jnp.maximum(b0, moved_up(b0))
        drag = drag_of(m0, moved_up(m0))
        q0 = (1.0 / SLOPE) * held[3, :, at]
        new_south = jnp.where(row == 7, q0, face(q0, s0, moved_up(s0), bed_max, drag))
        fields = (s0, b0, held_rough[:, at].astype(jnp.float32), new_east)
        for slot, block in enumerate(border_rows(even, fields, new_south)):
            to_other[slot * chunks + chunk] = block
    to_other[4 * chunks, 0:2, :] = own[...]


def join_kernel(before, section, cells, to_other):
    nodes = to_other.shape[0] - 1
    to_other[nodes, 2:3, :] = section[...]
    to_other[nodes, 3:4, :] = (cells[0:1, :] + 1).astype(jnp.float32)


def relay_kernel(by_other, prepared, near):
    del prepared
    near[...] = by_other[by_other.shape[0] - 1, 0:2, :]


def picking(reach, rows, key, lane, takes, masks):
    for block in range(key.shape[1] // LANES):
        mine = slice(block * LANES, (block + 1) * LANES)

        def column(row):
            wide = jnp.broadcast_to(row[:, mine].astype(jnp.float32), (LANES, LANES))
            return jnp.transpose(wide).astype(jnp.int32)

        spread = lanes_of(LANES)
        at = column(key)
        after = jnp.where(at < 0, at, at + rows)
        for first in range(0, takes.shape[2], LANES):
            for half, place in enumerate((at, after)):
                hit = jnp.where(spread + first == place, 1.0, 0.0)
                takes[half, mine, first : first + LANES] = hit.astype(jnp.bfloat16)
        ahead = spread - column(lane)
        masks[0, mine, :] = jnp.where((ahead >= 0) & (ahead < reach), 1.0, 0.0)
        masks[1, mine, :] = jnp.where(ahead + LANES < reach, 1.0, 0.0)


def load_kernel(
    depth_in, east_in, south_in, bed_in, rough_in, table_in, *refs
):
    surf, east, south, bed, rough, table_rows, table, sems = refs
    rows, columns = depth_in.shape
    own = pl.ds(0, rows)
    copies = [
        pltpu.make_async_copy(source, target.at[own, :], sems.at[slot])
        for slot, (source, target) in enumerate(
            (
                (depth_in, surf),
                (bed_in, bed),
                (rough_in, rough),
                (east_in, east),
                (south_in, south),
            )
        )
    ]
    copies.append(pltpu.make_async_copy(table_in, table, sems.at[5]))
    for copy in copies:
        copy.start()
    copies[5].wait()
    for k in range(table_rows.shape[0]):
        table_rows[k : k + 1, :] = jnp.broadcast_to(table[:, k : k + 1], (1, LANES))
    for copy in copies[:5]:
        copy.wait()


def prepare_kernel(table_rows, rough, *refs):
    surf, east, south, bed = refs[4:8]
    mann, bed_e, bed_s, drag_e, drag_s, to_partner = refs[8:]
    ext, columns = surf.shape
    rows = ext - 2 * HALO
    chunks = columns // LANES
    even = lax.axis_index("gy") % 2 == 0
    entries = [table_rows[k : k + 1, :] for k in range(table_rows.shape[0])]
    for chunk in range(chunks):
        at = cols(chunk)
        mann[:rows, at] = looked_up(rough[:, at], entries)
        surf[:rows, at] = surf[:rows, at] + bed[:rows, at]

    kept = lax.broadcasted_iota(jnp.int32, (rows, LANES), 0) == rows - 1
    for chunk in range(chunks):
        at, then = cols(chunk), cols(min(chunk + 1, chunks - 1))
        s0, b0, m0 = surf[:rows, at], bed[:rows, at], mann[:rows, at]
        bed_max = jnp.maximum(b0, moved_left(b0, bed[:rows, then], 1))
        drag = drag_of(m0, moved_left(m0, mann[:rows, then], 1))
        bed_e[:rows, at] = bed_max
        drag_e[:rows, at] = drag
        q0 = (1.0 / SLOPE) * east[:rows, at]
        new_east = face(q0, s0, moved_left(s0, surf[:rows, then], 1), bed_max, drag)
        new_east = east_walled(new_east, chunk, chunks)
        east[:rows, at] = new_east
        bed_max = jnp.maximum(b0, moved_up(b0))
        drag = drag_of(m0, moved_up(m0))
        bed_s[:rows, at] = bed_max
        drag_s[:rows, at] = drag
        q0 = (1.0 / SLOPE) * south[:rows, at]
        new_south = jnp.where(kept, q0, face(q0, s0, moved_up(s0), bed_max, drag))
        south[:rows, at] = new_south

        def ends(value):
            return jnp.where(even, value[rows - 8 :], value[:8])

        fields = (ends(s0), ends(b0), ends(rough[:, at].astype(jnp.float32)), ends(new_east))
        blocks = border_rows(jnp.logical_not(even), fields, ends(new_south))
        for slot, block in enumerate(blocks):
            to_partner[slot * chunks + chunk] = block


def nodes_kernel(reach, surf, own, partner_section, partner_cells, *refs):
    number, total, takes, masks, windows, given_1 = refs
    rows = surf.shape[0] - 2 * HALO
    ext, columns = number.shape
    chunks = columns // LANES
    tiles = lax.axis_size("gy")
    position = lax.axis_index("gy")
    side = jnp.where(position % 2 == 0, 1, -1)
    partner = jnp.where(position + side < tiles, partner_cells[0:1, :] + 1, 0).astype(jnp.float32)
    section = jnp.concatenate([own[0:1, :], partner_section[...]], axis=1)
    cell = jnp.concatenate([own[1:2, :], partner], axis=1)
    valid, node_row, node_chunk, node_lane = located(cell, position, rows, ext, columns)
    key = jnp.where(valid, node_chunk * ext + node_row, -1)
    starts, levels = scattered(section, key, node_lane, chunks * ext)
    for chunk in range(chunks):
        at = cols(chunk)
        number[:, at] = starts[chunk * ext : (chunk + 1) * ext]
        total[:, at] = levels[chunk * ext : (chunk + 1) * ext]
    key = jnp.where(valid & (node_row < rows), node_chunk * rows + node_row, -1)
    picking(reach, rows, key, node_lane, takes, masks)
    sums = window_sums([surf[:rows, cols(chunk)] for chunk in range(chunks)], reach, True)
    for chunk in range(chunks):
        windows[:, cols(chunk)] = sums[chunk]
    give(reach, 0, surf, None, given_1)


def wall_of(ext, tiles):
    position = lax.axis_index("gy")
    rows = ext - 2 * HALO
    row = lax.broadcasted_iota(jnp.int32, (16, LANES), 0) + (ext - 16)
    return ((row == ext - 1) & (position == 0)) | ((row == rows - 1) & (position == tiles - 1))


def border_kernel(reach, tiles, by_partner, by_other, table_rows, near, *refs):
    surf, east, south, bed, mann, bed_e, bed_s, drag_e, drag_s, number, total, takes, masks = refs[11:]
    ext, columns = surf.shape
    rows = ext - 2 * HALO
    chunks = columns // LANES
    position = lax.axis_index("gy")
    even = position % 2 == 0
    entries = [table_rows[k : k + 1, :] for k in range(table_rows.shape[0])]
    row = lax.broadcasted_iota(jnp.int32, (2 * HALO, LANES), 0)
    for chunk in range(chunks):
        at = cols(chunk)
        halos = []
        flux = jnp.zeros((2 * HALO, LANES), jnp.float32)
        for slot in range(4):
            a, b = by_partner[slot * chunks + chunk], by_other[slot * chunks + chunk]
            below = jnp.where(even, a, b)
            above = jnp.where(even, b, a)
            halos.append(jnp.concatenate([below, above], axis=0))
            flux = jnp.where(row == slot, below[HALO - 1 :], flux)
            flux = jnp.where(row == HALO + slot, above[:1], flux)
        surf[rows:, at] = halos[0]
        bed[rows:, at] = halos[1]
        mann[rows:, at] = looked_up(halos[2].astype(jnp.int32), entries)
        east[rows:, at] = halos[3]
        south[rows:, at] = flux

    beyond = by_other[4 * chunks, 2:4, :]
    section = jnp.concatenate([near[0:1, :], beyond[0:1, :]], axis=1)
    cell = jnp.concatenate([near[1:2, :], beyond[1:2, :]], axis=1)
    valid, node_row, node_chunk, node_lane = located(cell, position, rows, ext, columns)
    key = jnp.where(valid, node_chunk * ext + node_row, -1)
    starts, levels = scattered(section, key, node_lane, chunks * ext)

    key = jnp.where(valid & (node_row < rows), node_chunk * rows + node_row, -1)
    owned = near.shape[1]
    picking(reach, rows, key[:, :owned], node_lane[:, :owned], takes, masks)

    wall = wall_of(ext, tiles)
    kept = lax.broadcasted_iota(jnp.int32, (16, LANES), 0) % 8 < 7
    for chunk in range(chunks):
        at, then = cols(chunk), cols(min(chunk + 1, chunks - 1))
        number[:, at] += starts[chunk * ext : (chunk + 1) * ext]
        total[:, at] += levels[chunk * ext : (chunk + 1) * ext]
        b0, m0 = bed[rows:, at], mann[rows:, at]
        bed_e[rows:, at] = jnp.maximum(b0, moved_left(b0, bed[rows:, then], 1))
        drag_e[rows:, at] = drag_of(m0, moved_left(m0, mann[rows:, then], 1))

        def rolled_up(ref):
            value = jnp.concatenate([ref[rows - 8 :, at], ref[:8, at]], axis=0)
            return value[:16], moved_up(value)[:16]

        s0, s1 = rolled_up(surf)
        b0, b1 = rolled_up(bed)
        m0, m1 = rolled_up(mann)
        bed_max = jnp.maximum(b0, b1)
        drag = drag_of(m0, m1)
        bed_s[rows - 8 :, at] = bed_max
        drag_s[rows - 8 :, at] = drag
        q0 = south[rows - 8 :, at]
        new_south = jnp.where(kept, q0, face(q0, s0, s1, bed_max, drag))
        south[rows - 8 :, at] = jnp.where(wall, 0.0, new_south)


def fluxes(mine, wall, before, faces, east_out, south_out=None, scale=None):
    surf, east, south = before
    bed_e, bed_s, drag_e, drag_s = faces
    chunks = surf.shape[1] // LANES
    rolled = pltpu.roll(surf[mine, cols(0)], LANES - 1, 1)
    lane = lanes_of(rolled.shape[0])
    for chunk in range(chunks):
        at = cols(chunk)
        s0 = surf[mine, at]
        rolled_then = rolled
        if chunk + 1 < chunks:
            rolled_then = pltpu.roll(surf[mine, cols(chunk + 1)], LANES - 1, 1)
        left = jnp.where(lane >= LANES - 1, rolled_then, rolled)
        rolled = rolled_then
        new_east = face(east[mine, at], s0, left, bed_e[mine, at], drag_e[mine, at])
        if scale is not None:
            new_east = scale * new_east
        east_out[mine, at] = east_walled(new_east, chunk, chunks)
        if south_out is not None:
            s0 = surf[:, at]
            new_south = face(south[:, at], s0, moved_up(s0), bed_s[:, at], drag_s[:, at])
            if scale is not None:
                new_south = scale * new_south
            south_out[:, at] = jnp.concatenate(
                [new_south[:-16], jnp.where(wall, 0.0, new_south[-16:])], axis=0
            )


def settled(mine, surf, east, south, keep, sums, spread=SPREAD * SLOPE):
    ext, columns = surf.shape
    rolled = 0.0
    for chunk in range(columns // LANES):
        at = cols(chunk)
        new_east = east[mine, at]
        new_south = south[:, at]
        lane = lanes_of(new_east.shape[0])
        rolled_before, rolled = rolled, pltpu.roll(new_east, 1, 1)
        west = jnp.where(lane < 1, rolled_before, rolled)
        north = pltpu.roll(new_south, 1, 0)[mine]
        inflow = west + north
        s0 = surf[mine, at]
        outflow = new_east + new_south[mine]
        yield chunk, keep[mine, at] * s0 + (spread * (inflow - outflow) + sums[chunk])


def exchange(corridor, mine, surf, total, count, total_out, windows=None):
    chunks = surf.shape[1] // LANES
    sums = window_sums([total[mine, cols(chunk)] for chunk in range(chunks)], corridor, False)
    if total_out is not None:
        if windows is None:
            windows = window_sums(
                [surf[mine, cols(chunk)] for chunk in range(chunks)], corridor, True
            )
        for chunk in range(chunks):
            at = cols(chunk)
            kept = (1.0 - corridor * DRAIN) * total[mine, at]
            total_out[mine, at] = kept + count[mine, at] * windows[chunk]
    return sums


def give(corridor, step, surf, before, after):
    rows, columns = after.shape
    weight = DRAIN * (1.0 - corridor * DRAIN) ** (STEPS - 1 - step)
    for chunk in range(columns // LANES):
        at = cols(chunk)
        value = weight * surf[:rows, at]
        after[:, at] = value if before is None else before[:, at] + value


def first_kernel(corridor, surf, east, south, number, total, windows, *refs):
    surf_1, total_1, count, keep, total_0 = refs
    rows = surf.shape[0] - 2 * HALO
    chunks = surf.shape[1] // LANES
    own = slice(0, rows)
    covering = window_sums([number[own, cols(chunk)] for chunk in range(chunks)], corridor, False)
    for chunk in range(chunks):
        at = cols(chunk)
        count[own, at] = (FEED * DRAIN) * number[own, at]
        keep[own, at] = 1.0 - FEED * covering[chunk]
        total_0[own, at] = FEED * total[own, at]
    windows = [windows[:, cols(chunk)] for chunk in range(chunks)]
    sums = exchange(corridor, own, surf, total_0, count, total_1, windows)
    for chunk, new_surf in settled(own, surf, east, south, keep, sums):
        surf_1[own, cols(chunk)] = new_surf


def second_kernel(corridor, tiles, far, surf, east, south, *refs):
    faces = refs[:4]
    number, total, given_1 = refs[4:7]
    surf_1, total_1, count, keep = refs[11:15]
    surf_2, east_2, south_2, total_2, given_2, total_0 = refs[15:]
    ext, columns = surf.shape
    rows = ext - 2 * HALO
    chunks = columns // LANES
    position = lax.axis_index("gy")
    tail = slice(rows, ext)

    valid, node_row, node_chunk, node_lane = located(far[1:2, :], position, rows, ext, columns)
    key = jnp.where(valid & (node_row >= rows), node_chunk * 8 + (node_row - rows), -1)
    starts, levels = scattered(far[0:1, :], key, node_lane, chunks * 8)
    starting = [
        number[tail, cols(chunk)] + starts[chunk * 8 : chunk * 8 + 8] for chunk in range(chunks)
    ]
    covering = window_sums(starting, corridor, False)
    for chunk in range(chunks):
        at = cols(chunk)
        count[tail, at] = (FEED * DRAIN) * starting[chunk]
        keep[tail, at] = 1.0 - FEED * covering[chunk]
        total_0[tail, at] = FEED * (total[tail, at] + levels[chunk * 8 : chunk * 8 + 8])
    sums = exchange(corridor, tail, surf, total_0, count, total_1)
    for chunk, new_surf in settled(tail, surf, east, south, keep, sums):
        surf_1[tail, cols(chunk)] = new_surf

    every = slice(0, ext)
    sums = exchange(corridor, every, surf_1, total_1, count, total_2)
    fluxes(every, wall_of(ext, tiles), (surf_1, east, south), faces, east_2, south_2)
    for chunk, new_surf in settled(every, surf_1, east_2, south_2, keep, sums):
        surf_2[:, cols(chunk)] = new_surf
    give(corridor, 1, surf_1, given_1, given_2)


def third_kernel(corridor, tiles, surf, east, south, *refs):
    faces = refs[:4]
    total, keep, count, given_2, surf_3, east_3, south_3, total_3, given_3 = refs[4:]
    ext = surf.shape[0]
    own = slice(0, ext - 2 * HALO)
    sums = exchange(corridor, own, surf, total, count, total_3)
    fluxes(own, wall_of(ext, tiles), (surf, east, south), faces, east_3, south_3)
    for chunk, new_surf in settled(own, surf, east_3, south_3, keep, sums):
        surf_3[own, cols(chunk)] = new_surf
    give(corridor, 2, surf, given_2, given_3)


def terms_kernel(corridor, own, surf, given_3, *refs):
    takes, masks, takes_near, masks_near, own_term, partner_term, other_term = refs
    rows, columns = given_3.shape
    owned = own.shape[1]
    chunks = columns // LANES
    levels = [
        given_3[:, cols(chunk)] + DRAIN * surf[:rows, cols(chunk)] for chunk in range(chunks)
    ]
    spare = takes.shape[2] - chunks * rows
    if spare:
        levels.append(jnp.zeros((spare, LANES), jnp.float32))
    levels = jnp.concatenate(levels, axis=0)
    high = levels.astype(jnp.bfloat16)
    low = (levels - high.astype(jnp.float32)).astype(jnp.bfloat16)
    picked = jnp.dot(
        jnp.concatenate([takes[0], takes_near[0], takes[1], takes_near[1]], axis=0),
        jnp.concatenate([high, low], axis=1),
        preferred_element_type=jnp.float32,
    )
    hit = jnp.concatenate([masks[0], masks_near[0], masks[1], masks_near[1]], axis=0)
    picked = (picked * jnp.concatenate([hit, hit], axis=1)).astype(jnp.bfloat16)
    picked = jnp.concatenate([picked[: 3 * owned], picked[3 * owned :]], axis=1)
    terms = lax.dot_general(
        jnp.ones((8, 4 * LANES), jnp.bfloat16),
        picked,
        (((1,), (1,)), ((), ())),
        preferred_element_type=jnp.float32,
    )[0:1]
    own_term[...] = (1.0 - corridor * DRAIN) ** STEPS * own[0:1, :] + terms[:, :owned]
    partner_term[...] = terms[:, owned : 2 * owned]
    other_term[...] = terms[:, 2 * owned :]


def last_kernel(corridor, tiles, surf_2, east_2, south_3, *refs):
    faces = refs[:4]
    total_2, total_3, keep, bed, _, east_3 = refs[4:10]
    surf_3, depth_out, east_out, south_out, depth_4, east_4, south_4, east_tail, sems = refs[10:]
    ext, columns = surf_2.shape
    rows = ext - 2 * HALO
    chunks = columns // LANES
    own, tail = slice(0, rows), slice(rows, ext)
    sums = exchange(corridor, tail, surf_2, total_2, None, None)
    fluxes(tail, None, (surf_2, east_2, None), faces, east_tail)
    for chunk, new_surf in settled(tail, surf_2, east_tail, south_3, keep, sums):
        surf_3[tail, cols(chunk)] = new_surf

    def copy(slot, source, target, first, last):
        part = pl.ds(first * LANES, (last - first) * LANES)
        return pltpu.make_async_copy(
            source.at[pl.ds(0, rows), part], target.at[:, part], sems.at[slot]
        )

    fluxes(
        own, wall_of(ext, tiles), (surf_3, east_3, south_3), faces, east_4, south_4, scale=SLOPE
    )
    copies = [copy(0, east_4, east_out, 0, chunks), copy(1, south_4, south_out, 0, chunks)]
    for one in copies:
        one.start()
    sums = exchange(corridor, own, surf_3, total_3, None, None)
    group = 5
    for chunk, new_surf in settled(own, surf_3, east_4, south_4, keep, sums, spread=SPREAD):
        at = cols(chunk)
        depth_4[:, at] = new_surf - bed[own, at]
        if (chunk + 1) % group == 0 or chunk + 1 == chunks:
            first = chunk // group
            copies.append(copy(2 + first, depth_4, depth_out, first * group, chunk + 1))
            copies[-1].start()
    for one in copies:
        one.wait()


def local(
    depth, flux_east, flux_south, river_section, bed_level, rough_class, manning_table, bank_cell
):
    rows, columns = depth.shape
    owned = river_section.shape[0]
    corridor = bank_cell.shape[0]
    tiles = lax.axis_size("gy")
    ext = rows + 2 * HALO
    chunks = columns // LANES
    partner_section = swapped(river_section, 0).reshape(1, owned)
    partner_cells = swapped(bank_cell, 0)

    def held(value):
        return pltpu.with_memory_space_constraint(value, pltpu.VMEM)

    def far(value):
        return pltpu.with_memory_space_constraint(value, pltpu.HBM)

    params = pltpu.CompilerParams(vmem_limit_bytes=VMEM_LIMIT)
    halo = pltpu.VMEM((4 * chunks, HALO, LANES), jnp.float32)
    wide = pltpu.VMEM((4 * chunks + 1, HALO, LANES), jnp.float32)
    field = pltpu.VMEM((ext, columns), jnp.float32)
    small = pltpu.VMEM((rows, columns), jnp.float32)
    term = pltpu.VMEM((1, owned), jnp.float32)
    pair = pltpu.VMEM((2, owned), jnp.float32)
    result = pltpu.HBM((rows, columns), jnp.float32)
    cells = -(-chunks * rows // LANES) * LANES

    def call(kernel, name, outs, values, scratch=(), aliases=None):
        return pl.pallas_call(
            kernel,
            out_shape=outs,
            in_specs=[VMEM_SPEC] * len(values),
            out_specs=[HBM_SPEC if out is result else VMEM_SPEC for out in outs],
            scratch_shapes=scratch,
            input_output_aliases=aliases or {},
            compiler_params=params,
            name=name,
        )(*[held(value) for value in values])

    def picks(nodes):
        return [
            pltpu.VMEM((2, nodes, cells), jnp.bfloat16),
            pltpu.VMEM((2, nodes, LANES), jnp.float32),
        ]

    classes = manning_table.shape[0]
    table = far(manning_table.reshape(1, classes))
    table_held = pltpu.VMEM((1, classes), jnp.float32)
    to_other, own = pl.pallas_call(
        pack_kernel,
        out_shape=[wide, pair],
        in_specs=[HBM_SPEC] * 8,
        out_specs=[VMEM_SPEC] * 2,
        scratch_shapes=[
            pltpu.VMEM((4, 8, columns), jnp.float32),
            pltpu.VMEM((8, columns), jnp.int32),
            pltpu.VMEM((corridor, owned), jnp.int32),
            table_held,
            pltpu.SemaphoreType.DMA((8,)),
        ],
        compiler_params=params,
        name="pack",
    )(
        *[far(value) for value in (depth, bed_level, rough_class, flux_east, flux_south)],
        far(river_section.reshape(1, owned)),
        far(bank_cell),
        table,
    )
    (to_other,) = call(
        join_kernel,
        "join",
        [wide],
        (to_other, partner_section, partner_cells),
        aliases={0: 0},
    )
    by_other = swapped(to_other, 1)
    *loaded, rough, table_rows = pl.pallas_call(
        load_kernel,
        out_shape=[field] * 4
        + [pltpu.VMEM((rows, columns), jnp.int32), pltpu.VMEM((classes, LANES), jnp.float32)],
        in_specs=[HBM_SPEC] * 6,
        out_specs=[VMEM_SPEC] * 6,
        scratch_shapes=[table_held, pltpu.SemaphoreType.DMA((6,))],
        compiler_params=params,
        name="load",
    )(
        *[far(value) for value in (depth, flux_east, flux_south, bed_level, rough_class)],
        table,
    )
    *fields, to_partner = call(
        prepare_kernel,
        "prepare",
        [field] * 9 + [halo],
        (table_rows, rough, *loaded),
        aliases={2 + slot: slot for slot in range(4)},
    )
    by_partner = swapped(to_partner, 0)
    number, total, takes, masks, windows, given_1 = call(
        functools.partial(nodes_kernel, corridor),
        "nodes",
        [field] * 2 + picks(2 * owned) + [small] * 2,
        (fields[0], own, partner_section, partner_cells),
    )
    (near,) = call(relay_kernel, "relay", [pair], (by_other, masks))
    from_far = swapped(near, 0)
    *fields, takes_near, masks_near = call(
        functools.partial(border_kernel, corridor, tiles),
        "border",
        [field] * 11 + picks(owned),
        (by_partner, by_other, table_rows, near, *fields, number, total),
        aliases={4 + slot: slot for slot in range(11)},
    )
    surf, east, south, bed, _, *faces, number, total = fields
    surf_1, total_1, count, keep = call(
        functools.partial(first_kernel, corridor),
        "first",
        [field] * 4,
        (surf, east, south, number, total, windows),
        scratch=[field],
    )
    surf_1, total_1, count, keep, surf_2, east_2, south_2, total_2, given_2 = call(
        functools.partial(second_kernel, corridor, tiles),
        "second",
        [field] * 8 + [small],
        (
            *(from_far, surf, east, south, *faces, number, total, given_1),
            *(surf_1, total_1, count, keep),
        ),
        scratch=[field],
        aliases={11 + slot: slot for slot in range(4)},
    )
    surf_3, east_3, south_3, total_3, given_3 = call(
        functools.partial(third_kernel, corridor, tiles),
        "third",
        [field] * 4 + [small],
        (surf_2, east_2, south_2, *faces, total_2, keep, count, given_2),
    )
    own_term, partner_term, other_term = call(
        functools.partial(terms_kernel, corridor),
        "terms",
        [term] * 3,
        (own, surf_3, given_3, takes, masks, takes_near, masks_near),
    )
    from_other = swapped(other_term.reshape(owned), 1)
    from_partner = swapped(partner_term.reshape(owned), 0)
    _, depth, flux_east, flux_south = call(
        functools.partial(last_kernel, corridor, tiles),
        "last",
        [field, result, result, result],
        (surf_2, east_2, south_3, *faces, total_2, total_3, keep, bed, surf_3, east_3),
        scratch=[small, small, field, field, pltpu.SemaphoreType.DMA((2 + -(-chunks // 5),))],
        aliases={11: 0},
    )
    river_section = own_term.reshape(owned) + from_other + from_partner
    return (depth, flux_east, flux_south, river_section)


def solution(mesh):
    return jax.shard_map(
        local,
        mesh=mesh,
        in_specs=(
            P(("runs", "gy"), None),
            P(("runs", "gy"), None),
            P(("runs", "gy"), None),
            P(("runs", "gy")),
            P("gy", None),
            P("gy", None),
            P(),
            P(None, "gy"),
        ),
        out_specs=(
            P(("runs", "gy"), None),
            P(("runs", "gy"), None),
            P(("runs", "gy"), None),
            P(("runs", "gy")),
        ),
        check_vma=False,
    )
```

profile of v0, /device:TPU:0, one launch (start us, length us, event | category | flops | bytes accessed | tf_op | source)
XLA Modules:
  0.0 20.6 jit_solution(15582934278040333771)
XLA Ops:
  0.6 0.5 %collective-permute-start.1 = (s32[4,128]{1,0:T(4,128)}, s32[4,128]{1,0:T(4,128)S(1)}, u32[]{:S(2)}, u32[]{:S(2)}) collective-permute-start(s32[4,128]{1,0:T(4,128)} %cells.1), channel_id=1, source_target_pairs={{0,1},{1,0},{2,3},{3,2},{4,5},{5,4},{6,7},{7,6},{8,9},{9,8},{10,11... | collective-permute-start | bytes 6152 | tf_op jit(solution)/shard_map/ppermute | solution.py:37
  1.1 0.1 collective-permute-start
  1.2 1.2 %pack.1 = (f32[61,4,128]{2,1,0:T(4,128)S(1)}, f32[2,128]{1,0:T(2,128)S(1)}) custom-call(f32[32,1920]{1,0:T(8,128)} %depth_in.1, f32[32,1920]{1,0:T(8,128)} %bed_in.1, s32[32,1920]{1,0:T(8,128)} %rough_in.1, f32[32,1920]{1,0:T(8,128)} %east_in.1, f32[32,1920]{1,0:T(8,128)} %south_in.1, f32[1,128]{1,0:T(1,128)} %bitcast.15, s32[4,128]{1,0:T(4,128)} %cells.1, ...), custom_call_target="tpu_custom_call" | custom-call | tf_op jit(solution)/shard_map/pack/pallas_call | solution.py:677
  2.5 0.0 collective-permute-done
  2.5 0.0 collective-permute-done.1.cells.partner_cells
  2.5 0.7 %collective-permute-start.2 = (f32[61,4,128]{2,1,0:T(4,128)S(1)}, f32[61,4,128]{2,1,0:T(4,128)S(1)}, u32[]{:S(2)}, u32[]{:S(2)}) collective-permute-start(f32[61,4,128]{2,1,0:T(4,128)S(1)} %join.1), channel_id=1, source_target_pairs={{1,2},{2,1},{3,4},{4,3},{5,6},{6,5},{7,8},{8,7},{9,10},{10,9},{11,... | collective-permute-start | bytes 374792 | tf_op jit(solution)/shard_map/ppermute | solution.py:37
  3.2 1.4 %load.1 = (f32[40,1920]{1,0:T(8,128)S(1)}, f32[40,1920]{1,0:T(8,128)S(1)}, f32[40,1920]{1,0:T(8,128)S(1)}, f32[40,1920]{1,0:T(8,128)S(1)}, s32[32,1920]{1,0:T(8,128)S(1)}, /*index=5*/f32[8,128]{1,0:T(8,128)S(1)}) custom-call(f32[32,1920]{1,0:T(8,128)} %depth_in.1, f32[32,1920]{1,0:T(8,128)} %east_in.1, f32[32,1920]{1,0:T(8,128)} %south_in.1, ...), custom_call_target="tpu_custom_call" | custom-call | tf_op jit(solution)/shard_map/load/pallas_call | solution.py:705
  4.6 0.7 %prepare.1 = (f32[40,1920]{1,0:T(8,128)S(1)}, f32[40,1920]{1,0:T(8,128)S(1)}, f32[40,1920]{1,0:T(8,128)S(1)}, f32[40,1920]{1,0:T(8,128)S(1)}, f32[40,1920]{1,0:T...) custom-call(f32[8,128]{1,0:T(8,128)S(1)} %get-tuple-element.63.table, ...), custom_call_target="tpu_custom_call", output_to_operand_aliasing={{0}: (2, {}), {1}: (3, {}), {2}: (4, {}), {3}: (5, {})} | custom-call | tf_op jit(solution)/shard_map/prepare/pallas_call | solution.py:657
  5.3 4.4 %collective-permute-start.4 = (f32[60,4,128]{2,1,0:T(4,128)S(1)}, f32[60,4,128]{2,1,0:T(4,128)S(1)}, u32[]{:S(2)}, u32[]{:S(2)}) collective-permute-start(f32[60,4,128]{2,1,0:T(4,128)S(1)} %get-tuple-element.72), channel_id=1, source_target_pairs={{0,1},{1,0},{2,3},{3,2},{4,5},{5,4},{6,7},{7,6},{8,9},{9,8},{10,11... | collective-permute-start | bytes 368648 | tf_op jit(solution)/shard_map/ppermute | solution.py:37
  9.7 0.5 %nodes.1 = (f32[40,1920]{1,0:T(8,128)S(1)}, f32[40,1920]{1,0:T(8,128)S(1)}, bf16[2,256,512]{2,1,0:T(8,128)(2,1)S(1)}, f32[2,256,128]{2,1,0:T(8,128)S(1)}, f32[32...) custom-call(f32[40,1920]{1,0:T(8,128)S(1)} %get-tuple-element.69.surf.refs_0_, f32[2,128]{1,0:T(2,128)S(1)} %get-tuple-element.70.own, ...), custom_call_target="tpu_custom_call" | custom-call | tf_op jit(solution)/shard_map/nodes/pallas_call | solution.py:657
  10.2 0.0 collective-permute-done.2.by_other
  10.2 0.1 collective-permute-start.3
  10.3 0.3 %collective-permute-done.4.by_partner = f32[60,4,128]{2,1,0:T(4,128)S(1)} collective-permute-done((f32[60,4,128]{2,1,0:T(4,128)S(1)}, f32[60,4,128]{2,1,0:T(4,128)S(1)}, u32[]{:S(2)}, u32[]{:S(2)}) %collective-permute-start.4) | collective-permute-done | bytes 122912 | tf_op jit(solution)/shard_map/ppermute | solution.py:37
  10.7 0.6 %border.1 = (f32[40,1920]{1,0:T(8,128)S(1)}, f32[40,1920]{1,0:T(8,128)S(1)}, f32[40,1920]{1,0:T(8,128)S(1)}, f32[40,1920]{1,0:T(8,128)S(1)}, f32[40,1920]{1,0:T(...) custom-call(f32[60,4,128]{2,1,0:T(4,128)S(1)} %collective-permute-do, ...), custom_call_target="tpu_custom_call", output_to_operand_aliasing={{0}: (4, {}), {1}: (5, {}), {2}: (6, {}), {3}: (7, {}), {4}... | custom-call | tf_op jit(solution)/shard_map/border/pallas_call | solution.py:657
  11.2 0.3 %first.1 = (f32[40,1920]{1,0:T(8,128)S(1)}, f32[40,1920]{1,0:T(8,128)S(1)}, f32[40,1920]{1,0:T(8,128)S(1)}, f32[40,1920]{1,0:T(8,128)S(1)}) custom-call(f32[40,1920]{1,0:T(8,128)S(1)} %get-tuple-element.83.surf, f32[40,1920]{1,0:T(8,128)S(1)} %get-tuple-element.84.east, f32[40,1920]{1,0:T(8,128)S(1)} %get-tuple-element.85.south, ...), custom_call_target="tpu_custom_call" | custom-call | tf_op jit(solution)/shard_map/first/pallas_call | solution.py:657
  11.6 0.0 collective-permute-done.3.far
  11.6 1.0 %second.1 = (f32[40,1920]{1,0:T(8,128)S(1)}, f32[40,1920]{1,0:T(8,128)S(1)}, f32[40,1920]{1,0:T(8,128)S(1)}, f32[40,1920]{1,0:T(8,128)S(1)}, f32[40,1920]{1,0:T(...) custom-call(f32[2,128]{1,0:T(2,128)S(1)} %collective-permute-done.3., ...), custom_call_target="tpu_custom_call", output_to_operand_aliasing={{0}: (11, {}), {1}: (12, {}), {2}: (13, {}), {3}: (14, {})} | custom-call | tf_op jit(solution)/shard_map/second/pallas_call | solution.py:657
  12.6 0.7 %third.1 = (f32[40,1920]{1,0:T(8,128)S(1)}, f32[40,1920]{1,0:T(8,128)S(1)}, f32[40,1920]{1,0:T(8,128)S(1)}, f32[40,1920]{1,0:T(8,128)S(1)}, f32[32,1920]{1,0:T(8,128)S(1)}) custom-call(f32[40,1920]{1,0:T(8,128)S(1)} %get-tuple-element.98.surf.surf_2, f32[40,1920]{1,0:T(8,128)S(1)} %get-tuple-element.99.east.east_2, f32[40,1920]{1,0:T(8,128)S(1)} %get-tuple-element.100.south, ...), custom_call_target="tpu_custom_call" | custom-call | tf_op jit(solution)/shard_map/third/pallas_call | solution.py:657
  13.3 0.6 %terms.1 = (f32[1,128]{1,0:T(1,128)S(1)}, f32[1,128]{1,0:T(1,128)S(1)}, f32[1,128]{1,0:T(1,128)S(1)}) custom-call(f32[2,128]{1,0:T(2,128)S(1)} %get-tuple-element.70.own, f32[40,1920]{1,0:T(8,128)S(1)} %get-tuple-element.108.refs_8_.surf, f32[32,1920]{1,0:T(8,128)S(1)} %get-tuple-element.113.given_3, bf16[2,256,512]{2,1,0:T(8,128)(2,1)S(1)} %get-tuple-element.114.refs_0_, ...), custom_call_target="tpu_custom_call" | custom-call | tf_op jit(solution)/shard_map/terms/pallas_call | solution.py:657
  13.9 0.7 %collective-permute-start.5 = (f32[128]{0:T(128)S(1)}, f32[128]{0:T(128)S(1)}, u32[]{:S(2)}, u32[]{:S(2)}) collective-permute-start(f32[128]{0:T(128)S(1)} %bitcast.12), channel_id=1, source_target_pairs={{1,2},{2,1},{3,4},{4,3},{5,6},{6,5},{7,8},{8,7},{9,10},{10,9},{11,... | collective-permute-start | bytes 1544 | tf_op jit(solution)/shard_map/ppermute | solution.py:37
  14.6 4.0 %collective-permute-start.6 = (f32[128]{0:T(128)S(1)}, f32[128]{0:T(128)S(1)}, u32[]{:S(2)}, u32[]{:S(2)}) collective-permute-start(f32[128]{0:T(128)S(1)} %bitcast.11), channel_id=1, source_target_pairs={{0,1},{1,0},{2,3},{3,2},{4,5},{5,4},{6,7},{7,6},{8,9},{9,8},{10,11... | collective-permute-start | bytes 1544 | tf_op jit(solution)/shard_map/ppermute | solution.py:37
  18.6 1.5 %last.1 = (f32[40,1920]{1,0:T(8,128)S(1)}, f32[32,1920]{1,0:T(8,128)}, f32[32,1920]{1,0:T(8,128)}, f32[32,1920]{1,0:T(8,128)}) custom-call(f32[40,1920]{1,0:T(8,128)S(1)} %get-tuple-element.98.surf.surf_2, f32[40,1920]{1,0:T(8,128)S(1)} %get-tuple-element.99.east.east_2, ...), custom_call_target="tpu_custom_call", output_to_operand_aliasing={{0}: (11, {})} | custom-call | tf_op jit(solution)/shard_map/last/pallas_call | solution.py:657
  20.1 0.0 collective-permute-done.5
  20.1 0.0 collective-permute-done.6
  20.1 0.5 %fusion = f32[128]{0:T(128)} fusion(f32[128]{0:T(128)S(1)} %collective-permute-done.6, f32[128]{0:T(128)S(1)} %collective-permute-done.5, f32[1,128]{1,0:T(1,128)S(1)} %get-tuple-element.117), kind=kLoop, calls=%fused_computation.1 | loop fusion | flops 256 | bytes 2048 | tf_op jit(solution)/shard_map/add | solution.py:782
  (2 shorter events, 0.0 us)
Async XLA Ops:
  0.6 1.9 %collective-permute-start.1 = (s32[4,128]{1,0:T(4,128)}, s32[4,128]{1,0:T(4,128)S(1)}, u32[]{:S(2)}, u32[]{:S(2)}) collective-permute-start(s32[4,128]{1,0:T(4,128)} %cells.1), channel_id=1, source_target_pairs={{0,1},{1,0},{2,3},{3,2},{4,5},{5,4},{6,7},{7,6},{8,9},{9,8},{10,11... | collective-permute-start | bytes 6152 | tf_op jit(solution)/shard_map/ppermute | solution.py:37
  1.1 1.3 %collective-permute-start = (f32[128]{0:T(128)}, f32[128]{0:T(128)S(1)}, u32[]{:S(2)}, u32[]{:S(2)}) collective-permute-start(f32[128]{0:T(128)} %param.11), channel_id=1, source_target_pairs={{0,1},{1,0},{2,3},{3,2},{4,5},{5,4},{6,7},{7,6},{8,9},{9,8},{10,11... | collective-permute-start | bytes 1544 | tf_op jit(solution)/shard_map/ppermute | solution.py:37
  2.5 7.7 %collective-permute-start.2 = (f32[61,4,128]{2,1,0:T(4,128)S(1)}, f32[61,4,128]{2,1,0:T(4,128)S(1)}, u32[]{:S(2)}, u32[]{:S(2)}) collective-permute-start(f32[61,4,128]{2,1,0:T(4,128)S(1)} %join.1), channel_id=1, source_target_pairs={{1,2},{2,1},{3,4},{4,3},{5,6},{6,5},{7,8},{8,7},{9,10},{10,9},{11,... | collective-permute-start | bytes 374792 | tf_op jit(solution)/shard_map/ppermute | solution.py:37
  5.3 5.3 %collective-permute-start.4 = (f32[60,4,128]{2,1,0:T(4,128)S(1)}, f32[60,4,128]{2,1,0:T(4,128)S(1)}, u32[]{:S(2)}, u32[]{:S(2)}) collective-permute-start(f32[60,4,128]{2,1,0:T(4,128)S(1)} %get-tuple-element.72), channel_id=1, source_target_pairs={{0,1},{1,0},{2,3},{3,2},{4,5},{5,4},{6,7},{7,6},{8,9},{9,8},{10,11... | collective-permute-start | bytes 368648 | tf_op jit(solution)/shard_map/ppermute | solution.py:37
  10.2 1.3 %collective-permute-start.3 = (f32[2,128]{1,0:T(2,128)S(1)}, f32[2,128]{1,0:T(2,128)S(1)}, u32[]{:S(2)}, u32[]{:S(2)}) collective-permute-start(f32[2,128]{1,0:T(2,128)S(1)} %relay.1.near), channel_id=1, source_target_pairs={{0,1},{1,0},{2,3},{3,2},{4,5},{5,4},{6,7},{7,6},{8,9},{9,8},{10,11... | collective-permute-start | bytes 3080 | tf_op jit(solution)/shard_map/ppermute | solution.py:37
  13.9 6.2 %collective-permute-start.5 = (f32[128]{0:T(128)S(1)}, f32[128]{0:T(128)S(1)}, u32[]{:S(2)}, u32[]{:S(2)}) collective-permute-start(f32[128]{0:T(128)S(1)} %bitcast.12), channel_id=1, source_target_pairs={{1,2},{2,1},{3,4},{4,3},{5,6},{6,5},{7,8},{8,7},{9,10},{10,9},{11,... | collective-permute-start | bytes 1544 | tf_op jit(solution)/shard_map/ppermute | solution.py:37
  14.6 5.5 %collective-permute-start.6 = (f32[128]{0:T(128)S(1)}, f32[128]{0:T(128)S(1)}, u32[]{:S(2)}, u32[]{:S(2)}) collective-permute-start(f32[128]{0:T(128)S(1)} %bitcast.11), channel_id=1, source_target_pairs={{0,1},{1,0},{2,3},{3,2},{4,5},{5,4},{6,7},{7,6},{8,9},{9,8},{10,11... | collective-permute-start | bytes 1544 | tf_op jit(solution)/shard_map/ppermute | solution.py:37
where the time goes:
time: 20.9 us; the launch traced here: 20.6 us
  starting transfers between devices  10.4 us (50%)
  Pallas kernels  8.62 us (41%)
  between operations  0.77 us (4%)
  other arithmetic  0.52 us (2%)
  waiting for transfers between devices  0.34 us (2%)
    ppermute x7, starting transfers between devices, swapped(): return lax.ppermute(value, 'gy', pairs)  10.4 us
    pallas_call x10, Pallas kernels, call(): pl.pallas_call(kernel, out_shape=outs, in_specs=[VMEM_SPEC] * len(values)...  5.94 us
    pallas_call x1, Pallas kernels, local(): pl.pallas_call(load_kernel, out_shape=[field] * 4 + [pltpu.VMEM((rows, co...  1.44 us
    pallas_call x1, Pallas kernels, local(): pl.pallas_call(pack_kernel, out_shape=[wide, pair], in_specs=[HBM_SPEC] *...  1.24 us
    add x1, other arithmetic, local(): river_section = own_term.reshape(owned) + from_other + from_partner  0.52 us
  transfers between devices with their start and end apart: 7, of which 1 were waited for; matrix products, arithmetic and copies ran while one was open for 0% of the time, Pallas kernels for 30%

commit v1 on v0

--- a/solution.py
+++ b/solution.py
@@ -365,6 +365,13 @@
     chunks = columns // LANES
     position = lax.axis_index("gy")
     even = position % 2 == 0
+    beyond = by_other[4 * chunks, 2:4, :]
+    section = jnp.concatenate([near[0:1, :], beyond[0:1, :]], axis=1)
+    cell = jnp.concatenate([near[1:2, :], beyond[1:2, :]], axis=1)
+    valid, node_row, node_chunk, node_lane = located(cell, position, rows, ext, columns)
+    key = jnp.where(valid, node_chunk * ext + node_row, -1)
+    starts, levels = scattered(section, key, node_lane, chunks * ext)
+
     entries = [table_rows[k : k + 1, :] for k in range(table_rows.shape[0])]
     row = lax.broadcasted_iota(jnp.int32, (2 * HALO, LANES), 0)
     for chunk in range(chunks):
@@ -384,13 +391,6 @@
         east[rows:, at] = halos[3]
         south[rows:, at] = flux
 
-    beyond = by_other[4 * chunks, 2:4, :]
-    section = jnp.concatenate([near[0:1, :], beyond[0:1, :]], axis=1)
-    cell = jnp.concatenate([near[1:2, :], beyond[1:2, :]], axis=1)
-    valid, node_row, node_chunk, node_lane = located(cell, position, rows, ext, columns)
-    key = jnp.where(valid, node_chunk * ext + node_row, -1)
-    starts, levels = scattered(section, key, node_lane, chunks * ext)
-
     key = jnp.where(valid & (node_row < rows), node_chunk * rows + node_row, -1)
     owned = near.shape[1]
     picking(reach, rows, key[:, :owned], node_lane[:, :owned], takes, masks)
@@ -421,10 +421,11 @@
         south[rows - 8 :, at] = jnp.where(wall, 0.0, new_south)
 
 
-def fluxes(mine, wall, before, faces, east_out, south_out=None, scale=None):
+def fluxes(mine, upper, wall, before, faces, east_out, south_out, scale=None):
     surf, east, south = before
     bed_e, bed_s, drag_e, drag_s = faces
-    chunks = surf.shape[1] // LANES
+    ext, columns = surf.shape
+    chunks = columns // LANES
     rolled = pltpu.roll(surf[mine, cols(0)], LANES - 1, 1)
     lane = lanes_of(rolled.shape[0])
     for chunk in range(chunks):
@@ -439,14 +440,21 @@
         if scale is not None:
             new_east = scale * new_east
         east_out[mine, at] = east_walled(new_east, chunk, chunks)
-        if south_out is not None:
-            s0 = surf[:, at]
-            new_south = face(south[:, at], s0, moved_up(s0), bed_s[:, at], drag_s[:, at])
+        if upper:
+            s0 = surf[: upper + 8, at]
+            s1 = moved_up(s0)[:upper]
+            new_south = face(south[:upper, at], s0[:upper], s1, bed_s[:upper, at], drag_s[:upper, at])
             if scale is not None:
                 new_south = scale * new_south
-            south_out[:, at] = jnp.concatenate(
-                [new_south[:-16], jnp.where(wall, 0.0, new_south[-16:])], axis=0
-            )
+            south_out[:upper, at] = new_south
+        if wall is not None:
+            low = slice(ext - 16, ext)
+            s0 = jnp.concatenate([surf[low, at], surf[:8, at]], axis=0)
+            s1 = moved_up(s0)[:16]
+            new_south = face(south[low, at], s0[:16], s1, bed_s[low, at], drag_s[low, at])
+            if scale is not None:
+                new_south = scale * new_south
+            south_out[low, at] = jnp.where(wall, 0.0, new_south)
 
 
 def settled(mine, surf, east, south, keep, sums, spread=SPREAD * SLOPE):
@@ -531,37 +539,41 @@
         keep[tail, at] = 1.0 - FEED * covering[chunk]
         total_0[tail, at] = FEED * (total[tail, at] + levels[chunk * 8 : chunk * 8 + 8])
     sums = exchange(corridor, tail, surf, total_0, count, total_1)
+
+    own = slice(0, rows)
+    before = (surf_1, east, south)
+    fluxes(own, rows - 8, None, before, faces, east_2, south_2)
+    own_sums = exchange(corridor, own, surf_1, total_1, count, total_2)
+    give(corridor, 1, surf_1, given_1, given_2)
+
     for chunk, new_surf in settled(tail, surf, east, south, keep, sums):
         surf_1[tail, cols(chunk)] = new_surf
-
-    every = slice(0, ext)
-    sums = exchange(corridor, every, surf_1, total_1, count, total_2)
-    fluxes(every, wall_of(ext, tiles), (surf_1, east, south), faces, east_2, south_2)
-    for chunk, new_surf in settled(every, surf_1, east_2, south_2, keep, sums):
-        surf_2[:, cols(chunk)] = new_surf
-    give(corridor, 1, surf_1, given_1, given_2)
+    tail_sums = exchange(corridor, tail, surf_1, total_1, count, total_2)
+    fluxes(tail, 0, wall_of(ext, tiles), before, faces, east_2, south_2)
+    for mine, sums in ((own, own_sums), (tail, tail_sums)):
+        for chunk, new_surf in settled(mine, surf_1, east_2, south_2, keep, sums):
+            surf_2[mine, cols(chunk)] = new_surf
 
 
 def third_kernel(corridor, tiles, surf, east, south, *refs):
     faces = refs[:4]
-    total, keep, count, given_2, surf_3, east_3, south_3, total_3, given_3 = refs[4:]
-    ext = surf.shape[0]
-    own = slice(0, ext - 2 * HALO)
-    sums = exchange(corridor, own, surf, total, count, total_3)
-    fluxes(own, wall_of(ext, tiles), (surf, east, south), faces, east_3, south_3)
-    for chunk, new_surf in settled(own, surf, east_3, south_3, keep, sums):
-        surf_3[own, cols(chunk)] = new_surf
-    give(corridor, 2, surf, given_2, given_3)
-
-
-def terms_kernel(corridor, own, surf, given_3, *refs):
-    takes, masks, takes_near, masks_near, own_term, partner_term, other_term = refs
-    rows, columns = given_3.shape
+    total, keep, count, given_2, own, takes, masks, takes_near, masks_near = refs[4:13]
+    surf_3, east_3, south_3, total_3, own_term, partner_term, other_term = refs[13:]
+    ext, columns = surf.shape
+    rows = ext - 2 * HALO
+    mine = slice(0, rows)
     owned = own.shape[1]
     chunks = columns // LANES
-    levels = [
-        given_3[:, cols(chunk)] + DRAIN * surf[:rows, cols(chunk)] for chunk in range(chunks)
-    ]
+    sums = exchange(corridor, mine, surf, total, count, total_3)
+    fluxes(
+        mine, rows - 8, wall_of(ext, tiles), (surf, east, south), faces, east_3, south_3
+    )
+    weight = DRAIN * (1.0 - corridor * DRAIN)
+    levels = []
+    for chunk, new_surf in settled(mine, surf, east_3, south_3, keep, sums):
+        at = cols(chunk)
+        surf_3[mine, at] = new_surf
+        levels.append(given_2[:, at] + weight * surf[mine, at] + DRAIN * new_surf)
     spare = takes.shape[2] - chunks * rows
     if spare:
         levels.append(jnp.zeros((spare, LANES), jnp.float32))
@@ -596,7 +608,7 @@
     chunks = columns // LANES
     own, tail = slice(0, rows), slice(rows, ext)
     sums = exchange(corridor, tail, surf_2, total_2, None, None)
-    fluxes(tail, None, (surf_2, east_2, None), faces, east_tail)
+    fluxes(tail, 0, None, (surf_2, east_2, None), faces, east_tail, None)
     for chunk, new_surf in settled(tail, surf_2, east_tail, south_3, keep, sums):
         surf_3[tail, cols(chunk)] = new_surf
 
@@ -606,9 +618,8 @@
             source.at[pl.ds(0, rows), part], target.at[:, part], sems.at[slot]
         )
 
-    fluxes(
-        own, wall_of(ext, tiles), (surf_3, east_3, south_3), faces, east_4, south_4, scale=SLOPE
-    )
+    before = (surf_3, east_3, south_3)
+    fluxes(own, rows - 8, wall_of(ext, tiles), before, faces, east_4, south_4, scale=SLOPE)
     copies = [copy(0, east_4, east_out, 0, chunks), copy(1, south_4, south_out, 0, chunks)]
     for one in copies:
         one.start()
@@ -757,17 +768,14 @@
         scratch=[field],
         aliases={11 + slot: slot for slot in range(4)},
     )
-    surf_3, east_3, south_3, total_3, given_3 = call(
+    surf_3, east_3, south_3, total_3, own_term, partner_term, other_term = call(
         functools.partial(third_kernel, corridor, tiles),
         "third",
-        [field] * 4 + [small],
-        (surf_2, east_2, south_2, *faces, total_2, keep, count, given_2),
-    )
-    own_term, partner_term, other_term = call(
-        functools.partial(terms_kernel, corridor),
-        "terms",
-        [term] * 3,
-        (own, surf_3, given_3, takes, masks, takes_near, masks_near),
+        [field] * 4 + [term] * 3,
+        (
+            *(surf_2, east_2, south_2, *faces, total_2, keep, count, given_2),
+            *(own, takes, masks, takes_near, masks_near),
+        ),
     )
     from_other = swapped(other_term.reshape(owned), 1)
     from_partner = swapped(partner_term.reshape(owned), 0)

time: 20.9 us -> 20.7 us (level)
    pallas_call x10 -> x9, Pallas kernels: 5.94 us -> 5.78 us  [call(): pl.pallas_call(kernel, out_shape=outs, in_specs=[VMEM_SPEC] * len(values)...]
  transfers between devices with their start and end apart: 7 -> 7, of which waited for: 1 -> 1; matrix products, arithmetic and copies ran while one was open for 0% -> 0% of each run, Pallas kernels for 30% -> 31%
where the time goes in v1:
time: 20.7 us; the launch traced here: 20.5 us
  starting transfers between devices  10.4 us (50%)
  Pallas kernels  8.46 us (41%)
  between operations  0.76 us (4%)
  other arithmetic  0.52 us (3%)
  waiting for transfers between devices  0.34 us (2%)
    ppermute x7, starting transfers between devices, swapped(): return lax.ppermute(value, 'gy', pairs)  10.4 us
    pallas_call x9, Pallas kernels, call(): pl.pallas_call(kernel, out_shape=outs, in_specs=[VMEM_SPEC] * len(values)...  5.78 us
    pallas_call x1, Pallas kernels, local(): pl.pallas_call(load_kernel, out_shape=[field] * 4 + [pltpu.VMEM((rows, co...  1.44 us
    pallas_call x1, Pallas kernels, local(): pl.pallas_call(pack_kernel, out_shape=[wide, pair], in_specs=[HBM_SPEC] *...  1.24 us
    add x1, other arithmetic, local(): river_section = own_term.reshape(owned) + from_other + from_partner  0.52 us
  transfers between devices with their start and end apart: 7, of which 1 were waited for; matrix products, arithmetic and copies ran while one was open for 0% of the time, Pallas kernels for 31%

profile of v1, /device:TPU:0, one launch (start us, length us, event | category | flops | bytes accessed | tf_op | source)
XLA Modules:
  0.0 20.5 jit_solution(955870915513777661)
XLA Ops:
  0.6 0.5 %collective-permute-start.1 = (s32[4,128]{1,0:T(4,128)}, s32[4,128]{1,0:T(4,128)S(1)}, u32[]{:S(2)}, u32[]{:S(2)}) collective-permute-start(s32[4,128]{1,0:T(4,128)} %cells.1), channel_id=1, source_target_pairs={{0,1},{1,0},{2,3},{3,2},{4,5},{5,4},{6,7},{7,6},{8,9},{9,8},{10,11... | collective-permute-start | bytes 6152 | tf_op jit(solution)/shard_map/ppermute | solution.py:37
  1.1 0.1 collective-permute-start
  1.2 1.2 %pack.1 = (f32[61,4,128]{2,1,0:T(4,128)S(1)}, f32[2,128]{1,0:T(2,128)S(1)}) custom-call(f32[32,1920]{1,0:T(8,128)} %depth_in.1, f32[32,1920]{1,0:T(8,128)} %bed_in.1, s32[32,1920]{1,0:T(8,128)} %rough_in.1, f32[32,1920]{1,0:T(8,128)} %east_in.1, f32[32,1920]{1,0:T(8,128)} %south_in.1, f32[1,128]{1,0:T(1,128)} %bitcast.15, s32[4,128]{1,0:T(4,128)} %cells.1, ...), custom_call_target="tpu_custom_call" | custom-call | tf_op jit(solution)/shard_map/pack/pallas_call | solution.py:688
  2.5 0.0 collective-permute-done
  2.5 0.0 collective-permute-done.1.cells.partner_cells
  2.5 0.7 %collective-permute-start.2 = (f32[61,4,128]{2,1,0:T(4,128)S(1)}, f32[61,4,128]{2,1,0:T(4,128)S(1)}, u32[]{:S(2)}, u32[]{:S(2)}) collective-permute-start(f32[61,4,128]{2,1,0:T(4,128)S(1)} %join.1), channel_id=1, source_target_pairs={{1,2},{2,1},{3,4},{4,3},{5,6},{6,5},{7,8},{8,7},{9,10},{10,9},{11,... | collective-permute-start | bytes 374792 | tf_op jit(solution)/shard_map/ppermute | solution.py:37
  3.2 1.4 %load.1 = (f32[40,1920]{1,0:T(8,128)S(1)}, f32[40,1920]{1,0:T(8,128)S(1)}, f32[40,1920]{1,0:T(8,128)S(1)}, f32[40,1920]{1,0:T(8,128)S(1)}, s32[32,1920]{1,0:T(8,128)S(1)}, /*index=5*/f32[8,128]{1,0:T(8,128)S(1)}) custom-call(f32[32,1920]{1,0:T(8,128)} %depth_in.1, f32[32,1920]{1,0:T(8,128)} %east_in.1, f32[32,1920]{1,0:T(8,128)} %south_in.1, ...), custom_call_target="tpu_custom_call" | custom-call | tf_op jit(solution)/shard_map/load/pallas_call | solution.py:716
  4.6 0.7 %prepare.1 = (f32[40,1920]{1,0:T(8,128)S(1)}, f32[40,1920]{1,0:T(8,128)S(1)}, f32[40,1920]{1,0:T(8,128)S(1)}, f32[40,1920]{1,0:T(8,128)S(1)}, f32[40,1920]{1,0:T...) custom-call(f32[8,128]{1,0:T(8,128)S(1)} %get-tuple-element.62.table, ...), custom_call_target="tpu_custom_call", output_to_operand_aliasing={{0}: (2, {}), {1}: (3, {}), {2}: (4, {}), {3}: (5, {})} | custom-call | tf_op jit(solution)/shard_map/prepare/pallas_call | solution.py:668
  5.3 4.4 %collective-permute-start.4 = (f32[60,4,128]{2,1,0:T(4,128)S(1)}, f32[60,4,128]{2,1,0:T(4,128)S(1)}, u32[]{:S(2)}, u32[]{:S(2)}) collective-permute-start(f32[60,4,128]{2,1,0:T(4,128)S(1)} %get-tuple-element.71), channel_id=1, source_target_pairs={{0,1},{1,0},{2,3},{3,2},{4,5},{5,4},{6,7},{7,6},{8,9},{9,8},{10,11... | collective-permute-start | bytes 368648 | tf_op jit(solution)/shard_map/ppermute | solution.py:37
  9.7 0.5 %nodes.1 = (f32[40,1920]{1,0:T(8,128)S(1)}, f32[40,1920]{1,0:T(8,128)S(1)}, bf16[2,256,512]{2,1,0:T(8,128)(2,1)S(1)}, f32[2,256,128]{2,1,0:T(8,128)S(1)}, f32[32...) custom-call(f32[40,1920]{1,0:T(8,128)S(1)} %get-tuple-element.68.surf.refs_0_, f32[2,128]{1,0:T(2,128)S(1)} %get-tuple-element.69.own.refs_8_, ...), custom_call_target="tpu_custom_call" | custom-call | tf_op jit(solution)/shard_map/nodes/pallas_call | solution.py:668
  10.2 0.0 collective-permute-done.2.by_other
  10.2 0.1 collective-permute-start.3
  10.3 0.3 %collective-permute-done.4.by_partner = f32[60,4,128]{2,1,0:T(4,128)S(1)} collective-permute-done((f32[60,4,128]{2,1,0:T(4,128)S(1)}, f32[60,4,128]{2,1,0:T(4,128)S(1)}, u32[]{:S(2)}, u32[]{:S(2)}) %collective-permute-start.4) | collective-permute-done | bytes 122912 | tf_op jit(solution)/shard_map/ppermute | solution.py:37
  10.6 0.6 %border.1 = (f32[40,1920]{1,0:T(8,128)S(1)}, f32[40,1920]{1,0:T(8,128)S(1)}, f32[40,1920]{1,0:T(8,128)S(1)}, f32[40,1920]{1,0:T(8,128)S(1)}, f32[40,1920]{1,0:T(...) custom-call(f32[60,4,128]{2,1,0:T(4,128)S(1)} %collective-permute-do, ...), custom_call_target="tpu_custom_call", output_to_operand_aliasing={{0}: (4, {}), {1}: (5, {}), {2}: (6, {}), {3}: (7, {}), {4}... | custom-call | tf_op jit(solution)/shard_map/border/pallas_call | solution.py:668
  11.2 0.3 %first.1 = (f32[40,1920]{1,0:T(8,128)S(1)}, f32[40,1920]{1,0:T(8,128)S(1)}, f32[40,1920]{1,0:T(8,128)S(1)}, f32[40,1920]{1,0:T(8,128)S(1)}) custom-call(f32[40,1920]{1,0:T(8,128)S(1)} %get-tuple-element.82.surf, f32[40,1920]{1,0:T(8,128)S(1)} %get-tuple-element.83.east, f32[40,1920]{1,0:T(8,128)S(1)} %get-tuple-element.84.south, ...), custom_call_target="tpu_custom_call" | custom-call | tf_op jit(solution)/shard_map/first/pallas_call | solution.py:668
  11.6 0.0 collective-permute-done.3.far
  11.6 1.0 %second.1 = (f32[40,1920]{1,0:T(8,128)S(1)}, f32[40,1920]{1,0:T(8,128)S(1)}, f32[40,1920]{1,0:T(8,128)S(1)}, f32[40,1920]{1,0:T(8,128)S(1)}, f32[40,1920]{1,0:T(...) custom-call(f32[2,128]{1,0:T(2,128)S(1)} %collective-permute-done.3., ...), custom_call_target="tpu_custom_call", output_to_operand_aliasing={{0}: (11, {}), {1}: (12, {}), {2}: (13, {}), {3}: (14, {})} | custom-call | tf_op jit(solution)/shard_map/second/pallas_call | solution.py:668
  12.6 1.1 %third.1 = (f32[40,1920]{1,0:T(8,128)S(1)}, f32[40,1920]{1,0:T(8,128)S(1)}, f32[40,1920]{1,0:T(8,128)S(1)}, f32[40,1920]{1,0:T(8,128)S(1)}, f32[1,128]{1,0:T(1,1...) custom-call(f32[40,1920]{1,0:T(8,128)S(1)} %get-tuple-element.97.surf.surf_2, ...), custom_call_target="tpu_custom_call" | custom-call | tf_op jit(solution)/shard_map/third/pallas_call | solution.py:668
  13.8 0.7 %collective-permute-start.5 = (f32[128]{0:T(128)S(1)}, f32[128]{0:T(128)S(1)}, u32[]{:S(2)}, u32[]{:S(2)}) collective-permute-start(f32[128]{0:T(128)S(1)} %bitcast.12), channel_id=1, source_target_pairs={{1,2},{2,1},{3,4},{4,3},{5,6},{6,5},{7,8},{8,7},{9,10},{10,9},{11,... | collective-permute-start | bytes 1544 | tf_op jit(solution)/shard_map/ppermute | solution.py:37
  14.5 4.0 %collective-permute-start.6 = (f32[128]{0:T(128)S(1)}, f32[128]{0:T(128)S(1)}, u32[]{:S(2)}, u32[]{:S(2)}) collective-permute-start(f32[128]{0:T(128)S(1)} %bitcast.11), channel_id=1, source_target_pairs={{0,1},{1,0},{2,3},{3,2},{4,5},{5,4},{6,7},{7,6},{8,9},{9,8},{10,11... | collective-permute-start | bytes 1544 | tf_op jit(solution)/shard_map/ppermute | solution.py:37
  18.5 1.5 %last.1 = (f32[40,1920]{1,0:T(8,128)S(1)}, f32[32,1920]{1,0:T(8,128)}, f32[32,1920]{1,0:T(8,128)}, f32[32,1920]{1,0:T(8,128)}) custom-call(f32[40,1920]{1,0:T(8,128)S(1)} %get-tuple-element.97.surf.surf_2, f32[40,1920]{1,0:T(8,128)S(1)} %get-tuple-element.98.east.east_2, ...), custom_call_target="tpu_custom_call", output_to_operand_aliasing={{0}: (11, {})} | custom-call | tf_op jit(solution)/shard_map/last/pallas_call | solution.py:668
  19.9 0.0 collective-permute-done.5
  20.0 0.0 collective-permute-done.6
  20.0 0.5 %fusion = f32[128]{0:T(128)} fusion(f32[128]{0:T(128)S(1)} %collective-permute-done.6, f32[128]{0:T(128)S(1)} %collective-permute-done.5, f32[1,128]{1,0:T(1,128)S(1)} %get-tuple-element.115), kind=kLoop, calls=%fused_computation.1 | loop fusion | flops 256 | bytes 2048 | tf_op jit(solution)/shard_map/add | solution.py:790
  (2 shorter events, 0.0 us)
Async XLA Ops:
  0.6 1.9 %collective-permute-start.1 = (s32[4,128]{1,0:T(4,128)}, s32[4,128]{1,0:T(4,128)S(1)}, u32[]{:S(2)}, u32[]{:S(2)}) collective-permute-start(s32[4,128]{1,0:T(4,128)} %cells.1), channel_id=1, source_target_pairs={{0,1},{1,0},{2,3},{3,2},{4,5},{5,4},{6,7},{7,6},{8,9},{9,8},{10,11... | collective-permute-start | bytes 6152 | tf_op jit(solution)/shard_map/ppermute | solution.py:37
  1.1 1.3 %collective-permute-start = (f32[128]{0:T(128)}, f32[128]{0:T(128)S(1)}, u32[]{:S(2)}, u32[]{:S(2)}) collective-permute-start(f32[128]{0:T(128)} %param.11), channel_id=1, source_target_pairs={{0,1},{1,0},{2,3},{3,2},{4,5},{5,4},{6,7},{7,6},{8,9},{9,8},{10,11... | collective-permute-start | bytes 1544 | tf_op jit(solution)/shard_map/ppermute | solution.py:37
  2.5 7.7 %collective-permute-start.2 = (f32[61,4,128]{2,1,0:T(4,128)S(1)}, f32[61,4,128]{2,1,0:T(4,128)S(1)}, u32[]{:S(2)}, u32[]{:S(2)}) collective-permute-start(f32[61,4,128]{2,1,0:T(4,128)S(1)} %join.1), channel_id=1, source_target_pairs={{1,2},{2,1},{3,4},{4,3},{5,6},{6,5},{7,8},{8,7},{9,10},{10,9},{11,... | collective-permute-start | bytes 374792 | tf_op jit(solution)/shard_map/ppermute | solution.py:37
  5.3 5.3 %collective-permute-start.4 = (f32[60,4,128]{2,1,0:T(4,128)S(1)}, f32[60,4,128]{2,1,0:T(4,128)S(1)}, u32[]{:S(2)}, u32[]{:S(2)}) collective-permute-start(f32[60,4,128]{2,1,0:T(4,128)S(1)} %get-tuple-element.71), channel_id=1, source_target_pairs={{0,1},{1,0},{2,3},{3,2},{4,5},{5,4},{6,7},{7,6},{8,9},{9,8},{10,11... | collective-permute-start | bytes 368648 | tf_op jit(solution)/shard_map/ppermute | solution.py:37
  10.2 1.3 %collective-permute-start.3 = (f32[2,128]{1,0:T(2,128)S(1)}, f32[2,128]{1,0:T(2,128)S(1)}, u32[]{:S(2)}, u32[]{:S(2)}) collective-permute-start(f32[2,128]{1,0:T(2,128)S(1)} %relay.1.near), channel_id=1, source_target_pairs={{0,1},{1,0},{2,3},{3,2},{4,5},{5,4},{6,7},{7,6},{8,9},{9,8},{10,11... | collective-permute-start | bytes 3080 | tf_op jit(solution)/shard_map/ppermute | solution.py:37
  13.8 6.2 %collective-permute-start.5 = (f32[128]{0:T(128)S(1)}, f32[128]{0:T(128)S(1)}, u32[]{:S(2)}, u32[]{:S(2)}) collective-permute-start(f32[128]{0:T(128)S(1)} %bitcast.12), channel_id=1, source_target_pairs={{1,2},{2,1},{3,4},{4,3},{5,6},{6,5},{7,8},{8,7},{9,10},{10,9},{11,... | collective-permute-start | bytes 1544 | tf_op jit(solution)/shard_map/ppermute | solution.py:37
  14.5 5.5 %collective-permute-start.6 = (f32[128]{0:T(128)S(1)}, f32[128]{0:T(128)S(1)}, u32[]{:S(2)}, u32[]{:S(2)}) collective-permute-start(f32[128]{0:T(128)S(1)} %bitcast.11), channel_id=1, source_target_pairs={{0,1},{1,0},{2,3},{3,2},{4,5},{5,4},{6,7},{7,6},{8,9},{9,8},{10,11... | collective-permute-start | bytes 1544 | tf_op jit(solution)/shard_map/ppermute | solution.py:37

commit v2 on v1

--- a/solution.py
+++ b/solution.py
@@ -558,7 +558,7 @@
 def third_kernel(corridor, tiles, surf, east, south, *refs):
     faces = refs[:4]
     total, keep, count, given_2, own, takes, masks, takes_near, masks_near = refs[4:13]
-    surf_3, east_3, south_3, total_3, own_term, partner_term, other_term = refs[13:]
+    surf_3, east_3, south_3, total_3, own_term, sent = refs[13:]
     ext, columns = surf.shape
     rows = ext - 2 * HALO
     mine = slice(0, rows)
@@ -595,8 +595,12 @@
         preferred_element_type=jnp.float32,
     )[0:1]
     own_term[...] = (1.0 - corridor * DRAIN) ** STEPS * own[0:1, :] + terms[:, :owned]
-    partner_term[...] = terms[:, owned : 2 * owned]
-    other_term[...] = terms[:, 2 * owned :]
+    position = lax.axis_index("gy")
+    side = jnp.where(position % 2 == 0, 1, -1)
+    tile = lax.broadcasted_iota(jnp.int32, (tiles, owned), 0)
+    sent[...] = jnp.where(tile == position + side, terms[:, owned : 2 * owned], 0.0) + jnp.where(
+        tile == position - side, terms[:, 2 * owned :], 0.0
+    )
 
 
 def last_kernel(corridor, tiles, surf_2, east_2, south_3, *refs):
@@ -768,17 +772,16 @@
         scratch=[field],
         aliases={11 + slot: slot for slot in range(4)},
     )
-    surf_3, east_3, south_3, total_3, own_term, partner_term, other_term = call(
+    surf_3, east_3, south_3, total_3, own_term, sent = call(
         functools.partial(third_kernel, corridor, tiles),
         "third",
-        [field] * 4 + [term] * 3,
+        [field] * 4 + [term, pltpu.VMEM((tiles, owned), jnp.float32)],
         (
             *(surf_2, east_2, south_2, *faces, total_2, keep, count, given_2),
             *(own, takes, masks, takes_near, masks_near),
         ),
     )
-    from_other = swapped(other_term.reshape(owned), 1)
-    from_partner = swapped(partner_term.reshape(owned), 0)
+    received = lax.all_to_all(sent, "gy", 0, 0, tiled=True)
     _, depth, flux_east, flux_south = call(
         functools.partial(last_kernel, corridor, tiles),
         "last",
@@ -787,7 +790,7 @@
         scratch=[small, small, field, field, pltpu.SemaphoreType.DMA((2 + -(-chunks // 5),))],
         aliases={11: 0},
     )
-    river_section = own_term.reshape(owned) + from_other + from_partner
+    river_section = own_term.reshape(owned) + jnp.sum(received, axis=0)
     return (depth, flux_east, flux_south, river_section)
 
 

time: 20.7 us -> 29.1 us (1.41)
  local copies, waits for them, and re-layouts: 0 us -> 3.36 us
  waiting for transfers between devices: 0.34 us -> 3.33 us
  starting transfers between devices: 10.4 us -> 11.7 us
  Pallas kernels: 8.46 us -> 9.11 us
    all_to_all x0 -> x1, starting transfers between devices: none -> 5.97 us  [local(): received = lax.all_to_all(sent, 'gy', 0, 0, tiled=True)]
    ppermute x7 -> x5, starting transfers between devices: 10.4 us -> 5.72 us  [swapped(): return lax.ppermute(value, 'gy', pairs)]
    unnamed x0 -> x8, local copies, waits for them, and re-layouts: none -> 3.36 us
    all_to_all x0 -> x1, waiting for transfers between devices: none -> 2.99 us  [local(): received = lax.all_to_all(sent, 'gy', 0, 0, tiled=True)]
    pallas_call x9, Pallas kernels: 5.78 us -> 6.43 us  [call(): pl.pallas_call(kernel, out_shape=outs, in_specs=[VMEM_SPEC] * len(values)...]
  transfers between devices with their start and end apart: 7 -> 6, of which waited for: 1 -> 2; matrix products, arithmetic and copies ran while one was open for 0% -> 0% of each run, Pallas kernels for 31% -> 22%
where the time goes in v2:
time: 29.1 us; the launch traced here: 28.8 us
  starting transfers between devices  11.7 us (40%)
  Pallas kernels  9.11 us (31%)
  local copies, waits for them, and re-layouts  3.36 us (12%)
  waiting for transfers between devices  3.33 us (11%)
  between operations  0.76 us (3%)
  other arithmetic  0.55 us (2%)
    pallas_call x9, Pallas kernels, call(): pl.pallas_call(kernel, out_shape=outs, in_specs=[VMEM_SPEC] * len(values)...  6.43 us
    all_to_all x1, starting transfers between devices, local(): received = lax.all_to_all(sent, 'gy', 0, 0, tiled=True)  5.97 us
    ppermute x5, starting transfers between devices, swapped(): return lax.ppermute(value, 'gy', pairs)  5.72 us
    unnamed x8, local copies, waits for them, and re-layouts  3.36 us
    all_to_all x1, waiting for transfers between devices, local(): received = lax.all_to_all(sent, 'gy', 0, 0, tiled=True)  2.99 us
    pallas_call x1, Pallas kernels, local(): pl.pallas_call(load_kernel, out_shape=[field] * 4 + [pltpu.VMEM((rows, co...  1.44 us
    pallas_call x1, Pallas kernels, local(): pl.pallas_call(pack_kernel, out_shape=[wide, pair], in_specs=[HBM_SPEC] *...  1.24 us
  transfers between devices with their start and end apart: 6, of which 2 were waited for; matrix products, arithmetic and copies ran while one was open for 0% of the time, Pallas kernels for 22%

profile of v2, /device:TPU:0, one launch (start us, length us, event | category | flops | bytes accessed | tf_op | source)
XLA Modules:
  0.0 28.8 jit_solution(2886802747917928086)
XLA Ops:
  0.6 0.5 %collective-permute-start.1 = (s32[4,128]{1,0:T(4,128)}, s32[4,128]{1,0:T(4,128)S(1)}, u32[]{:S(2)}, u32[]{:S(2)}) collective-permute-start(s32[4,128]{1,0:T(4,128)} %cells.1), channel_id=1, source_target_pairs={{0,1},{1,0},{2,3},{3,2},{4,5},{5,4},{6,7},{7,6},{8,9},{9,8},{10,11... | collective-permute-start | bytes 6152 | tf_op jit(solution)/shard_map/ppermute | solution.py:37
  1.1 0.1 collective-permute-start
  1.2 1.2 %pack.1 = (f32[61,4,128]{2,1,0:T(4,128)S(1)}, f32[2,128]{1,0:T(2,128)S(1)}) custom-call(f32[32,1920]{1,0:T(8,128)} %depth_in.1, f32[32,1920]{1,0:T(8,128)} %bed_in.1, s32[32,1920]{1,0:T(8,128)} %rough_in.1, f32[32,1920]{1,0:T(8,128)} %east_in.1, f32[32,1920]{1,0:T(8,128)} %south_in.1, f32[1,128]{1,0:T(1,128)} %bitcast.12, s32[4,128]{1,0:T(4,128)} %cells.1, ...), custom_call_target="tpu_custom_call" | custom-call | tf_op jit(solution)/shard_map/pack/pallas_call | solution.py:692
  2.5 0.0 collective-permute-done
  2.5 0.0 collective-permute-done.1.cells.partner_cells
  2.5 0.7 %collective-permute-start.2 = (f32[61,4,128]{2,1,0:T(4,128)S(1)}, f32[61,4,128]{2,1,0:T(4,128)S(1)}, u32[]{:S(2)}, u32[]{:S(2)}) collective-permute-start(f32[61,4,128]{2,1,0:T(4,128)S(1)} %join.1), channel_id=1, source_target_pairs={{1,2},{2,1},{3,4},{4,3},{5,6},{6,5},{7,8},{8,7},{9,10},{10,9},{11,... | collective-permute-start | bytes 374792 | tf_op jit(solution)/shard_map/ppermute | solution.py:37
  3.2 1.4 %load.1 = (f32[40,1920]{1,0:T(8,128)S(1)}, f32[40,1920]{1,0:T(8,128)S(1)}, f32[40,1920]{1,0:T(8,128)S(1)}, f32[40,1920]{1,0:T(8,128)S(1)}, s32[32,1920]{1,0:T(8,128)S(1)}, /*index=5*/f32[8,128]{1,0:T(8,128)S(1)}) custom-call(f32[32,1920]{1,0:T(8,128)} %depth_in.1, f32[32,1920]{1,0:T(8,128)} %east_in.1, f32[32,1920]{1,0:T(8,128)} %south_in.1, ...), custom_call_target="tpu_custom_call" | custom-call | tf_op jit(solution)/shard_map/load/pallas_call | solution.py:720
  4.6 0.7 %prepare.1 = (f32[40,1920]{1,0:T(8,128)S(1)}, f32[40,1920]{1,0:T(8,128)S(1)}, f32[40,1920]{1,0:T(8,128)S(1)}, f32[40,1920]{1,0:T(8,128)S(1)}, f32[40,1920]{1,0:T...) custom-call(f32[8,128]{1,0:T(8,128)S(1)} %get-tuple-element.61.table, ...), custom_call_target="tpu_custom_call", output_to_operand_aliasing={{0}: (2, {}), {1}: (3, {}), {2}: (4, {}), {3}: (5, {})} | custom-call | tf_op jit(solution)/shard_map/prepare/pallas_call | solution.py:672
  5.3 4.4 %collective-permute-start.4 = (f32[60,4,128]{2,1,0:T(4,128)S(1)}, f32[60,4,128]{2,1,0:T(4,128)S(1)}, u32[]{:S(2)}, u32[]{:S(2)}) collective-permute-start(f32[60,4,128]{2,1,0:T(4,128)S(1)} %get-tuple-element.70), channel_id=1, source_target_pairs={{0,1},{1,0},{2,3},{3,2},{4,5},{5,4},{6,7},{7,6},{8,9},{9,8},{10,11... | collective-permute-start | bytes 368648 | tf_op jit(solution)/shard_map/ppermute | solution.py:37
  9.7 0.5 %nodes.1 = (f32[40,1920]{1,0:T(8,128)S(1)}, f32[40,1920]{1,0:T(8,128)S(1)}, bf16[2,256,512]{2,1,0:T(8,128)(2,1)S(1)}, f32[2,256,128]{2,1,0:T(8,128)S(1)}, f32[32...) custom-call(f32[40,1920]{1,0:T(8,128)S(1)} %get-tuple-element.67.surf.refs_0_, f32[2,128]{1,0:T(2,128)S(1)} %get-tuple-element.68.own.refs_8_, ...), custom_call_target="tpu_custom_call" | custom-call | tf_op jit(solution)/shard_map/nodes/pallas_call | solution.py:672
  10.2 0.0 collective-permute-done.2.by_other
  10.2 0.1 collective-permute-start.3
  10.3 0.3 %collective-permute-done.4.by_partner = f32[60,4,128]{2,1,0:T(4,128)S(1)} collective-permute-done((f32[60,4,128]{2,1,0:T(4,128)S(1)}, f32[60,4,128]{2,1,0:T(4,128)S(1)}, u32[]{:S(2)}, u32[]{:S(2)}) %collective-permute-start.4) | collective-permute-done | bytes 122912 | tf_op jit(solution)/shard_map/ppermute | solution.py:37
  10.7 0.6 %border.1 = (f32[40,1920]{1,0:T(8,128)S(1)}, f32[40,1920]{1,0:T(8,128)S(1)}, f32[40,1920]{1,0:T(8,128)S(1)}, f32[40,1920]{1,0:T(8,128)S(1)}, f32[40,1920]{1,0:T(...) custom-call(f32[60,4,128]{2,1,0:T(4,128)S(1)} %collective-permute-do, ...), custom_call_target="tpu_custom_call", output_to_operand_aliasing={{0}: (4, {}), {1}: (5, {}), {2}: (6, {}), {3}: (7, {}), {4}... | custom-call | tf_op jit(solution)/shard_map/border/pallas_call | solution.py:672
  11.2 0.3 %first.1 = (f32[40,1920]{1,0:T(8,128)S(1)}, f32[40,1920]{1,0:T(8,128)S(1)}, f32[40,1920]{1,0:T(8,128)S(1)}, f32[40,1920]{1,0:T(8,128)S(1)}) custom-call(f32[40,1920]{1,0:T(8,128)S(1)} %get-tuple-element.81.surf, f32[40,1920]{1,0:T(8,128)S(1)} %get-tuple-element.82.east, f32[40,1920]{1,0:T(8,128)S(1)} %get-tuple-element.83.south, ...), custom_call_target="tpu_custom_call" | custom-call | tf_op jit(solution)/shard_map/first/pallas_call | solution.py:672
  11.6 0.0 collective-permute-done.3.far
  11.6 1.1 %second.1 = (f32[40,1920]{1,0:T(8,128)S(1)}, f32[40,1920]{1,0:T(8,128)S(1)}, f32[40,1920]{1,0:T(8,128)S(1)}, f32[40,1920]{1,0:T(8,128)S(1)}, f32[40,1920]{1,0:T(...) custom-call(f32[2,128]{1,0:T(2,128)S(1)} %collective-permute-done.3., ...), custom_call_target="tpu_custom_call", output_to_operand_aliasing={{0}: (11, {}), {1}: (12, {}), {2}: (13, {}), {3}: (14, {})} | custom-call | tf_op jit(solution)/shard_map/second/pallas_call | solution.py:672
  12.6 1.8 %third.1 = (f32[40,1920]{1,0:T(8,128)S(1)}, f32[40,1920]{1,0:T(8,128)S(1)}, f32[40,1920]{1,0:T(8,128)S(1)}, f32[40,1920]{1,0:T(8,128)S(1)}, f32[1,128]{1,0:T(1,128)S(1)}, /*index=5*/f32[16,128]{1,0:T(8,128)}) custom-call(f32[40,1920]{1,0:T(8,128)S(1)} %get-tuple-element.96.surf.surf_2, f32[40,1920]{1,0:T(8,128)S(1)} %get-tuple-element.97.east.east_2, ...), custom_call_target="tpu_custom_call" | custom-call | tf_op jit(solution)/shard_map/third/pallas_call | solution.py:672
  14.4 0.0 copy-start
  14.4 0.7 %copy-done = f32[40,1920]{1,0:T(8,128)} copy-done((f32[40,1920]{1,0:T(8,128)}, f32[40,1920]{1,0:T(8,128)S(1)}, u32[]{:S(2)}) %copy-start) | copy-done | bytes 307224
  15.1 0.0 copy-start.2
  15.1 0.7 %copy-done.2 = f32[40,1920]{1,0:T(8,128)} copy-done((f32[40,1920]{1,0:T(8,128)}, f32[40,1920]{1,0:T(8,128)S(1)}, u32[]{:S(2)}) %copy-start.2) | copy-done | bytes 307224
  15.9 6.0 %all-to-all-start = ((f32[16,1,128]{2,1,0:T(1,128)}), f32[16,1,128]{2,1,0:T(1,128)S(1)}, u32[]{:S(2)}, u32[]{:S(2)}) async-start(f32[16,1,128]{2,1,0:T(1,128)} %bitcast.5), calls=%async_computation | async-start | bytes 16384 | tf_op jit(solution)/shard_map/all_to_all | solution.py:784
  21.8 0.0 copy-start.1
  21.9 1.0 %copy-done.1 = f32[40,1920]{1,0:T(8,128)S(1)} copy-done((f32[40,1920]{1,0:T(8,128)S(1)}, f32[40,1920]{1,0:T(8,128)}, u32[]{:S(2)}) %copy-start.1) | copy-done | bytes 307224
  22.8 0.0 copy-start.3
  22.8 1.0 %copy-done.3 = f32[40,1920]{1,0:T(8,128)S(1)} copy-done((f32[40,1920]{1,0:T(8,128)S(1)}, f32[40,1920]{1,0:T(8,128)}, u32[]{:S(2)}) %copy-start.3) | copy-done | bytes 307224
  23.8 1.5 %last.1 = (f32[40,1920]{1,0:T(8,128)S(1)}, f32[32,1920]{1,0:T(8,128)}, f32[32,1920]{1,0:T(8,128)}, f32[32,1920]{1,0:T(8,128)}) custom-call(f32[40,1920]{1,0:T(8,128)S(1)} %get-tuple-element.96.surf.surf_2, f32[40,1920]{1,0:T(8,128)S(1)} %get-tuple-element.97.east.east_2, f32[40,1920]{1,0:T(8,128)S(1)} %copy-done.1, ...), custom_call_target="tpu_custom_call", output_to_operand_aliasing={{0}: (11, {})} | custom-call | tf_op jit(solution)/shard_map/last/pallas_call | solution.py:672
  25.3 3.0 %all-to-all-done = f32[16,1,128]{2,1,0:T(1,128)S(1)} async-done(((f32[16,1,128]{2,1,0:T(1,128)}), f32[16,1,128]{2,1,0:T(1,128)S(1)}, u32[]{:S(2)}, u32[]{:S(2)}) %all-to-all-start) | async-done | bytes 8224 | tf_op jit(solution)/shard_map/all_to_all | solution.py:784
  28.3 0.5 %bitcast_add_fusion = f32[128]{0:T(128)} fusion(f32[128]{0:T(128)S(1)} %reduce_sum.9, f32[1,128]{1,0:T(1,128)S(1)} %get-tuple-element.114), kind=kLoop, calls=%fused_computation | loop fusion | flops 128 | bytes 1536 | tf_op jit(solution)/shard_map/add | solution.py:793
  (3 shorter events, 0.0 us)
Async XLA Ops:
  0.6 1.9 %collective-permute-start.1 = (s32[4,128]{1,0:T(4,128)}, s32[4,128]{1,0:T(4,128)S(1)}, u32[]{:S(2)}, u32[]{:S(2)}) collective-permute-start(s32[4,128]{1,0:T(4,128)} %cells.1), channel_id=1, source_target_pairs={{0,1},{1,0},{2,3},{3,2},{4,5},{5,4},{6,7},{7,6},{8,9},{9,8},{10,11... | collective-permute-start | bytes 6152 | tf_op jit(solution)/shard_map/ppermute | solution.py:37
  1.1 1.3 %collective-permute-start = (f32[128]{0:T(128)}, f32[128]{0:T(128)S(1)}, u32[]{:S(2)}, u32[]{:S(2)}) collective-permute-start(f32[128]{0:T(128)} %param.11), channel_id=1, source_target_pairs={{0,1},{1,0},{2,3},{3,2},{4,5},{5,4},{6,7},{7,6},{8,9},{9,8},{10,11... | collective-permute-start | bytes 1544 | tf_op jit(solution)/shard_map/ppermute | solution.py:37
  2.5 7.7 %collective-permute-start.2 = (f32[61,4,128]{2,1,0:T(4,128)S(1)}, f32[61,4,128]{2,1,0:T(4,128)S(1)}, u32[]{:S(2)}, u32[]{:S(2)}) collective-permute-start(f32[61,4,128]{2,1,0:T(4,128)S(1)} %join.1), channel_id=1, source_target_pairs={{1,2},{2,1},{3,4},{4,3},{5,6},{6,5},{7,8},{8,7},{9,10},{10,9},{11,... | collective-permute-start | bytes 374792 | tf_op jit(solution)/shard_map/ppermute | solution.py:37
  5.3 5.3 %collective-permute-start.4 = (f32[60,4,128]{2,1,0:T(4,128)S(1)}, f32[60,4,128]{2,1,0:T(4,128)S(1)}, u32[]{:S(2)}, u32[]{:S(2)}) collective-permute-start(f32[60,4,128]{2,1,0:T(4,128)S(1)} %get-tuple-element.70), channel_id=1, source_target_pairs={{0,1},{1,0},{2,3},{3,2},{4,5},{5,4},{6,7},{7,6},{8,9},{9,8},{10,11... | collective-permute-start | bytes 368648 | tf_op jit(solution)/shard_map/ppermute | solution.py:37
  10.2 1.3 %collective-permute-start.3 = (f32[2,128]{1,0:T(2,128)S(1)}, f32[2,128]{1,0:T(2,128)S(1)}, u32[]{:S(2)}, u32[]{:S(2)}) collective-permute-start(f32[2,128]{1,0:T(2,128)S(1)} %relay.1.near), channel_id=1, source_target_pairs={{0,1},{1,0},{2,3},{3,2},{4,5},{5,4},{6,7},{7,6},{8,9},{9,8},{10,11... | collective-permute-start | bytes 3080 | tf_op jit(solution)/shard_map/ppermute | solution.py:37
  14.4 0.7 %copy-start = (f32[40,1920]{1,0:T(8,128)}, f32[40,1920]{1,0:T(8,128)S(1)}, u32[]{:S(2)}) copy-start(f32[40,1920]{1,0:T(8,128)S(1)} %get-tuple-element.106.south_3) | copy-start | bytes 921604
  15.1 0.7 %copy-start.2 = (f32[40,1920]{1,0:T(8,128)}, f32[40,1920]{1,0:T(8,128)S(1)}, u32[]{:S(2)}) copy-start(f32[40,1920]{1,0:T(8,128)S(1)} %get-tuple-element.107.refs_5_) | copy-start | bytes 921604
  15.9 12.4 %all-to-all-start = ((f32[16,1,128]{2,1,0:T(1,128)}), f32[16,1,128]{2,1,0:T(1,128)S(1)}, u32[]{:S(2)}, u32[]{:S(2)}) async-start(f32[16,1,128]{2,1,0:T(1,128)} %bitcast.5), calls=%async_computation | async-start | bytes 16384 | tf_op jit(solution)/shard_map/all_to_all | solution.py:784
  21.8 1.0 %copy-start.1 = (f32[40,1920]{1,0:T(8,128)S(1)}, f32[40,1920]{1,0:T(8,128)}, u32[]{:S(2)}) copy-start(f32[40,1920]{1,0:T(8,128)} %copy-done) | copy-start | bytes 921604
  22.8 1.0 %copy-start.3 = (f32[40,1920]{1,0:T(8,128)S(1)}, f32[40,1920]{1,0:T(8,128)}, u32[]{:S(2)}) copy-start(f32[40,1920]{1,0:T(8,128)} %copy-done.2) | copy-start | bytes 921604

commit v3 on v1

--- a/solution.py
+++ b/solution.py
@@ -175,6 +175,7 @@
         pltpu.make_async_copy(source, target, sems.at[slot])
         for slot, (source, target) in enumerate(
             (
+                (table_in, table),
                 (rough.at[near, :], held_rough),
                 (bed.at[near, :], held.at[1]),
                 (depth.at[near, :], held.at[0]),
@@ -182,21 +183,21 @@
                 (south.at[near, :], held.at[3]),
                 (section, own.at[pl.ds(0, 1), :]),
                 (cells, held_cells),
-                (table_in, table),
             )
         )
     ]
     for copy in copies:
         copy.start()
-    for copy in copies:
-        copy.wait()
-    own[1:2, :] = (held_cells[0:1, :] + 1).astype(jnp.float32)
+    copies[0].wait()
+    copies[1].wait()
     entries = [
         jnp.broadcast_to(table[:, k : k + 1], (1, LANES)) for k in range(table.shape[1])
     ]
     manns = [looked_up(held_rough[:, cols(chunk)], entries) for chunk in range(chunks)]
     row = lax.broadcasted_iota(jnp.int32, (8, LANES), 0)
+    copies[2].wait()
     beds = [held[1, :, cols(chunk)] for chunk in range(chunks)]
+    copies[3].wait()
     surfs = [held[0, :, cols(chunk)] + beds[chunk] for chunk in range(chunks)]
 
     def moved(values):
@@ -206,6 +207,9 @@
         return [jnp.where(edge, rolled[c + 1], rolled[c]) for c in range(chunks)]
 
     beds_left, surfs_left, manns_left = moved(beds), moved(surfs), moved(manns)
+    for copy in copies[4:]:
+        copy.wait()
+    own[1:2, :] = (held_cells[0:1, :] + 1).astype(jnp.float32)
     for chunk in range(chunks):
         at = cols(chunk)
         m0, b0, s0 = manns[chunk], beds[chunk], surfs[chunk]
@@ -230,9 +234,10 @@
     to_other[nodes, 3:4, :] = (cells[0:1, :] + 1).astype(jnp.float32)
 
 
-def relay_kernel(by_other, prepared, near):
+def relay_kernel(by_other, prepared, near, nodes):
     del prepared
     near[...] = by_other[by_other.shape[0] - 1, 0:2, :]
+    nodes[...] = by_other[by_other.shape[0] - 1]
 
 
 def picking(reach, rows, key, lane, takes, masks):
@@ -365,12 +370,9 @@
     chunks = columns // LANES
     position = lax.axis_index("gy")
     even = position % 2 == 0
-    beyond = by_other[4 * chunks, 2:4, :]
-    section = jnp.concatenate([near[0:1, :], beyond[0:1, :]], axis=1)
-    cell = jnp.concatenate([near[1:2, :], beyond[1:2, :]], axis=1)
-    valid, node_row, node_chunk, node_lane = located(cell, position, rows, ext, columns)
+    valid, node_row, node_chunk, node_lane = located(near[1:2, :], position, rows, ext, columns)
     key = jnp.where(valid, node_chunk * ext + node_row, -1)
-    starts, levels = scattered(section, key, node_lane, chunks * ext)
+    starts, levels = scattered(near[0:1, :], key, node_lane, chunks * ext)
 
     entries = [table_rows[k : k + 1, :] for k in range(table_rows.shape[0])]
     row = lax.broadcasted_iota(jnp.int32, (2 * HALO, LANES), 0)
@@ -392,8 +394,7 @@
         south[rows:, at] = flux
 
     key = jnp.where(valid & (node_row < rows), node_chunk * rows + node_row, -1)
-    owned = near.shape[1]
-    picking(reach, rows, key[:, :owned], node_lane[:, :owned], takes, masks)
+    picking(reach, rows, key, node_lane, takes, masks)
 
     wall = wall_of(ext, tiles)
     kept = lax.broadcasted_iota(jnp.int32, (16, LANES), 0) % 8 < 7
@@ -515,20 +516,34 @@
         surf_1[own, cols(chunk)] = new_surf
 
 
-def second_kernel(corridor, tiles, far, surf, east, south, *refs):
+def ahead_kernel(corridor, surf_1, east, south, *refs):
     faces = refs[:4]
-    number, total, given_1 = refs[4:7]
-    surf_1, total_1, count, keep = refs[11:15]
-    surf_2, east_2, south_2, total_2, given_2, total_0 = refs[15:]
+    total_1, count, given_1, east_2, south_2, total_2, given_2, sums_2 = refs[4:]
+    ext, columns = surf_1.shape
+    rows = ext - 2 * HALO
+    own = slice(0, rows)
+    sums = exchange(corridor, own, surf_1, total_1, count, total_2)
+    fluxes(own, rows - 8, None, (surf_1, east, south), faces, east_2, south_2)
+    for chunk in range(columns // LANES):
+        sums_2[:, cols(chunk)] = sums[chunk]
+    give(corridor, 1, surf_1, given_1, given_2)
+
+
+def second_kernel(corridor, tiles, far, beyond, surf, east, south, *refs):
+    faces = refs[:4]
+    number, total, sums_2 = refs[4:7]
+    surf_1, total_1, count, keep, east_2, south_2, total_2, surf_2, total_0 = refs[14:]
     ext, columns = surf.shape
     rows = ext - 2 * HALO
     chunks = columns // LANES
     position = lax.axis_index("gy")
-    tail = slice(rows, ext)
-
-    valid, node_row, node_chunk, node_lane = located(far[1:2, :], position, rows, ext, columns)
+    own, tail = slice(0, rows), slice(rows, ext)
+
+    section = jnp.concatenate([far[0:1, :], beyond[2:3, :]], axis=1)
+    cell = jnp.concatenate([far[1:2, :], beyond[3:4, :]], axis=1)
+    valid, node_row, node_chunk, node_lane = located(cell, position, rows, ext, columns)
     key = jnp.where(valid & (node_row >= rows), node_chunk * 8 + (node_row - rows), -1)
-    starts, levels = scattered(far[0:1, :], key, node_lane, chunks * 8)
+    starts, levels = scattered(section, key, node_lane, chunks * 8)
     starting = [
         number[tail, cols(chunk)] + starts[chunk * 8 : chunk * 8 + 8] for chunk in range(chunks)
     ]
@@ -539,17 +554,11 @@
         keep[tail, at] = 1.0 - FEED * covering[chunk]
         total_0[tail, at] = FEED * (total[tail, at] + levels[chunk * 8 : chunk * 8 + 8])
     sums = exchange(corridor, tail, surf, total_0, count, total_1)
-
-    own = slice(0, rows)
-    before = (surf_1, east, south)
-    fluxes(own, rows - 8, None, before, faces, east_2, south_2)
-    own_sums = exchange(corridor, own, surf_1, total_1, count, total_2)
-    give(corridor, 1, surf_1, given_1, given_2)
-
     for chunk, new_surf in settled(tail, surf, east, south, keep, sums):
         surf_1[tail, cols(chunk)] = new_surf
     tail_sums = exchange(corridor, tail, surf_1, total_1, count, total_2)
-    fluxes(tail, 0, wall_of(ext, tiles), before, faces, east_2, south_2)
+    fluxes(tail, 0, wall_of(ext, tiles), (surf_1, east, south), faces, east_2, south_2)
+    own_sums = [sums_2[:, cols(chunk)] for chunk in range(chunks)]
     for mine, sums in ((own, own_sums), (tail, tail_sums)):
         for chunk, new_surf in settled(mine, surf_1, east_2, south_2, keep, sums):
             surf_2[mine, cols(chunk)] = new_surf
@@ -740,7 +749,12 @@
         [field] * 2 + picks(2 * owned) + [small] * 2,
         (fields[0], own, partner_section, partner_cells),
     )
-    (near,) = call(relay_kernel, "relay", [pair], (by_other, masks))
+    near, beyond = call(
+        relay_kernel,
+        "relay",
+        [pair, pltpu.VMEM((HALO, LANES), jnp.float32)],
+        (by_other, masks),
+    )
     from_far = swapped(near, 0)
     *fields, takes_near, masks_near = call(
         functools.partial(border_kernel, corridor, tiles),
@@ -757,16 +771,22 @@
         (surf, east, south, number, total, windows),
         scratch=[field],
     )
-    surf_1, total_1, count, keep, surf_2, east_2, south_2, total_2, given_2 = call(
+    east_2, south_2, total_2, given_2, sums_2 = call(
+        functools.partial(ahead_kernel, corridor),
+        "ahead",
+        [field] * 3 + [small] * 2,
+        (surf_1, east, south, *faces, total_1, count, given_1),
+    )
+    surf_1, total_1, count, keep, east_2, south_2, total_2, surf_2 = call(
         functools.partial(second_kernel, corridor, tiles),
         "second",
-        [field] * 8 + [small],
+        [field] * 8,
         (
-            *(from_far, surf, east, south, *faces, number, total, given_1),
-            *(surf_1, total_1, count, keep),
+            *(from_far, beyond, surf, east, south, *faces, number, total, sums_2),
+            *(surf_1, total_1, count, keep, east_2, south_2, total_2),
         ),
         scratch=[field],
-        aliases={11 + slot: slot for slot in range(4)},
+        aliases={12 + slot: slot for slot in range(7)},
     )
     surf_3, east_3, south_3, total_3, own_term, partner_term, other_term = call(
         functools.partial(third_kernel, corridor, tiles),

time: 20.7 us -> 20.7 us (level)
  the two profiles are of different devices: /device:TPU:0 before, /device:TPU:7 now
where the time goes in v3:
time: 20.7 us; the launch traced here: 20.4 us
  Pallas kernels  8.69 us (42%)
  starting transfers between devices  8.33 us (40%)
  waiting for transfers between devices  2.08 us (10%)
  between operations  0.76 us (4%)
  other arithmetic  0.52 us (3%)
    ppermute x7, starting transfers between devices, swapped(): return lax.ppermute(value, 'gy', pairs)  8.33 us
    pallas_call x10, Pallas kernels, call(): pl.pallas_call(kernel, out_shape=outs, in_specs=[VMEM_SPEC] * len(values)...  5.95 us
    ppermute x7, waiting for transfers between devices, swapped(): return lax.ppermute(value, 'gy', pairs)  2.08 us
    pallas_call x1, Pallas kernels, local(): pl.pallas_call(load_kernel, out_shape=[field] * 4 + [pltpu.VMEM((rows, co...  1.44 us
    pallas_call x1, Pallas kernels, local(): pl.pallas_call(pack_kernel, out_shape=[wide, pair], in_specs=[HBM_SPEC] *...  1.3 us
    add x1, other arithmetic, local(): river_section = own_term.reshape(owned) + from_other + from_partner  0.52 us
  transfers between devices with their start and end apart: 7, of which 2 were waited for; matrix products, arithmetic and copies ran while one was open for 0% of the time, Pallas kernels for 33%

profile of v3, /device:TPU:7, one launch (start us, length us, event | category | flops | bytes accessed | tf_op | source)
XLA Modules:
  0.0 20.4 jit_solution(10862604115319367847)
XLA Ops:
  0.6 0.7 %collective-permute-start.1 = (s32[4,128]{1,0:T(4,128)}, s32[4,128]{1,0:T(4,128)S(1)}, u32[]{:S(2)}, u32[]{:S(2)}) collective-permute-start(s32[4,128]{1,0:T(4,128)} %cells.1), channel_id=1, source_target_pairs={{0,1},{1,0},{2,3},{3,2},{4,5},{5,4},{6,7},{7,6},{8,9},{9,8},{10,11... | collective-permute-start | bytes 6152 | tf_op jit(solution)/shard_map/ppermute | solution.py:37
  1.4 0.1 collective-permute-start
  1.4 1.3 %pack.1 = (f32[61,4,128]{2,1,0:T(4,128)S(1)}, f32[2,128]{1,0:T(2,128)S(1)}) custom-call(f32[32,1920]{1,0:T(8,128)} %depth_in.1, f32[32,1920]{1,0:T(8,128)} %bed_in.1, s32[32,1920]{1,0:T(8,128)} %rough_in.1, f32[32,1920]{1,0:T(8,128)} %east_in.1, f32[32,1920]{1,0:T(8,128)} %south_in.1, f32[1,128]{1,0:T(1,128)} %bitcast.15, s32[4,128]{1,0:T(4,128)} %cells.1, ...), custom_call_target="tpu_custom_call" | custom-call | tf_op jit(solution)/shard_map/pack/pallas_call | solution.py:697
  2.8 0.0 collective-permute-done
  2.8 0.0 collective-permute-done.1.cells.partner_cells
  2.8 3.5 %collective-permute-start.2 = (f32[61,4,128]{2,1,0:T(4,128)S(1)}, f32[61,4,128]{2,1,0:T(4,128)S(1)}, u32[]{:S(2)}, u32[]{:S(2)}) collective-permute-start(f32[61,4,128]{2,1,0:T(4,128)S(1)} %join.1), channel_id=1, source_target_pairs={{1,2},{2,1},{3,4},{4,3},{5,6},{6,5},{7,8},{8,7},{9,10},{10,9},{11,... | collective-permute-start | bytes 374792 | tf_op jit(solution)/shard_map/ppermute | solution.py:37
  6.3 1.4 %load.1 = (f32[40,1920]{1,0:T(8,128)S(1)}, f32[40,1920]{1,0:T(8,128)S(1)}, f32[40,1920]{1,0:T(8,128)S(1)}, f32[40,1920]{1,0:T(8,128)S(1)}, s32[32,1920]{1,0:T(8,128)S(1)}, /*index=5*/f32[8,128]{1,0:T(8,128)S(1)}) custom-call(f32[32,1920]{1,0:T(8,128)} %depth_in.1, f32[32,1920]{1,0:T(8,128)} %east_in.1, f32[32,1920]{1,0:T(8,128)} %south_in.1, ...), custom_call_target="tpu_custom_call" | custom-call | tf_op jit(solution)/shard_map/load/pallas_call | solution.py:725
  7.7 0.7 %prepare.1 = (f32[40,1920]{1,0:T(8,128)S(1)}, f32[40,1920]{1,0:T(8,128)S(1)}, f32[40,1920]{1,0:T(8,128)S(1)}, f32[40,1920]{1,0:T(8,128)S(1)}, f32[40,1920]{1,0:T...) custom-call(f32[8,128]{1,0:T(8,128)S(1)} %get-tuple-element.68.table, ...), custom_call_target="tpu_custom_call", output_to_operand_aliasing={{0}: (2, {}), {1}: (3, {}), {2}: (4, {}), {3}: (5, {})} | custom-call | tf_op jit(solution)/shard_map/prepare/pallas_call | solution.py:677
  8.4 0.1 collective-permute-start.4
  8.5 0.5 %nodes.1 = (f32[40,1920]{1,0:T(8,128)S(1)}, f32[40,1920]{1,0:T(8,128)S(1)}, bf16[2,256,512]{2,1,0:T(8,128)(2,1)S(1)}, f32[2,256,128]{2,1,0:T(8,128)S(1)}, f32[32...) custom-call(f32[40,1920]{1,0:T(8,128)S(1)} %get-tuple-element.74.surf.refs_0_, f32[2,128]{1,0:T(2,128)S(1)} %get-tuple-element.75.own.refs_8_, ...), custom_call_target="tpu_custom_call" | custom-call | tf_op jit(solution)/shard_map/nodes/pallas_call | solution.py:677
  9.0 1.0 %collective-permute-done.2.by_other = f32[61,4,128]{2,1,0:T(4,128)S(1)} collective-permute-done((f32[61,4,128]{2,1,0:T(4,128)S(1)}, f32[61,4,128]{2,1,0:T(4,128)S(1)}, u32[]{:S(2)}, u32[]{:S(2)}) %collective-permute-start.2) | collective-permute-done | bytes 124960 | tf_op jit(solution)/shard_map/ppermute | solution.py:37
  10.0 0.8 %collective-permute-start.3 = (f32[2,128]{1,0:T(2,128)S(1)}, f32[2,128]{1,0:T(2,128)S(1)}, u32[]{:S(2)}, u32[]{:S(2)}) collective-permute-start(f32[2,128]{1,0:T(2,128)S(1)} %get-tuple-element.77.near), channel_id=1, source_target_pairs={{0,1},{1,0},{2,3},{3,2},{4,5},{5,4},{6,7},{7,6},{8,9},{9,8},{10,11... | collective-permute-start | bytes 3080 | tf_op jit(solution)/shard_map/ppermute | solution.py:37
  10.8 0.0 collective-permute-done.4.by_partner
  10.8 0.5 %border.1 = (f32[40,1920]{1,0:T(8,128)S(1)}, f32[40,1920]{1,0:T(8,128)S(1)}, f32[40,1920]{1,0:T(8,128)S(1)}, f32[40,1920]{1,0:T(8,128)S(1)}, f32[40,1920]{1,0:T(...) custom-call(f32[60,4,128]{2,1,0:T(4,128)S(1)} %collective-permute-do, ...), custom_call_target="tpu_custom_call", output_to_operand_aliasing={{0}: (4, {}), {1}: (5, {}), {2}: (6, {}), {3}: (7, {}), {4}... | custom-call | tf_op jit(solution)/shard_map/border/pallas_call | solution.py:677
  11.3 0.3 %first.1 = (f32[40,1920]{1,0:T(8,128)S(1)}, f32[40,1920]{1,0:T(8,128)S(1)}, f32[40,1920]{1,0:T(8,128)S(1)}, f32[40,1920]{1,0:T(8,128)S(1)}) custom-call(f32[40,1920]{1,0:T(8,128)S(1)} %get-tuple-element.90.surf, f32[40,1920]{1,0:T(8,128)S(1)} %get-tuple-element.91.east, f32[40,1920]{1,0:T(8,128)S(1)} %get-tuple-element.92.south, ...), custom_call_target="tpu_custom_call" | custom-call | tf_op jit(solution)/shard_map/first/pallas_call | solution.py:677
  11.7 0.5 %ahead.1 = (f32[40,1920]{1,0:T(8,128)S(1)}, f32[40,1920]{1,0:T(8,128)S(1)}, f32[40,1920]{1,0:T(8,128)S(1)}, f32[32,1920]{1,0:T(8,128)S(1)}, f32[32,1920]{1,0:T(8,128)S(1)}) custom-call(f32[40,1920]{1,0:T(8,128)S(1)} %get-tuple-element.100.surf_1.refs_7_, f32[40,1920]{1,0:T(8,128)S(1)} %get-tuple-element.91.east, f32[40,1920]{1,0:T(8,128)S(1)} %get-tuple-element.92.south, ...), custom_call_target="tpu_custom_call" | custom-call | tf_op jit(solution)/shard_map/ahead/pallas_call | solution.py:677
  12.2 0.0 collective-permute-done.3.far
  12.2 0.7 %second.1 = (f32[40,1920]{1,0:T(8,128)S(1)}, f32[40,1920]{1,0:T(8,128)S(1)}, f32[40,1920]{1,0:T(8,128)S(1)}, f32[40,1920]{1,0:T(8,128)S(1)}, f32[40,1920]{1,0:T(...) custom-call(f32[2,128]{1,0:T(2,128)S(1)} %collective-permute-done.3., ...), custom_call_target="tpu_custom_call", output_to_operand_aliasing={{0}: (12, {}), {1}: (13, {}), {2}: (14, {}), {3}: (15, {}),... | custom-call | tf_op jit(solution)/shard_map/second/pallas_call | solution.py:677
  12.9 1.1 %third.1 = (f32[40,1920]{1,0:T(8,128)S(1)}, f32[40,1920]{1,0:T(8,128)S(1)}, f32[40,1920]{1,0:T(8,128)S(1)}, f32[40,1920]{1,0:T(8,128)S(1)}, f32[1,128]{1,0:T(1,1...) custom-call(f32[40,1920]{1,0:T(8,128)S(1)} %get-tuple-element.109.surf.surf_2, ...), custom_call_target="tpu_custom_call" | custom-call | tf_op jit(solution)/shard_map/third/pallas_call | solution.py:677
  14.1 3.1 %collective-permute-start.5 = (f32[128]{0:T(128)S(1)}, f32[128]{0:T(128)S(1)}, u32[]{:S(2)}, u32[]{:S(2)}) collective-permute-start(f32[128]{0:T(128)S(1)} %bitcast.12), channel_id=1, source_target_pairs={{1,2},{2,1},{3,4},{4,3},{5,6},{6,5},{7,8},{8,7},{9,10},{10,9},{11,... | collective-permute-start | bytes 1544 | tf_op jit(solution)/shard_map/ppermute | solution.py:37
  17.2 0.1 collective-permute-start.6
  17.3 1.5 %last.1 = (f32[40,1920]{1,0:T(8,128)S(1)}, f32[32,1920]{1,0:T(8,128)}, f32[32,1920]{1,0:T(8,128)}, f32[32,1920]{1,0:T(8,128)}) custom-call(f32[40,1920]{1,0:T(8,128)S(1)} %get-tuple-element.109.surf.surf_2, f32[40,1920]{1,0:T(8,128)S(1)} %get-tuple-element.110.east.east_2, ...), custom_call_target="tpu_custom_call", output_to_operand_aliasing={{0}: (11, {})} | custom-call | tf_op jit(solution)/shard_map/last/pallas_call | solution.py:677
  18.8 1.1 %collective-permute-done.5 = f32[128]{0:T(128)S(1)} collective-permute-done((f32[128]{0:T(128)S(1)}, f32[128]{0:T(128)S(1)}, u32[]{:S(2)}, u32[]{:S(2)}) %collective-permute-start.5) | collective-permute-done | bytes 544 | tf_op jit(solution)/shard_map/ppermute | solution.py:37
  19.8 0.0 collective-permute-done.6
  19.8 0.5 %fusion = f32[128]{0:T(128)} fusion(f32[128]{0:T(128)S(1)} %collective-permute-done.6, f32[128]{0:T(128)S(1)} %collective-permute-done.5, f32[1,128]{1,0:T(1,128)S(1)} %get-tuple-element.127), kind=kLoop, calls=%fused_computation.1 | loop fusion | flops 256 | bytes 2048 | tf_op jit(solution)/shard_map/add | solution.py:810
  (2 shorter events, 0.0 us)
Async XLA Ops:
  0.6 2.1 %collective-permute-start.1 = (s32[4,128]{1,0:T(4,128)}, s32[4,128]{1,0:T(4,128)S(1)}, u32[]{:S(2)}, u32[]{:S(2)}) collective-permute-start(s32[4,128]{1,0:T(4,128)} %cells.1), channel_id=1, source_target_pairs={{0,1},{1,0},{2,3},{3,2},{4,5},{5,4},{6,7},{7,6},{8,9},{9,8},{10,11... | collective-permute-start | bytes 6152 | tf_op jit(solution)/shard_map/ppermute | solution.py:37
  1.4 1.4 %collective-permute-start = (f32[128]{0:T(128)}, f32[128]{0:T(128)S(1)}, u32[]{:S(2)}, u32[]{:S(2)}) collective-permute-start(f32[128]{0:T(128)} %param.11), channel_id=1, source_target_pairs={{0,1},{1,0},{2,3},{3,2},{4,5},{5,4},{6,7},{7,6},{8,9},{9,8},{10,11... | collective-permute-start | bytes 1544 | tf_op jit(solution)/shard_map/ppermute | solution.py:37
  2.8 7.2 %collective-permute-start.2 = (f32[61,4,128]{2,1,0:T(4,128)S(1)}, f32[61,4,128]{2,1,0:T(4,128)S(1)}, u32[]{:S(2)}, u32[]{:S(2)}) collective-permute-start(f32[61,4,128]{2,1,0:T(4,128)S(1)} %join.1), channel_id=1, source_target_pairs={{1,2},{2,1},{3,4},{4,3},{5,6},{6,5},{7,8},{8,7},{9,10},{10,9},{11,... | collective-permute-start | bytes 374792 | tf_op jit(solution)/shard_map/ppermute | solution.py:37
  8.4 2.4 %collective-permute-start.4 = (f32[60,4,128]{2,1,0:T(4,128)S(1)}, f32[60,4,128]{2,1,0:T(4,128)S(1)}, u32[]{:S(2)}, u32[]{:S(2)}) collective-permute-start(f32[60,4,128]{2,1,0:T(4,128)S(1)} %get-tuple-element.79), channel_id=1, source_target_pairs={{0,1},{1,0},{2,3},{3,2},{4,5},{5,4},{6,7},{7,6},{8,9},{9,8},{10,11... | collective-permute-start | bytes 368648 | tf_op jit(solution)/shard_map/ppermute | solution.py:37
  10.0 2.2 %collective-permute-start.3 = (f32[2,128]{1,0:T(2,128)S(1)}, f32[2,128]{1,0:T(2,128)S(1)}, u32[]{:S(2)}, u32[]{:S(2)}) collective-permute-start(f32[2,128]{1,0:T(2,128)S(1)} %get-tuple-element.77.near), channel_id=1, source_target_pairs={{0,1},{1,0},{2,3},{3,2},{4,5},{5,4},{6,7},{7,6},{8,9},{9,8},{10,11... | collective-permute-start | bytes 3080 | tf_op jit(solution)/shard_map/ppermute | solution.py:37
  14.1 5.8 %collective-permute-start.5 = (f32[128]{0:T(128)S(1)}, f32[128]{0:T(128)S(1)}, u32[]{:S(2)}, u32[]{:S(2)}) collective-permute-start(f32[128]{0:T(128)S(1)} %bitcast.12), channel_id=1, source_target_pairs={{1,2},{2,1},{3,4},{4,3},{5,6},{6,5},{7,8},{8,7},{9,10},{10,9},{11,... | collective-permute-start | bytes 1544 | tf_op jit(solution)/shard_map/ppermute | solution.py:37
  17.2 2.6 %collective-permute-start.6 = (f32[128]{0:T(128)S(1)}, f32[128]{0:T(128)S(1)}, u32[]{:S(2)}, u32[]{:S(2)}) collective-permute-start(f32[128]{0:T(128)S(1)} %bitcast.11), channel_id=1, source_target_pairs={{0,1},{1,0},{2,3},{3,2},{4,5},{5,4},{6,7},{7,6},{8,9},{9,8},{10,11... | collective-permute-start | bytes 1544 | tf_op jit(solution)/shard_map/ppermute | solution.py:37

commit v4 on v1

--- a/solution.py
+++ b/solution.py
@@ -230,9 +230,11 @@
     to_other[nodes, 3:4, :] = (cells[0:1, :] + 1).astype(jnp.float32)
 
 
-def relay_kernel(by_other, prepared, near):
+def relay_kernel(by_other, prepared, near, beyond):
     del prepared
-    near[...] = by_other[by_other.shape[0] - 1, 0:2, :]
+    nodes = by_other.shape[0] - 1
+    near[...] = by_other[nodes, 0:2, :]
+    beyond[...] = by_other[nodes, 2:4, :]
 
 
 def picking(reach, rows, key, lane, takes, masks):
@@ -365,12 +367,9 @@
     chunks = columns // LANES
     position = lax.axis_index("gy")
     even = position % 2 == 0
-    beyond = by_other[4 * chunks, 2:4, :]
-    section = jnp.concatenate([near[0:1, :], beyond[0:1, :]], axis=1)
-    cell = jnp.concatenate([near[1:2, :], beyond[1:2, :]], axis=1)
-    valid, node_row, node_chunk, node_lane = located(cell, position, rows, ext, columns)
+    valid, node_row, node_chunk, node_lane = located(near[1:2, :], position, rows, ext, columns)
     key = jnp.where(valid, node_chunk * ext + node_row, -1)
-    starts, levels = scattered(section, key, node_lane, chunks * ext)
+    starts, levels = scattered(near[0:1, :], key, node_lane, chunks * ext)
 
     entries = [table_rows[k : k + 1, :] for k in range(table_rows.shape[0])]
     row = lax.broadcasted_iota(jnp.int32, (2 * HALO, LANES), 0)
@@ -392,8 +391,7 @@
         south[rows:, at] = flux
 
     key = jnp.where(valid & (node_row < rows), node_chunk * rows + node_row, -1)
-    owned = near.shape[1]
-    picking(reach, rows, key[:, :owned], node_lane[:, :owned], takes, masks)
+    picking(reach, rows, key, node_lane, takes, masks)
 
     wall = wall_of(ext, tiles)
     kept = lax.broadcasted_iota(jnp.int32, (16, LANES), 0) % 8 < 7
@@ -426,20 +424,23 @@
     bed_e, bed_s, drag_e, drag_s = faces
     ext, columns = surf.shape
     chunks = columns // LANES
-    rolled = pltpu.roll(surf[mine, cols(0)], LANES - 1, 1)
-    lane = lanes_of(rolled.shape[0])
-    for chunk in range(chunks):
-        at = cols(chunk)
-        s0 = surf[mine, at]
-        rolled_then = rolled
-        if chunk + 1 < chunks:
-            rolled_then = pltpu.roll(surf[mine, cols(chunk + 1)], LANES - 1, 1)
-        left = jnp.where(lane >= LANES - 1, rolled_then, rolled)
-        rolled = rolled_then
-        new_east = face(east[mine, at], s0, left, bed_e[mine, at], drag_e[mine, at])
-        if scale is not None:
-            new_east = scale * new_east
-        east_out[mine, at] = east_walled(new_east, chunk, chunks)
+    rolled = lane = None
+    if east_out is not None:
+        rolled = pltpu.roll(surf[mine, cols(0)], LANES - 1, 1)
+        lane = lanes_of(rolled.shape[0])
+    for chunk in range(chunks):
+        at = cols(chunk)
+        if east_out is not None:
+            s0 = surf[mine, at]
+            rolled_then = rolled
+            if chunk + 1 < chunks:
+                rolled_then = pltpu.roll(surf[mine, cols(chunk + 1)], LANES - 1, 1)
+            left = jnp.where(lane >= LANES - 1, rolled_then, rolled)
+            rolled = rolled_then
+            new_east = face(east[mine, at], s0, left, bed_e[mine, at], drag_e[mine, at])
+            if scale is not None:
+                new_east = scale * new_east
+            east_out[mine, at] = east_walled(new_east, chunk, chunks)
         if upper:
             s0 = surf[: upper + 8, at]
             s1 = moved_up(s0)[:upper]
@@ -474,18 +475,24 @@
         yield chunk, keep[mine, at] * s0 + (spread * (inflow - outflow) + sums[chunk])
 
 
+def refill(corridor, mine, surf, total, count, total_out, windows=None):
+    chunks = surf.shape[1] // LANES
+    if windows is None:
+        windows = window_sums([surf[mine, cols(chunk)] for chunk in range(chunks)], corridor, True)
+    for chunk in range(chunks):
+        at = cols(chunk)
+        kept = (1.0 - corridor * DRAIN) * total[mine, at]
+        total_out[mine, at] = kept + count[mine, at] * windows[chunk]
+
+
+def summed(corridor, mine, total):
+    chunks = total.shape[1] // LANES
+    return window_sums([total[mine, cols(chunk)] for chunk in range(chunks)], corridor, False)
+
+
 def exchange(corridor, mine, surf, total, count, total_out, windows=None):
-    chunks = surf.shape[1] // LANES
-    sums = window_sums([total[mine, cols(chunk)] for chunk in range(chunks)], corridor, False)
-    if total_out is not None:
-        if windows is None:
-            windows = window_sums(
-                [surf[mine, cols(chunk)] for chunk in range(chunks)], corridor, True
-            )
-        for chunk in range(chunks):
-            at = cols(chunk)
-            kept = (1.0 - corridor * DRAIN) * total[mine, at]
-            total_out[mine, at] = kept + count[mine, at] * windows[chunk]
+    sums = summed(corridor, mine, total)
+    refill(corridor, mine, surf, total, count, total_out, windows)
     return sums
 
 
@@ -515,7 +522,7 @@
         surf_1[own, cols(chunk)] = new_surf
 
 
-def second_kernel(corridor, tiles, far, surf, east, south, *refs):
+def second_kernel(corridor, tiles, far, beyond, surf, east, south, *refs):
     faces = refs[:4]
     number, total, given_1 = refs[4:7]
     surf_1, total_1, count, keep = refs[11:15]
@@ -526,9 +533,11 @@
     position = lax.axis_index("gy")
     tail = slice(rows, ext)
 
-    valid, node_row, node_chunk, node_lane = located(far[1:2, :], position, rows, ext, columns)
+    section = jnp.concatenate([far[0:1, :], beyond[0:1, :]], axis=1)
+    cell = jnp.concatenate([far[1:2, :], beyond[1:2, :]], axis=1)
+    valid, node_row, node_chunk, node_lane = located(cell, position, rows, ext, columns)
     key = jnp.where(valid & (node_row >= rows), node_chunk * 8 + (node_row - rows), -1)
-    starts, levels = scattered(far[0:1, :], key, node_lane, chunks * 8)
+    starts, levels = scattered(section, key, node_lane, chunks * 8)
     starting = [
         number[tail, cols(chunk)] + starts[chunk * 8 : chunk * 8 + 8] for chunk in range(chunks)
     ]
@@ -557,14 +566,14 @@
 
 def third_kernel(corridor, tiles, surf, east, south, *refs):
     faces = refs[:4]
-    total, keep, count, given_2, own, takes, masks, takes_near, masks_near = refs[4:13]
-    surf_3, east_3, south_3, total_3, own_term, partner_term, other_term = refs[13:]
+    total, keep, given_2, own, takes, masks, takes_near, masks_near = refs[4:12]
+    surf_3, east_3, south_3, own_term, partner_term, other_term = refs[12:]
     ext, columns = surf.shape
     rows = ext - 2 * HALO
     mine = slice(0, rows)
     owned = own.shape[1]
     chunks = columns // LANES
-    sums = exchange(corridor, mine, surf, total, count, total_3)
+    sums = summed(corridor, mine, total)
     fluxes(
         mine, rows - 8, wall_of(ext, tiles), (surf, east, south), faces, east_3, south_3
     )
@@ -601,16 +610,13 @@
 
 def last_kernel(corridor, tiles, surf_2, east_2, south_3, *refs):
     faces = refs[:4]
-    total_2, total_3, keep, bed, _, east_3 = refs[4:10]
-    surf_3, depth_out, east_out, south_out, depth_4, east_4, south_4, east_tail, sems = refs[10:]
+    total_2, count, keep, bed, _, east_3 = refs[4:10]
+    surf_3, depth_out, east_out, south_out = refs[10:14]
+    depth_4, east_4, south_4, east_tail, total_3, sems = refs[14:]
     ext, columns = surf_2.shape
     rows = ext - 2 * HALO
     chunks = columns // LANES
     own, tail = slice(0, rows), slice(rows, ext)
-    sums = exchange(corridor, tail, surf_2, total_2, None, None)
-    fluxes(tail, 0, None, (surf_2, east_2, None), faces, east_tail, None)
-    for chunk, new_surf in settled(tail, surf_2, east_tail, south_3, keep, sums):
-        surf_3[tail, cols(chunk)] = new_surf
 
     def copy(slot, source, target, first, last):
         part = pl.ds(first * LANES, (last - first) * LANES)
@@ -619,11 +625,18 @@
         )
 
     before = (surf_3, east_3, south_3)
-    fluxes(own, rows - 8, wall_of(ext, tiles), before, faces, east_4, south_4, scale=SLOPE)
-    copies = [copy(0, east_4, east_out, 0, chunks), copy(1, south_4, south_out, 0, chunks)]
-    for one in copies:
-        one.start()
-    sums = exchange(corridor, own, surf_3, total_3, None, None)
+    tail_sums = summed(corridor, tail, total_2)
+    refill(corridor, own, surf_2, total_2, count, total_3)
+    fluxes(own, rows - 8, None, before, faces, east_4, south_4, scale=SLOPE)
+    copies = [copy(0, east_4, east_out, 0, chunks)]
+    copies[0].start()
+    fluxes(tail, 0, None, (surf_2, east_2, None), faces, east_tail, None)
+    for chunk, new_surf in settled(tail, surf_2, east_tail, south_3, keep, tail_sums):
+        surf_3[tail, cols(chunk)] = new_surf
+    sums = summed(corridor, own, total_3)
+    fluxes(slice(0, 0), 0, wall_of(ext, tiles), before, faces, None, south_4, scale=SLOPE)
+    copies.append(copy(1, south_4, south_out, 0, chunks))
+    copies[1].start()
     group = 5
     for chunk, new_surf in settled(own, surf_3, east_4, south_4, keep, sums, spread=SPREAD):
         at = cols(chunk)
@@ -740,7 +753,7 @@
         [field] * 2 + picks(2 * owned) + [small] * 2,
         (fields[0], own, partner_section, partner_cells),
     )
-    (near,) = call(relay_kernel, "relay", [pair], (by_other, masks))
+    near, beyond = call(relay_kernel, "relay", [pair, pair], (by_other, masks))
     from_far = swapped(near, 0)
     *fields, takes_near, masks_near = call(
         functools.partial(border_kernel, corridor, tiles),
@@ -762,18 +775,18 @@
         "second",
         [field] * 8 + [small],
         (
-            *(from_far, surf, east, south, *faces, number, total, given_1),
+            *(from_far, beyond, surf, east, south, *faces, number, total, given_1),
             *(surf_1, total_1, count, keep),
         ),
         scratch=[field],
-        aliases={11 + slot: slot for slot in range(4)},
-    )
-    surf_3, east_3, south_3, total_3, own_term, partner_term, other_term = call(
+        aliases={12 + slot: slot for slot in range(4)},
+    )
+    surf_3, east_3, south_3, own_term, partner_term, other_term = call(
         functools.partial(third_kernel, corridor, tiles),
         "third",
-        [field] * 4 + [term] * 3,
+        [field] * 3 + [term] * 3,
         (
-            *(surf_2, east_2, south_2, *faces, total_2, keep, count, given_2),
+            *(surf_2, east_2, south_2, *faces, total_2, keep, given_2),
             *(own, takes, masks, takes_near, masks_near),
         ),
     )
@@ -783,8 +796,8 @@
         functools.partial(last_kernel, corridor, tiles),
         "last",
         [field, result, result, result],
-        (surf_2, east_2, south_3, *faces, total_2, total_3, keep, bed, surf_3, east_3),
-        scratch=[small, small, field, field, pltpu.SemaphoreType.DMA((2 + -(-chunks // 5),))],
+        (surf_2, east_2, south_3, *faces, total_2, count, keep, bed, surf_3, east_3),
+        scratch=[small, small, field, field, small, pltpu.SemaphoreType.DMA((2 + -(-chunks // 5),))],
         aliases={11: 0},
     )
     river_section = own_term.reshape(owned) + from_other + from_partner

time: 20.7 us -> 20.8 us (level)
  no operation moved by 1% of the time
where the time goes in v4:
time: 20.8 us; the launch traced here: 20.6 us
  starting transfers between devices  10.4 us (50%)
  Pallas kernels  8.54 us (41%)
  between operations  0.77 us (4%)
  other arithmetic  0.52 us (2%)
  waiting for transfers between devices  0.34 us (2%)
    ppermute x7, starting transfers between devices, swapped(): return lax.ppermute(value, 'gy', pairs)  10.4 us
    pallas_call x9, Pallas kernels, call(): pl.pallas_call(kernel, out_shape=outs, in_specs=[VMEM_SPEC] * len(values)...  5.86 us
    pallas_call x1, Pallas kernels, local(): pl.pallas_call(load_kernel, out_shape=[field] * 4 + [pltpu.VMEM((rows, co...  1.44 us
    pallas_call x1, Pallas kernels, local(): pl.pallas_call(pack_kernel, out_shape=[wide, pair], in_specs=[HBM_SPEC] *...  1.24 us
    add x1, other arithmetic, local(): river_section = own_term.reshape(owned) + from_other + from_partner  0.52 us
  transfers between devices with their start and end apart: 7, of which 1 were waited for; matrix products, arithmetic and copies ran while one was open for 0% of the time, Pallas kernels for 31%

profile of v4, /device:TPU:0, one launch (start us, length us, event | category | flops | bytes accessed | tf_op | source)
XLA Modules:
  0.0 20.6 jit_solution(7233408620200944645)
XLA Ops:
  0.6 0.5 %collective-permute-start.1 = (s32[4,128]{1,0:T(4,128)}, s32[4,128]{1,0:T(4,128)S(1)}, u32[]{:S(2)}, u32[]{:S(2)}) collective-permute-start(s32[4,128]{1,0:T(4,128)} %cells.1), channel_id=1, source_target_pairs={{0,1},{1,0},{2,3},{3,2},{4,5},{5,4},{6,7},{7,6},{8,9},{9,8},{10,11... | collective-permute-start | bytes 6152 | tf_op jit(solution)/shard_map/ppermute | solution.py:37
  1.1 0.1 collective-permute-start
  1.2 1.2 %pack.1 = (f32[61,4,128]{2,1,0:T(4,128)S(1)}, f32[2,128]{1,0:T(2,128)S(1)}) custom-call(f32[32,1920]{1,0:T(8,128)} %depth_in.1, f32[32,1920]{1,0:T(8,128)} %bed_in.1, s32[32,1920]{1,0:T(8,128)} %rough_in.1, f32[32,1920]{1,0:T(8,128)} %east_in.1, f32[32,1920]{1,0:T(8,128)} %south_in.1, f32[1,128]{1,0:T(1,128)} %bitcast.15, s32[4,128]{1,0:T(4,128)} %cells.1, ...), custom_call_target="tpu_custom_call" | custom-call | tf_op jit(solution)/shard_map/pack/pallas_call | solution.py:701
  2.5 0.0 collective-permute-done
  2.5 0.0 collective-permute-done.1.cells.partner_cells
  2.5 0.7 %collective-permute-start.2 = (f32[61,4,128]{2,1,0:T(4,128)S(1)}, f32[61,4,128]{2,1,0:T(4,128)S(1)}, u32[]{:S(2)}, u32[]{:S(2)}) collective-permute-start(f32[61,4,128]{2,1,0:T(4,128)S(1)} %join.1), channel_id=1, source_target_pairs={{1,2},{2,1},{3,4},{4,3},{5,6},{6,5},{7,8},{8,7},{9,10},{10,9},{11,... | collective-permute-start | bytes 374792 | tf_op jit(solution)/shard_map/ppermute | solution.py:37
  3.2 1.4 %load.1 = (f32[40,1920]{1,0:T(8,128)S(1)}, f32[40,1920]{1,0:T(8,128)S(1)}, f32[40,1920]{1,0:T(8,128)S(1)}, f32[40,1920]{1,0:T(8,128)S(1)}, s32[32,1920]{1,0:T(8,128)S(1)}, /*index=5*/f32[8,128]{1,0:T(8,128)S(1)}) custom-call(f32[32,1920]{1,0:T(8,128)} %depth_in.1, f32[32,1920]{1,0:T(8,128)} %east_in.1, f32[32,1920]{1,0:T(8,128)} %south_in.1, ...), custom_call_target="tpu_custom_call" | custom-call | tf_op jit(solution)/shard_map/load/pallas_call | solution.py:729
  4.6 0.7 %prepare.1 = (f32[40,1920]{1,0:T(8,128)S(1)}, f32[40,1920]{1,0:T(8,128)S(1)}, f32[40,1920]{1,0:T(8,128)S(1)}, f32[40,1920]{1,0:T(8,128)S(1)}, f32[40,1920]{1,0:T...) custom-call(f32[8,128]{1,0:T(8,128)S(1)} %get-tuple-element.63.table, ...), custom_call_target="tpu_custom_call", output_to_operand_aliasing={{0}: (2, {}), {1}: (3, {}), {2}: (4, {}), {3}: (5, {})} | custom-call | tf_op jit(solution)/shard_map/prepare/pallas_call | solution.py:681
  5.3 4.4 %collective-permute-start.4 = (f32[60,4,128]{2,1,0:T(4,128)S(1)}, f32[60,4,128]{2,1,0:T(4,128)S(1)}, u32[]{:S(2)}, u32[]{:S(2)}) collective-permute-start(f32[60,4,128]{2,1,0:T(4,128)S(1)} %get-tuple-element.74), channel_id=1, source_target_pairs={{0,1},{1,0},{2,3},{3,2},{4,5},{5,4},{6,7},{7,6},{8,9},{9,8},{10,11... | collective-permute-start | bytes 368648 | tf_op jit(solution)/shard_map/ppermute | solution.py:37
  9.7 0.5 %nodes.1 = (f32[40,1920]{1,0:T(8,128)S(1)}, f32[40,1920]{1,0:T(8,128)S(1)}, bf16[2,256,512]{2,1,0:T(8,128)(2,1)S(1)}, f32[2,256,128]{2,1,0:T(8,128)S(1)}, f32[32...) custom-call(f32[40,1920]{1,0:T(8,128)S(1)} %get-tuple-element.69.surf.refs_0_, f32[2,128]{1,0:T(2,128)S(1)} %get-tuple-element.70.own.refs_7_, ...), custom_call_target="tpu_custom_call" | custom-call | tf_op jit(solution)/shard_map/nodes/pallas_call | solution.py:681
  10.2 0.0 collective-permute-done.2.by_other
  10.2 0.1 collective-permute-start.3
  10.3 0.3 %collective-permute-done.4.by_partner = f32[60,4,128]{2,1,0:T(4,128)S(1)} collective-permute-done((f32[60,4,128]{2,1,0:T(4,128)S(1)}, f32[60,4,128]{2,1,0:T(4,128)S(1)}, u32[]{:S(2)}, u32[]{:S(2)}) %collective-permute-start.4) | collective-permute-done | bytes 122912 | tf_op jit(solution)/shard_map/ppermute | solution.py:37
  10.7 0.5 %border.1 = (f32[40,1920]{1,0:T(8,128)S(1)}, f32[40,1920]{1,0:T(8,128)S(1)}, f32[40,1920]{1,0:T(8,128)S(1)}, f32[40,1920]{1,0:T(8,128)S(1)}, f32[40,1920]{1,0:T(...) custom-call(f32[60,4,128]{2,1,0:T(4,128)S(1)} %collective-permute-do, ...), custom_call_target="tpu_custom_call", output_to_operand_aliasing={{0}: (4, {}), {1}: (5, {}), {2}: (6, {}), {3}: (7, {}), {4}... | custom-call | tf_op jit(solution)/shard_map/border/pallas_call | solution.py:681
  11.2 0.3 %first.1 = (f32[40,1920]{1,0:T(8,128)S(1)}, f32[40,1920]{1,0:T(8,128)S(1)}, f32[40,1920]{1,0:T(8,128)S(1)}, f32[40,1920]{1,0:T(8,128)S(1)}) custom-call(f32[40,1920]{1,0:T(8,128)S(1)} %get-tuple-element.85.surf, f32[40,1920]{1,0:T(8,128)S(1)} %get-tuple-element.86.east, f32[40,1920]{1,0:T(8,128)S(1)} %get-tuple-element.87.south, ...), custom_call_target="tpu_custom_call" | custom-call | tf_op jit(solution)/shard_map/first/pallas_call | solution.py:681
  11.5 0.0 collective-permute-done.3.far
  11.5 1.1 %second.1 = (f32[40,1920]{1,0:T(8,128)S(1)}, f32[40,1920]{1,0:T(8,128)S(1)}, f32[40,1920]{1,0:T(8,128)S(1)}, f32[40,1920]{1,0:T(8,128)S(1)}, f32[40,1920]{1,0:T(...) custom-call(f32[2,128]{1,0:T(2,128)S(1)} %collective-permute-done.3., ...), custom_call_target="tpu_custom_call", output_to_operand_aliasing={{0}: (12, {}), {1}: (13, {}), {2}: (14, {}), {3}: (15, {})} | custom-call | tf_op jit(solution)/shard_map/second/pallas_call | solution.py:681
  12.7 1.1 %third.1 = (f32[40,1920]{1,0:T(8,128)S(1)}, f32[40,1920]{1,0:T(8,128)S(1)}, f32[40,1920]{1,0:T(8,128)S(1)}, f32[1,128]{1,0:T(1,128)S(1)}, f32[1,128]{1,0:T(1,128)S(1)}, /*index=5*/f32[1,128]{1,0:T(1,128)S(1)}) custom-call(f32[40,1920]{1,0:T(8,128)S(1)} %get-tuple-element.100.surf.surf_2, f32[40,1920]{1,0:T(8,128)S(1)} %get-tuple-element.101.east.east_2, ...), custom_call_target="tpu_custom_call" | custom-call | tf_op jit(solution)/shard_map/third/pallas_call | solution.py:681
  13.8 0.7 %collective-permute-start.5 = (f32[128]{0:T(128)S(1)}, f32[128]{0:T(128)S(1)}, u32[]{:S(2)}, u32[]{:S(2)}) collective-permute-start(f32[128]{0:T(128)S(1)} %bitcast.12), channel_id=1, source_target_pairs={{1,2},{2,1},{3,4},{4,3},{5,6},{6,5},{7,8},{8,7},{9,10},{10,9},{11,... | collective-permute-start | bytes 1544 | tf_op jit(solution)/shard_map/ppermute | solution.py:37
  14.5 4.0 %collective-permute-start.6 = (f32[128]{0:T(128)S(1)}, f32[128]{0:T(128)S(1)}, u32[]{:S(2)}, u32[]{:S(2)}) collective-permute-start(f32[128]{0:T(128)S(1)} %bitcast.11), channel_id=1, source_target_pairs={{0,1},{1,0},{2,3},{3,2},{4,5},{5,4},{6,7},{7,6},{8,9},{9,8},{10,11... | collective-permute-start | bytes 1544 | tf_op jit(solution)/shard_map/ppermute | solution.py:37
  18.5 1.5 %last.1 = (f32[40,1920]{1,0:T(8,128)S(1)}, f32[32,1920]{1,0:T(8,128)}, f32[32,1920]{1,0:T(8,128)}, f32[32,1920]{1,0:T(8,128)}) custom-call(f32[40,1920]{1,0:T(8,128)S(1)} %get-tuple-element.100.surf.surf_2, f32[40,1920]{1,0:T(8,128)S(1)} %get-tuple-element.101.east.east_2, ...), custom_call_target="tpu_custom_call", output_to_operand_aliasing={{0}: (11, {})} | custom-call | tf_op jit(solution)/shard_map/last/pallas_call | solution.py:681
  20.1 0.0 collective-permute-done.5
  20.1 0.0 collective-permute-done.6
  20.1 0.5 %fusion = f32[128]{0:T(128)} fusion(f32[128]{0:T(128)S(1)} %collective-permute-done.6, f32[128]{0:T(128)S(1)} %collective-permute-done.5, f32[1,128]{1,0:T(1,128)S(1)} %get-tuple-element.117), kind=kLoop, calls=%fused_computation.1 | loop fusion | flops 256 | bytes 2048 | tf_op jit(solution)/shard_map/add | solution.py:803
  (2 shorter events, 0.0 us)
Async XLA Ops:
  0.6 1.9 %collective-permute-start.1 = (s32[4,128]{1,0:T(4,128)}, s32[4,128]{1,0:T(4,128)S(1)}, u32[]{:S(2)}, u32[]{:S(2)}) collective-permute-start(s32[4,128]{1,0:T(4,128)} %cells.1), channel_id=1, source_target_pairs={{0,1},{1,0},{2,3},{3,2},{4,5},{5,4},{6,7},{7,6},{8,9},{9,8},{10,11... | collective-permute-start | bytes 6152 | tf_op jit(solution)/shard_map/ppermute | solution.py:37
  1.1 1.3 %collective-permute-start = (f32[128]{0:T(128)}, f32[128]{0:T(128)S(1)}, u32[]{:S(2)}, u32[]{:S(2)}) collective-permute-start(f32[128]{0:T(128)} %param.11), channel_id=1, source_target_pairs={{0,1},{1,0},{2,3},{3,2},{4,5},{5,4},{6,7},{7,6},{8,9},{9,8},{10,11... | collective-permute-start | bytes 1544 | tf_op jit(solution)/shard_map/ppermute | solution.py:37
  2.5 7.7 %collective-permute-start.2 = (f32[61,4,128]{2,1,0:T(4,128)S(1)}, f32[61,4,128]{2,1,0:T(4,128)S(1)}, u32[]{:S(2)}, u32[]{:S(2)}) collective-permute-start(f32[61,4,128]{2,1,0:T(4,128)S(1)} %join.1), channel_id=1, source_target_pairs={{1,2},{2,1},{3,4},{4,3},{5,6},{6,5},{7,8},{8,7},{9,10},{10,9},{11,... | collective-permute-start | bytes 374792 | tf_op jit(solution)/shard_map/ppermute | solution.py:37
  5.3 5.3 %collective-permute-start.4 = (f32[60,4,128]{2,1,0:T(4,128)S(1)}, f32[60,4,128]{2,1,0:T(4,128)S(1)}, u32[]{:S(2)}, u32[]{:S(2)}) collective-permute-start(f32[60,4,128]{2,1,0:T(4,128)S(1)} %get-tuple-element.74), channel_id=1, source_target_pairs={{0,1},{1,0},{2,3},{3,2},{4,5},{5,4},{6,7},{7,6},{8,9},{9,8},{10,11... | collective-permute-start | bytes 368648 | tf_op jit(solution)/shard_map/ppermute | solution.py:37
  10.2 1.3 %collective-permute-start.3 = (f32[2,128]{1,0:T(2,128)S(1)}, f32[2,128]{1,0:T(2,128)S(1)}, u32[]{:S(2)}, u32[]{:S(2)}) collective-permute-start(f32[2,128]{1,0:T(2,128)S(1)} %get-tuple-element.72.near), channel_id=1, source_target_pairs={{0,1},{1,0},{2,3},{3,2},{4,5},{5,4},{6,7},{7,6},{8,9},{9,8},{10,11... | collective-permute-start | bytes 3080 | tf_op jit(solution)/shard_map/ppermute | solution.py:37
  13.8 6.3 %collective-permute-start.5 = (f32[128]{0:T(128)S(1)}, f32[128]{0:T(128)S(1)}, u32[]{:S(2)}, u32[]{:S(2)}) collective-permute-start(f32[128]{0:T(128)S(1)} %bitcast.12), channel_id=1, source_target_pairs={{1,2},{2,1},{3,4},{4,3},{5,6},{6,5},{7,8},{8,7},{9,10},{10,9},{11,... | collective-permute-start | bytes 1544 | tf_op jit(solution)/shard_map/ppermute | solution.py:37
  14.5 5.6 %collective-permute-start.6 = (f32[128]{0:T(128)S(1)}, f32[128]{0:T(128)S(1)}, u32[]{:S(2)}, u32[]{:S(2)}) collective-permute-start(f32[128]{0:T(128)S(1)} %bitcast.11), channel_id=1, source_target_pairs={{0,1},{1,0},{2,3},{3,2},{4,5},{5,4},{6,7},{7,6},{8,9},{9,8},{10,11... | collective-permute-start | bytes 1544 | tf_op jit(solution)/shard_map/ppermute | solution.py:37

commit v5 on v4

--- a/solution.py
+++ b/solution.py
@@ -608,7 +608,22 @@
     other_term[...] = terms[:, 2 * owned :]
 
 
-def last_kernel(corridor, tiles, surf_2, east_2, south_3, *refs):
+def last_kernel(corridor, tiles, early, *refs):
+    inputs, outputs, scratch = refs[:13], refs[15:19], refs[21:]
+    if early:
+        refs[19][...] = refs[13][...]
+        refs[20][...] = refs[14][...]
+    else:
+        outputs, scratch = refs[16:20], refs[20:]
+    position = lax.axis_index("gy")
+    at_edge = (position == 0) | (position == tiles - 1)
+
+    @pl.when(at_edge if early else jnp.logical_not(at_edge))
+    def _():
+        last_substep(corridor, tiles, *inputs, *outputs, *scratch)
+
+
+def last_substep(corridor, tiles, surf_2, east_2, south_3, *refs):
     faces = refs[:4]
     total_2, count, keep, bed, _, east_3 = refs[4:10]
     surf_3, depth_out, east_out, south_out = refs[10:14]
@@ -790,16 +805,35 @@
             *(own, takes, masks, takes_near, masks_near),
         ),
     )
+    last_in = [
+        held(value)
+        for value in (surf_2, east_2, south_3, *faces, total_2, count, keep, bed, surf_3, east_3)
+    ]
+    last_scratch = [small, small, field, field, small]
+    last_scratch.append(pltpu.SemaphoreType.DMA((2 + -(-chunks // 5),)))
+    surf_3, *results, partner_term, other_term = pl.pallas_call(
+        functools.partial(last_kernel, corridor, tiles, True),
+        out_shape=[field] + [result] * 3 + [term] * 2,
+        in_specs=[VMEM_SPEC] * 15,
+        out_specs=[VMEM_SPEC] + [HBM_SPEC] * 3 + [VMEM_SPEC] * 2,
+        scratch_shapes=last_scratch,
+        input_output_aliases={11: 0},
+        compiler_params=params,
+        name="last_early",
+    )(*last_in, held(partner_term), held(other_term))
     from_other = swapped(other_term.reshape(owned), 1)
     from_partner = swapped(partner_term.reshape(owned), 0)
-    _, depth, flux_east, flux_south = call(
-        functools.partial(last_kernel, corridor, tiles),
-        "last",
-        [field, result, result, result],
-        (surf_2, east_2, south_3, *faces, total_2, count, keep, bed, surf_3, east_3),
-        scratch=[small, small, field, field, small, pltpu.SemaphoreType.DMA((2 + -(-chunks // 5),))],
-        aliases={11: 0},
-    )
+    last_in[11] = held(surf_3)
+    _, depth, flux_east, flux_south = pl.pallas_call(
+        functools.partial(last_kernel, corridor, tiles, False),
+        out_shape=[field] + [result] * 3,
+        in_specs=[VMEM_SPEC] * 13 + [HBM_SPEC] * 3,
+        out_specs=[VMEM_SPEC] + [HBM_SPEC] * 3,
+        scratch_shapes=last_scratch,
+        input_output_aliases={11: 0, 13: 1, 14: 2, 15: 3},
+        compiler_params=params,
+        name="last",
+    )(*last_in, *[far(value) for value in results])
     river_section = own_term.reshape(owned) + from_other + from_partner
     return (depth, flux_east, flux_south, river_section)
 

time: 20.8 us -> 20.5 us (0.986)
  the two profiles are of different devices: /device:TPU:0 before, /device:TPU:7 now
where the time goes in v5:
time: 20.5 us; the launch traced here: 20.2 us
  Pallas kernels  8.65 us (42%)
  starting transfers between devices  8.3 us (40%)
  waiting for transfers between devices  2 us (10%)
  between operations  0.76 us (4%)
  other arithmetic  0.52 us (3%)
    ppermute x7, starting transfers between devices, swapped(): return lax.ppermute(value, 'gy', pairs)  8.3 us
    pallas_call x8, Pallas kernels, call(): pl.pallas_call(kernel, out_shape=outs, in_specs=[VMEM_SPEC] * len(values)...  4.34 us
    ppermute x7, waiting for transfers between devices, swapped(): return lax.ppermute(value, 'gy', pairs)  2 us
    pallas_call x1, Pallas kernels, local(): pl.pallas_call(functools.partial(last_kernel, corridor, tiles, False), ou...  1.55 us
    pallas_call x1, Pallas kernels, local(): pl.pallas_call(load_kernel, out_shape=[field] * 4 + [pltpu.VMEM((rows, co...  1.44 us
    pallas_call x1, Pallas kernels, local(): pl.pallas_call(pack_kernel, out_shape=[wide, pair], in_specs=[HBM_SPEC] *...  1.24 us
    add x1, other arithmetic, local(): river_section = own_term.reshape(owned) + from_other + from_partner  0.52 us
  transfers between devices with their start and end apart: 7, of which 2 were waited for; matrix products, arithmetic and copies ran while one was open for 0% of the time, Pallas kernels for 31%

profile of v5, /device:TPU:7, one launch (start us, length us, event | category | flops | bytes accessed | tf_op | source)
XLA Modules:
  0.0 20.2 jit_solution(13023605036863888925)
XLA Ops:
  0.6 0.7 %collective-permute-start.1 = (s32[4,128]{1,0:T(4,128)}, s32[4,128]{1,0:T(4,128)S(1)}, u32[]{:S(2)}, u32[]{:S(2)}) collective-permute-start(s32[4,128]{1,0:T(4,128)} %cells.1), channel_id=1, source_target_pairs={{0,1},{1,0},{2,3},{3,2},{4,5},{5,4},{6,7},{7,6},{8,9},{9,8},{10,11... | collective-permute-start | bytes 6152 | tf_op jit(solution)/shard_map/ppermute | solution.py:37
  1.4 0.1 collective-permute-start
  1.4 1.2 %pack.1 = (f32[61,4,128]{2,1,0:T(4,128)S(1)}, f32[2,128]{1,0:T(2,128)S(1)}) custom-call(f32[32,1920]{1,0:T(8,128)} %depth_in.1, f32[32,1920]{1,0:T(8,128)} %bed_in.1, s32[32,1920]{1,0:T(8,128)} %rough_in.1, f32[32,1920]{1,0:T(8,128)} %east_in.1, f32[32,1920]{1,0:T(8,128)} %south_in.1, f32[1,128]{1,0:T(1,128)} %bitcast.15, s32[4,128]{1,0:T(4,128)} %cells.1, ...), custom_call_target="tpu_custom_call" | custom-call | tf_op jit(solution)/shard_map/pack/pallas_call | solution.py:716
  2.7 0.0 collective-permute-done
  2.7 0.0 collective-permute-done.1.cells.partner_cells
  2.7 3.5 %collective-permute-start.2 = (f32[61,4,128]{2,1,0:T(4,128)S(1)}, f32[61,4,128]{2,1,0:T(4,128)S(1)}, u32[]{:S(2)}, u32[]{:S(2)}) collective-permute-start(f32[61,4,128]{2,1,0:T(4,128)S(1)} %join.1), channel_id=1, source_target_pairs={{1,2},{2,1},{3,4},{4,3},{5,6},{6,5},{7,8},{8,7},{9,10},{10,9},{11,... | collective-permute-start | bytes 374792 | tf_op jit(solution)/shard_map/ppermute | solution.py:37
  6.2 1.4 %load.1 = (f32[40,1920]{1,0:T(8,128)S(1)}, f32[40,1920]{1,0:T(8,128)S(1)}, f32[40,1920]{1,0:T(8,128)S(1)}, f32[40,1920]{1,0:T(8,128)S(1)}, s32[32,1920]{1,0:T(8,128)S(1)}, /*index=5*/f32[8,128]{1,0:T(8,128)S(1)}) custom-call(f32[32,1920]{1,0:T(8,128)} %depth_in.1, f32[32,1920]{1,0:T(8,128)} %east_in.1, f32[32,1920]{1,0:T(8,128)} %south_in.1, ...), custom_call_target="tpu_custom_call" | custom-call | tf_op jit(solution)/shard_map/load/pallas_call | solution.py:744
  7.7 0.7 %prepare.1 = (f32[40,1920]{1,0:T(8,128)S(1)}, f32[40,1920]{1,0:T(8,128)S(1)}, f32[40,1920]{1,0:T(8,128)S(1)}, f32[40,1920]{1,0:T(8,128)S(1)}, f32[40,1920]{1,0:T...) custom-call(f32[8,128]{1,0:T(8,128)S(1)} %get-tuple-element.69.table, ...), custom_call_target="tpu_custom_call", output_to_operand_aliasing={{0}: (2, {}), {1}: (3, {}), {2}: (4, {}), {3}: (5, {})} | custom-call | tf_op jit(solution)/shard_map/prepare/pallas_call | solution.py:696
  8.3 0.1 collective-permute-start.4
  8.4 0.5 %nodes.1 = (f32[40,1920]{1,0:T(8,128)S(1)}, f32[40,1920]{1,0:T(8,128)S(1)}, bf16[2,256,512]{2,1,0:T(8,128)(2,1)S(1)}, f32[2,256,128]{2,1,0:T(8,128)S(1)}, f32[32...) custom-call(f32[40,1920]{1,0:T(8,128)S(1)} %get-tuple-element.75.surf.refs_0_, f32[2,128]{1,0:T(2,128)S(1)} %get-tuple-element.76.own.refs_7_, ...), custom_call_target="tpu_custom_call" | custom-call | tf_op jit(solution)/shard_map/nodes/pallas_call | solution.py:696
  9.0 1.0 %collective-permute-done.2.by_other = f32[61,4,128]{2,1,0:T(4,128)S(1)} collective-permute-done((f32[61,4,128]{2,1,0:T(4,128)S(1)}, f32[61,4,128]{2,1,0:T(4,128)S(1)}, u32[]{:S(2)}, u32[]{:S(2)}) %collective-permute-start.2) | collective-permute-done | bytes 124960 | tf_op jit(solution)/shard_map/ppermute | solution.py:37
  10.0 0.8 %collective-permute-start.3 = (f32[2,128]{1,0:T(2,128)S(1)}, f32[2,128]{1,0:T(2,128)S(1)}, u32[]{:S(2)}, u32[]{:S(2)}) collective-permute-start(f32[2,128]{1,0:T(2,128)S(1)} %get-tuple-element.78.near), channel_id=1, source_target_pairs={{0,1},{1,0},{2,3},{3,2},{4,5},{5,4},{6,7},{7,6},{8,9},{9,8},{10,11... | collective-permute-start | bytes 3080 | tf_op jit(solution)/shard_map/ppermute | solution.py:37
  10.7 0.0 collective-permute-done.4.by_partner
  10.7 0.5 %border.1 = (f32[40,1920]{1,0:T(8,128)S(1)}, f32[40,1920]{1,0:T(8,128)S(1)}, f32[40,1920]{1,0:T(8,128)S(1)}, f32[40,1920]{1,0:T(8,128)S(1)}, f32[40,1920]{1,0:T(...) custom-call(f32[60,4,128]{2,1,0:T(4,128)S(1)} %collective-permute-do, ...), custom_call_target="tpu_custom_call", output_to_operand_aliasing={{0}: (4, {}), {1}: (5, {}), {2}: (6, {}), {3}: (7, {}), {4}... | custom-call | tf_op jit(solution)/shard_map/border/pallas_call | solution.py:696
  11.3 0.3 %first.1 = (f32[40,1920]{1,0:T(8,128)S(1)}, f32[40,1920]{1,0:T(8,128)S(1)}, f32[40,1920]{1,0:T(8,128)S(1)}, f32[40,1920]{1,0:T(8,128)S(1)}) custom-call(f32[40,1920]{1,0:T(8,128)S(1)} %get-tuple-element.91.surf, f32[40,1920]{1,0:T(8,128)S(1)} %get-tuple-element.92.east, f32[40,1920]{1,0:T(8,128)S(1)} %get-tuple-element.93.south, ...), custom_call_target="tpu_custom_call" | custom-call | tf_op jit(solution)/shard_map/first/pallas_call | solution.py:696
  11.6 0.0 collective-permute-done.3.far
  11.6 1.1 %second.1 = (f32[40,1920]{1,0:T(8,128)S(1)}, f32[40,1920]{1,0:T(8,128)S(1)}, f32[40,1920]{1,0:T(8,128)S(1)}, f32[40,1920]{1,0:T(8,128)S(1)}, f32[40,1920]{1,0:T(...) custom-call(f32[2,128]{1,0:T(2,128)S(1)} %collective-permute-done.3., ...), custom_call_target="tpu_custom_call", output_to_operand_aliasing={{0}: (12, {}), {1}: (13, {}), {2}: (14, {}), {3}: (15, {})} | custom-call | tf_op jit(solution)/shard_map/second/pallas_call | solution.py:696
  12.7 1.1 %third.1 = (f32[40,1920]{1,0:T(8,128)S(1)}, f32[40,1920]{1,0:T(8,128)S(1)}, f32[40,1920]{1,0:T(8,128)S(1)}, f32[1,128]{1,0:T(1,128)S(1)}, f32[1,128]{1,0:T(1,128)S(1)}, /*index=5*/f32[1,128]{1,0:T(1,128)S(1)}) custom-call(f32[40,1920]{1,0:T(8,128)S(1)} %get-tuple-element.106.surf.refs_0_, f32[40,1920]{1,0:T(8,128)S(1)} %get-tuple-element.107.east.refs_1_, ...), custom_call_target="tpu_custom_call" | custom-call | tf_op jit(solution)/shard_map/third/pallas_call | solution.py:696
  13.9 0.1 last_early.1
  14.0 3.1 %collective-permute-start.5 = (f32[128]{0:T(128)S(1)}, f32[128]{0:T(128)S(1)}, u32[]{:S(2)}, u32[]{:S(2)}) collective-permute-start(f32[128]{0:T(128)S(1)} %bitcast.12), channel_id=1, source_target_pairs={{1,2},{2,1},{3,4},{4,3},{5,6},{6,5},{7,8},{8,7},{9,10},{10,9},{11,... | collective-permute-start | bytes 1544 | tf_op jit(solution)/shard_map/ppermute | solution.py:37
  17.1 0.1 collective-permute-start.6
  17.1 1.6 %last.1 = (f32[40,1920]{1,0:T(8,128)S(1)}, f32[32,1920]{1,0:T(8,128)}, f32[32,1920]{1,0:T(8,128)}, f32[32,1920]{1,0:T(8,128)}) custom-call(f32[40,1920]{1,0:T(8,128)S(1)} %get-tuple-element.106.surf.refs_0_, f32[40,1920]{1,0:T(8,128)S(1)} %get-tuple-element.107.east.refs_1_, ...), custom_call_target="tpu_custom_call", output_to_operand_aliasing={{0}: (11, {}), {1}: (13, {}), {2}: (14, {}), {3}: (15, {})} | custom-call | tf_op jit(solution)/shard_map/last/pallas_call | solution.py:827
  18.7 1.0 %collective-permute-done.5 = f32[128]{0:T(128)S(1)} collective-permute-done((f32[128]{0:T(128)S(1)}, f32[128]{0:T(128)S(1)}, u32[]{:S(2)}, u32[]{:S(2)}) %collective-permute-start.5) | collective-permute-done | bytes 544 | tf_op jit(solution)/shard_map/ppermute | solution.py:37
  19.7 0.0 collective-permute-done.6
  19.7 0.5 %fusion = f32[128]{0:T(128)} fusion(f32[128]{0:T(128)S(1)} %collective-permute-done.6, f32[128]{0:T(128)S(1)} %collective-permute-done.5, f32[1,128]{1,0:T(1,128)S(1)} %get-tuple-element.129), kind=kLoop, calls=%fused_computation.1 | loop fusion | flops 256 | bytes 2048 | tf_op jit(solution)/shard_map/add | solution.py:837
  (2 shorter events, 0.0 us)
Async XLA Ops:
  0.6 2.1 %collective-permute-start.1 = (s32[4,128]{1,0:T(4,128)}, s32[4,128]{1,0:T(4,128)S(1)}, u32[]{:S(2)}, u32[]{:S(2)}) collective-permute-start(s32[4,128]{1,0:T(4,128)} %cells.1), channel_id=1, source_target_pairs={{0,1},{1,0},{2,3},{3,2},{4,5},{5,4},{6,7},{7,6},{8,9},{9,8},{10,11... | collective-permute-start | bytes 6152 | tf_op jit(solution)/shard_map/ppermute | solution.py:37
  1.4 1.3 %collective-permute-start = (f32[128]{0:T(128)}, f32[128]{0:T(128)S(1)}, u32[]{:S(2)}, u32[]{:S(2)}) collective-permute-start(f32[128]{0:T(128)} %param.11), channel_id=1, source_target_pairs={{0,1},{1,0},{2,3},{3,2},{4,5},{5,4},{6,7},{7,6},{8,9},{9,8},{10,11... | collective-permute-start | bytes 1544 | tf_op jit(solution)/shard_map/ppermute | solution.py:37
  2.7 7.2 %collective-permute-start.2 = (f32[61,4,128]{2,1,0:T(4,128)S(1)}, f32[61,4,128]{2,1,0:T(4,128)S(1)}, u32[]{:S(2)}, u32[]{:S(2)}) collective-permute-start(f32[61,4,128]{2,1,0:T(4,128)S(1)} %join.1), channel_id=1, source_target_pairs={{1,2},{2,1},{3,4},{4,3},{5,6},{6,5},{7,8},{8,7},{9,10},{10,9},{11,... | collective-permute-start | bytes 374792 | tf_op jit(solution)/shard_map/ppermute | solution.py:37
  8.3 2.4 %collective-permute-start.4 = (f32[60,4,128]{2,1,0:T(4,128)S(1)}, f32[60,4,128]{2,1,0:T(4,128)S(1)}, u32[]{:S(2)}, u32[]{:S(2)}) collective-permute-start(f32[60,4,128]{2,1,0:T(4,128)S(1)} %get-tuple-element.80), channel_id=1, source_target_pairs={{0,1},{1,0},{2,3},{3,2},{4,5},{5,4},{6,7},{7,6},{8,9},{9,8},{10,11... | collective-permute-start | bytes 368648 | tf_op jit(solution)/shard_map/ppermute | solution.py:37
  10.0 1.6 %collective-permute-start.3 = (f32[2,128]{1,0:T(2,128)S(1)}, f32[2,128]{1,0:T(2,128)S(1)}, u32[]{:S(2)}, u32[]{:S(2)}) collective-permute-start(f32[2,128]{1,0:T(2,128)S(1)} %get-tuple-element.78.near), channel_id=1, source_target_pairs={{0,1},{1,0},{2,3},{3,2},{4,5},{5,4},{6,7},{7,6},{8,9},{9,8},{10,11... | collective-permute-start | bytes 3080 | tf_op jit(solution)/shard_map/ppermute | solution.py:37
  14.0 5.8 %collective-permute-start.5 = (f32[128]{0:T(128)S(1)}, f32[128]{0:T(128)S(1)}, u32[]{:S(2)}, u32[]{:S(2)}) collective-permute-start(f32[128]{0:T(128)S(1)} %bitcast.12), channel_id=1, source_target_pairs={{1,2},{2,1},{3,4},{4,3},{5,6},{6,5},{7,8},{8,7},{9,10},{10,9},{11,... | collective-permute-start | bytes 1544 | tf_op jit(solution)/shard_map/ppermute | solution.py:37
  17.1 2.6 %collective-permute-start.6 = (f32[128]{0:T(128)S(1)}, f32[128]{0:T(128)S(1)}, u32[]{:S(2)}, u32[]{:S(2)}) collective-permute-start(f32[128]{0:T(128)S(1)} %bitcast.11), channel_id=1, source_target_pairs={{0,1},{1,0},{2,3},{3,2},{4,5},{5,4},{6,7},{7,6},{8,9},{9,8},{10,11... | collective-permute-start | bytes 1544 | tf_op jit(solution)/shard_map/ppermute | solution.py:37

commit v6 on v4

--- a/solution.py
+++ b/solution.py
@@ -566,8 +566,8 @@
 
 def third_kernel(corridor, tiles, surf, east, south, *refs):
     faces = refs[:4]
-    total, keep, given_2, own, takes, masks, takes_near, masks_near = refs[4:12]
-    surf_3, east_3, south_3, own_term, partner_term, other_term = refs[12:]
+    total, keep, given_2, own, takes, masks, takes_near, masks_near, count, bed = refs[4:14]
+    surf_3, east_3, south_3, own_term, partner_term, other_term = refs[14:20]
     ext, columns = surf.shape
     rows = ext - 2 * HALO
     mine = slice(0, rows)
@@ -607,8 +607,26 @@
     partner_term[...] = terms[:, owned : 2 * owned]
     other_term[...] = terms[:, 2 * owned :]
 
-
-def last_kernel(corridor, tiles, surf_2, east_2, south_3, *refs):
+    @pl.when(is_edge(tiles))
+    def _():
+        last_substep(
+            *(corridor, tiles, surf, east, south_3, *faces, total, count, keep, bed),
+            *(None, east_3, surf_3, *refs[20:]),
+        )
+
+
+def is_edge(tiles):
+    position = lax.axis_index("gy")
+    return (position == 0) | (position == tiles - 1)
+
+
+def last_kernel(corridor, tiles, *refs):
+    @pl.when(jnp.logical_not(is_edge(tiles)))
+    def _():
+        last_substep(corridor, tiles, *refs[:13], *refs[16:])
+
+
+def last_substep(corridor, tiles, surf_2, east_2, south_3, *refs):
     faces = refs[:4]
     total_2, count, keep, bed, _, east_3 = refs[4:10]
     surf_3, depth_out, east_out, south_out = refs[10:14]
@@ -781,25 +799,31 @@
         scratch=[field],
         aliases={12 + slot: slot for slot in range(4)},
     )
-    surf_3, east_3, south_3, own_term, partner_term, other_term = call(
+    last_scratch = [small, small, field, field, small]
+    last_scratch.append(pltpu.SemaphoreType.DMA((2 + -(-chunks // 5),)))
+    surf_3, east_3, south_3, own_term, partner_term, other_term, *results = call(
         functools.partial(third_kernel, corridor, tiles),
         "third",
-        [field] * 3 + [term] * 3,
+        [field] * 3 + [term] * 3 + [result] * 3,
         (
             *(surf_2, east_2, south_2, *faces, total_2, keep, given_2),
-            *(own, takes, masks, takes_near, masks_near),
+            *(own, takes, masks, takes_near, masks_near, count, bed),
         ),
+        scratch=last_scratch,
     )
     from_other = swapped(other_term.reshape(owned), 1)
     from_partner = swapped(partner_term.reshape(owned), 0)
-    _, depth, flux_east, flux_south = call(
+    last_in = (surf_2, east_2, south_3, *faces, total_2, count, keep, bed, surf_3, east_3)
+    _, depth, flux_east, flux_south = pl.pallas_call(
         functools.partial(last_kernel, corridor, tiles),
-        "last",
-        [field, result, result, result],
-        (surf_2, east_2, south_3, *faces, total_2, count, keep, bed, surf_3, east_3),
-        scratch=[small, small, field, field, small, pltpu.SemaphoreType.DMA((2 + -(-chunks // 5),))],
-        aliases={11: 0},
-    )
+        out_shape=[field] + [result] * 3,
+        in_specs=[VMEM_SPEC] * 13 + [HBM_SPEC] * 3,
+        out_specs=[VMEM_SPEC] + [HBM_SPEC] * 3,
+        scratch_shapes=last_scratch,
+        input_output_aliases={11: 0, 13: 1, 14: 2, 15: 3},
+        compiler_params=params,
+        name="last",
+    )(*[held(value) for value in last_in], *[far(value) for value in results])
     river_section = own_term.reshape(owned) + from_other + from_partner
     return (depth, flux_east, flux_south, river_section)
 

time: 20.8 us -> 20.4 us (0.981)
  the two profiles are of different devices: /device:TPU:0 before, /device:TPU:7 now
where the time goes in v6:
time: 20.4 us; the launch traced here: 20.2 us
  Pallas kernels  8.64 us (42%)
  starting transfers between devices  8.3 us (41%)
  waiting for transfers between devices  2.01 us (10%)
  between operations  0.76 us (4%)
  other arithmetic  0.52 us (3%)
    ppermute x7, starting transfers between devices, swapped(): return lax.ppermute(value, 'gy', pairs)  8.3 us
    pallas_call x8, Pallas kernels, call(): pl.pallas_call(kernel, out_shape=outs, in_specs=[VMEM_SPEC] * len(values)...  4.42 us
    ppermute x7, waiting for transfers between devices, swapped(): return lax.ppermute(value, 'gy', pairs)  2.01 us
    pallas_call x1, Pallas kernels, local(): pl.pallas_call(functools.partial(last_kernel, corridor, tiles), out_shape...  1.55 us
    pallas_call x1, Pallas kernels, local(): pl.pallas_call(load_kernel, out_shape=[field] * 4 + [pltpu.VMEM((rows, co...  1.44 us
    pallas_call x1, Pallas kernels, local(): pl.pallas_call(pack_kernel, out_shape=[wide, pair], in_specs=[HBM_SPEC] *...  1.24 us
    add x1, other arithmetic, local(): river_section = own_term.reshape(owned) + from_other + from_partner  0.52 us
  transfers between devices with their start and end apart: 7, of which 2 were waited for; matrix products, arithmetic and copies ran while one was open for 0% of the time, Pallas kernels for 31%

profile of v6, /device:TPU:7, one launch (start us, length us, event | category | flops | bytes accessed | tf_op | source)
XLA Modules:
  0.0 20.2 jit_solution(1869422690083066299)
XLA Ops:
  0.6 0.7 %collective-permute-start.1 = (s32[4,128]{1,0:T(4,128)}, s32[4,128]{1,0:T(4,128)S(1)}, u32[]{:S(2)}, u32[]{:S(2)}) collective-permute-start(s32[4,128]{1,0:T(4,128)} %cells.1), channel_id=1, source_target_pairs={{0,1},{1,0},{2,3},{3,2},{4,5},{5,4},{6,7},{7,6},{8,9},{9,8},{10,11... | collective-permute-start | bytes 6152 | tf_op jit(solution)/shard_map/ppermute | solution.py:37
  1.4 0.1 collective-permute-start
  1.4 1.2 %pack.1 = (f32[61,4,128]{2,1,0:T(4,128)S(1)}, f32[2,128]{1,0:T(2,128)S(1)}) custom-call(f32[32,1920]{1,0:T(8,128)} %depth_in.1, f32[32,1920]{1,0:T(8,128)} %bed_in.1, s32[32,1920]{1,0:T(8,128)} %rough_in.1, f32[32,1920]{1,0:T(8,128)} %east_in.1, f32[32,1920]{1,0:T(8,128)} %south_in.1, f32[1,128]{1,0:T(1,128)} %bitcast.15, s32[4,128]{1,0:T(4,128)} %cells.1, ...), custom_call_target="tpu_custom_call" | custom-call | tf_op jit(solution)/shard_map/pack/pallas_call | solution.py:719
  2.7 0.0 collective-permute-done
  2.7 0.0 collective-permute-done.1.cells.partner_cells
  2.7 3.5 %collective-permute-start.2 = (f32[61,4,128]{2,1,0:T(4,128)S(1)}, f32[61,4,128]{2,1,0:T(4,128)S(1)}, u32[]{:S(2)}, u32[]{:S(2)}) collective-permute-start(f32[61,4,128]{2,1,0:T(4,128)S(1)} %join.1), channel_id=1, source_target_pairs={{1,2},{2,1},{3,4},{4,3},{5,6},{6,5},{7,8},{8,7},{9,10},{10,9},{11,... | collective-permute-start | bytes 374792 | tf_op jit(solution)/shard_map/ppermute | solution.py:37
  6.2 1.4 %load.1 = (f32[40,1920]{1,0:T(8,128)S(1)}, f32[40,1920]{1,0:T(8,128)S(1)}, f32[40,1920]{1,0:T(8,128)S(1)}, f32[40,1920]{1,0:T(8,128)S(1)}, s32[32,1920]{1,0:T(8,128)S(1)}, /*index=5*/f32[8,128]{1,0:T(8,128)S(1)}) custom-call(f32[32,1920]{1,0:T(8,128)} %depth_in.1, f32[32,1920]{1,0:T(8,128)} %east_in.1, f32[32,1920]{1,0:T(8,128)} %south_in.1, ...), custom_call_target="tpu_custom_call" | custom-call | tf_op jit(solution)/shard_map/load/pallas_call | solution.py:747
  7.7 0.7 %prepare.1 = (f32[40,1920]{1,0:T(8,128)S(1)}, f32[40,1920]{1,0:T(8,128)S(1)}, f32[40,1920]{1,0:T(8,128)S(1)}, f32[40,1920]{1,0:T(8,128)S(1)}, f32[40,1920]{1,0:T...) custom-call(f32[8,128]{1,0:T(8,128)S(1)} %get-tuple-element.66.table, ...), custom_call_target="tpu_custom_call", output_to_operand_aliasing={{0}: (2, {}), {1}: (3, {}), {2}: (4, {}), {3}: (5, {})} | custom-call | tf_op jit(solution)/shard_map/prepare/pallas_call | solution.py:699
  8.3 0.1 collective-permute-start.4
  8.4 0.5 %nodes.1 = (f32[40,1920]{1,0:T(8,128)S(1)}, f32[40,1920]{1,0:T(8,128)S(1)}, bf16[2,256,512]{2,1,0:T(8,128)(2,1)S(1)}, f32[2,256,128]{2,1,0:T(8,128)S(1)}, f32[32...) custom-call(f32[40,1920]{1,0:T(8,128)S(1)} %get-tuple-element.72.surf.refs_0_, f32[2,128]{1,0:T(2,128)S(1)} %get-tuple-element.73.own.refs_7_, ...), custom_call_target="tpu_custom_call" | custom-call | tf_op jit(solution)/shard_map/nodes/pallas_call | solution.py:699
  9.0 1.0 %collective-permute-done.2.by_other = f32[61,4,128]{2,1,0:T(4,128)S(1)} collective-permute-done((f32[61,4,128]{2,1,0:T(4,128)S(1)}, f32[61,4,128]{2,1,0:T(4,128)S(1)}, u32[]{:S(2)}, u32[]{:S(2)}) %collective-permute-start.2) | collective-permute-done | bytes 124960 | tf_op jit(solution)/shard_map/ppermute | solution.py:37
  10.0 0.8 %collective-permute-start.3 = (f32[2,128]{1,0:T(2,128)S(1)}, f32[2,128]{1,0:T(2,128)S(1)}, u32[]{:S(2)}, u32[]{:S(2)}) collective-permute-start(f32[2,128]{1,0:T(2,128)S(1)} %get-tuple-element.75.near), channel_id=1, source_target_pairs={{0,1},{1,0},{2,3},{3,2},{4,5},{5,4},{6,7},{7,6},{8,9},{9,8},{10,11... | collective-permute-start | bytes 3080 | tf_op jit(solution)/shard_map/ppermute | solution.py:37
  10.7 0.0 collective-permute-done.4.by_partner
  10.7 0.5 %border.1 = (f32[40,1920]{1,0:T(8,128)S(1)}, f32[40,1920]{1,0:T(8,128)S(1)}, f32[40,1920]{1,0:T(8,128)S(1)}, f32[40,1920]{1,0:T(8,128)S(1)}, f32[40,1920]{1,0:T(...) custom-call(f32[60,4,128]{2,1,0:T(4,128)S(1)} %collective-permute-do, ...), custom_call_target="tpu_custom_call", output_to_operand_aliasing={{0}: (4, {}), {1}: (5, {}), {2}: (6, {}), {3}: (7, {}), {4}... | custom-call | tf_op jit(solution)/shard_map/border/pallas_call | solution.py:699
  11.3 0.3 %first.1 = (f32[40,1920]{1,0:T(8,128)S(1)}, f32[40,1920]{1,0:T(8,128)S(1)}, f32[40,1920]{1,0:T(8,128)S(1)}, f32[40,1920]{1,0:T(8,128)S(1)}) custom-call(f32[40,1920]{1,0:T(8,128)S(1)} %get-tuple-element.88.surf, f32[40,1920]{1,0:T(8,128)S(1)} %get-tuple-element.89.east, f32[40,1920]{1,0:T(8,128)S(1)} %get-tuple-element.90.south, ...), custom_call_target="tpu_custom_call" | custom-call | tf_op jit(solution)/shard_map/first/pallas_call | solution.py:699
  11.6 0.0 collective-permute-done.3.far
  11.6 1.1 %second.1 = (f32[40,1920]{1,0:T(8,128)S(1)}, f32[40,1920]{1,0:T(8,128)S(1)}, f32[40,1920]{1,0:T(8,128)S(1)}, f32[40,1920]{1,0:T(8,128)S(1)}, f32[40,1920]{1,0:T(...) custom-call(f32[2,128]{1,0:T(2,128)S(1)} %collective-permute-done.3., ...), custom_call_target="tpu_custom_call", output_to_operand_aliasing={{0}: (12, {}), {1}: (13, {}), {2}: (14, {}), {3}: (15, {})} | custom-call | tf_op jit(solution)/shard_map/second/pallas_call | solution.py:699
  12.7 1.2 %third.1 = (f32[40,1920]{1,0:T(8,128)S(1)}, f32[40,1920]{1,0:T(8,128)S(1)}, f32[40,1920]{1,0:T(8,128)S(1)}, f32[1,128]{1,0:T(1,128)S(1)}, f32[1,128]{1,0:T(1,128...) custom-call(f32[40,1920]{1,0:T(8,128)S(1)} %get-tuple-element.103.surf.refs_0_, ...), custom_call_target="tpu_custom_call" | custom-call | tf_op jit(solution)/shard_map/third/pallas_call | solution.py:699
  13.9 3.1 %collective-permute-start.5 = (f32[128]{0:T(128)S(1)}, f32[128]{0:T(128)S(1)}, u32[]{:S(2)}, u32[]{:S(2)}) collective-permute-start(f32[128]{0:T(128)S(1)} %bitcast.12), channel_id=1, source_target_pairs={{1,2},{2,1},{3,4},{4,3},{5,6},{6,5},{7,8},{8,7},{9,10},{10,9},{11,... | collective-permute-start | bytes 1544 | tf_op jit(solution)/shard_map/ppermute | solution.py:37
  17.1 0.1 collective-permute-start.6
  17.1 1.5 %last.1 = (f32[40,1920]{1,0:T(8,128)S(1)}, f32[32,1920]{1,0:T(8,128)}, f32[32,1920]{1,0:T(8,128)}, f32[32,1920]{1,0:T(8,128)}) custom-call(f32[40,1920]{1,0:T(8,128)S(1)} %get-tuple-element.103.surf.refs_0_, f32[40,1920]{1,0:T(8,128)S(1)} %get-tuple-element.104.east.refs_1_, ...), custom_call_target="tpu_custom_call", output_to_operand_aliasing={{0}: (11, {}), {1}: (13, {}), {2}: (14, {}), {3}: (15, {})} | custom-call | tf_op jit(solution)/shard_map/last/pallas_call | solution.py:817
  18.7 1.0 %collective-permute-done.5 = f32[128]{0:T(128)S(1)} collective-permute-done((f32[128]{0:T(128)S(1)}, f32[128]{0:T(128)S(1)}, u32[]{:S(2)}, u32[]{:S(2)}) %collective-permute-start.5) | collective-permute-done | bytes 544 | tf_op jit(solution)/shard_map/ppermute | solution.py:37
  19.7 0.0 collective-permute-done.6
  19.7 0.5 %fusion = f32[128]{0:T(128)} fusion(f32[128]{0:T(128)S(1)} %collective-permute-done.6, f32[128]{0:T(128)S(1)} %collective-permute-done.5, f32[1,128]{1,0:T(1,128)S(1)} %get-tuple-element.123), kind=kLoop, calls=%fused_computation.1 | loop fusion | flops 256 | bytes 2048 | tf_op jit(solution)/shard_map/add | solution.py:827
  (2 shorter events, 0.0 us)
Async XLA Ops:
  0.6 2.1 %collective-permute-start.1 = (s32[4,128]{1,0:T(4,128)}, s32[4,128]{1,0:T(4,128)S(1)}, u32[]{:S(2)}, u32[]{:S(2)}) collective-permute-start(s32[4,128]{1,0:T(4,128)} %cells.1), channel_id=1, source_target_pairs={{0,1},{1,0},{2,3},{3,2},{4,5},{5,4},{6,7},{7,6},{8,9},{9,8},{10,11... | collective-permute-start | bytes 6152 | tf_op jit(solution)/shard_map/ppermute | solution.py:37
  1.4 1.3 %collective-permute-start = (f32[128]{0:T(128)}, f32[128]{0:T(128)S(1)}, u32[]{:S(2)}, u32[]{:S(2)}) collective-permute-start(f32[128]{0:T(128)} %param.11), channel_id=1, source_target_pairs={{0,1},{1,0},{2,3},{3,2},{4,5},{5,4},{6,7},{7,6},{8,9},{9,8},{10,11... | collective-permute-start | bytes 1544 | tf_op jit(solution)/shard_map/ppermute | solution.py:37
  2.7 7.2 %collective-permute-start.2 = (f32[61,4,128]{2,1,0:T(4,128)S(1)}, f32[61,4,128]{2,1,0:T(4,128)S(1)}, u32[]{:S(2)}, u32[]{:S(2)}) collective-permute-start(f32[61,4,128]{2,1,0:T(4,128)S(1)} %join.1), channel_id=1, source_target_pairs={{1,2},{2,1},{3,4},{4,3},{5,6},{6,5},{7,8},{8,7},{9,10},{10,9},{11,... | collective-permute-start | bytes 374792 | tf_op jit(solution)/shard_map/ppermute | solution.py:37
  8.3 2.4 %collective-permute-start.4 = (f32[60,4,128]{2,1,0:T(4,128)S(1)}, f32[60,4,128]{2,1,0:T(4,128)S(1)}, u32[]{:S(2)}, u32[]{:S(2)}) collective-permute-start(f32[60,4,128]{2,1,0:T(4,128)S(1)} %get-tuple-element.77), channel_id=1, source_target_pairs={{0,1},{1,0},{2,3},{3,2},{4,5},{5,4},{6,7},{7,6},{8,9},{9,8},{10,11... | collective-permute-start | bytes 368648 | tf_op jit(solution)/shard_map/ppermute | solution.py:37
  10.0 1.7 %collective-permute-start.3 = (f32[2,128]{1,0:T(2,128)S(1)}, f32[2,128]{1,0:T(2,128)S(1)}, u32[]{:S(2)}, u32[]{:S(2)}) collective-permute-start(f32[2,128]{1,0:T(2,128)S(1)} %get-tuple-element.75.near), channel_id=1, source_target_pairs={{0,1},{1,0},{2,3},{3,2},{4,5},{5,4},{6,7},{7,6},{8,9},{9,8},{10,11... | collective-permute-start | bytes 3080 | tf_op jit(solution)/shard_map/ppermute | solution.py:37
  13.9 5.8 %collective-permute-start.5 = (f32[128]{0:T(128)S(1)}, f32[128]{0:T(128)S(1)}, u32[]{:S(2)}, u32[]{:S(2)}) collective-permute-start(f32[128]{0:T(128)S(1)} %bitcast.12), channel_id=1, source_target_pairs={{1,2},{2,1},{3,4},{4,3},{5,6},{6,5},{7,8},{8,7},{9,10},{10,9},{11,... | collective-permute-start | bytes 1544 | tf_op jit(solution)/shard_map/ppermute | solution.py:37
  17.1 2.6 %collective-permute-start.6 = (f32[128]{0:T(128)S(1)}, f32[128]{0:T(128)S(1)}, u32[]{:S(2)}, u32[]{:S(2)}) collective-permute-start(f32[128]{0:T(128)S(1)} %bitcast.11), channel_id=1, source_target_pairs={{0,1},{1,0},{2,3},{3,2},{4,5},{5,4},{6,7},{7,6},{8,9},{9,8},{10,11... | collective-permute-start | bytes 1544 | tf_op jit(solution)/shard_map/ppermute | solution.py:37

commit v7 on v6

--- a/solution.py
+++ b/solution.py
@@ -505,8 +505,8 @@
         after[:, at] = value if before is None else before[:, at] + value
 
 
-def first_kernel(corridor, surf, east, south, number, total, windows, *refs):
-    surf_1, total_1, count, keep, total_0 = refs
+def first_kernel(corridor, surf, east, south, number, total, windows, given_1, *refs):
+    surf_1, total_1, count, keep, total_2, sums_2, given_2, total_0 = refs
     rows = surf.shape[0] - 2 * HALO
     chunks = surf.shape[1] // LANES
     own = slice(0, rows)
@@ -518,15 +518,19 @@
         total_0[own, at] = FEED * total[own, at]
     windows = [windows[:, cols(chunk)] for chunk in range(chunks)]
     sums = exchange(corridor, own, surf, total_0, count, total_1, windows)
+    after = summed(corridor, own, total_1)
     for chunk, new_surf in settled(own, surf, east, south, keep, sums):
         surf_1[own, cols(chunk)] = new_surf
+        sums_2[:, cols(chunk)] = after[chunk]
+    refill(corridor, own, surf_1, total_1, count, total_2)
+    give(corridor, 1, surf_1, given_1, given_2)
 
 
 def second_kernel(corridor, tiles, far, beyond, surf, east, south, *refs):
     faces = refs[:4]
-    number, total, given_1 = refs[4:7]
-    surf_1, total_1, count, keep = refs[11:15]
-    surf_2, east_2, south_2, total_2, given_2, total_0 = refs[15:]
+    number, total, sums_2 = refs[4:7]
+    surf_1, total_1, count, keep, total_2 = refs[12:17]
+    surf_2, east_2, south_2, total_0 = refs[17:]
     ext, columns = surf.shape
     rows = ext - 2 * HALO
     chunks = columns // LANES
@@ -552,8 +556,7 @@
     own = slice(0, rows)
     before = (surf_1, east, south)
     fluxes(own, rows - 8, None, before, faces, east_2, south_2)
-    own_sums = exchange(corridor, own, surf_1, total_1, count, total_2)
-    give(corridor, 1, surf_1, given_1, given_2)
+    own_sums = [sums_2[:, cols(chunk)] for chunk in range(chunks)]
 
     for chunk, new_surf in settled(tail, surf, east, south, keep, sums):
         surf_1[tail, cols(chunk)] = new_surf
@@ -781,23 +784,23 @@
         aliases={4 + slot: slot for slot in range(11)},
     )
     surf, east, south, bed, _, *faces, number, total = fields
-    surf_1, total_1, count, keep = call(
+    surf_1, total_1, count, keep, total_2, sums_2, given_2 = call(
         functools.partial(first_kernel, corridor),
         "first",
-        [field] * 4,
-        (surf, east, south, number, total, windows),
+        [field] * 5 + [small] * 2,
+        (surf, east, south, number, total, windows, given_1),
         scratch=[field],
     )
-    surf_1, total_1, count, keep, surf_2, east_2, south_2, total_2, given_2 = call(
+    surf_1, total_1, count, keep, total_2, surf_2, east_2, south_2 = call(
         functools.partial(second_kernel, corridor, tiles),
         "second",
-        [field] * 8 + [small],
+        [field] * 8,
         (
-            *(from_far, beyond, surf, east, south, *faces, number, total, given_1),
-            *(surf_1, total_1, count, keep),
+            *(from_far, beyond, surf, east, south, *faces, number, total, sums_2),
+            *(surf_1, total_1, count, keep, total_2),
         ),
         scratch=[field],
-        aliases={12 + slot: slot for slot in range(4)},
+        aliases={12 + slot: slot for slot in range(5)},
     )
     last_scratch = [small, small, field, field, small]
     last_scratch.append(pltpu.SemaphoreType.DMA((2 + -(-chunks // 5),)))

time: 20.4 us -> 20.5 us (level)
  transfers between devices with their start and end apart: 7 -> 7, of which waited for: 2 -> 2; matrix products, arithmetic and copies ran while one was open for 0% -> 0% of each run, Pallas kernels for 31% -> 32%
where the time goes in v7:
time: 20.5 us; the launch traced here: 20.3 us
  Pallas kernels  8.7 us (42%)
  starting transfers between devices  8.3 us (40%)
  waiting for transfers between devices  2.01 us (10%)
  between operations  0.76 us (4%)
  other arithmetic  0.52 us (3%)
    ppermute x7, starting transfers between devices, swapped(): return lax.ppermute(value, 'gy', pairs)  8.3 us
    pallas_call x8, Pallas kernels, call(): pl.pallas_call(kernel, out_shape=outs, in_specs=[VMEM_SPEC] * len(values)...  4.47 us
    ppermute x7, waiting for transfers between devices, swapped(): return lax.ppermute(value, 'gy', pairs)  2.01 us
    pallas_call x1, Pallas kernels, local(): pl.pallas_call(functools.partial(last_kernel, corridor, tiles), out_shape...  1.55 us
    pallas_call x1, Pallas kernels, local(): pl.pallas_call(load_kernel, out_shape=[field] * 4 + [pltpu.VMEM((rows, co...  1.44 us
    pallas_call x1, Pallas kernels, local(): pl.pallas_call(pack_kernel, out_shape=[wide, pair], in_specs=[HBM_SPEC] *...  1.24 us
    add x1, other arithmetic, local(): river_section = own_term.reshape(owned) + from_other + from_partner  0.52 us
  transfers between devices with their start and end apart: 7, of which 2 were waited for; matrix products, arithmetic and copies ran while one was open for 0% of the time, Pallas kernels for 32%

profile of v7, /device:TPU:7, one launch (start us, length us, event | category | flops | bytes accessed | tf_op | source)
XLA Modules:
  0.0 20.3 jit_solution(3906897475581226538)
XLA Ops:
  0.6 0.7 %collective-permute-start.1 = (s32[4,128]{1,0:T(4,128)}, s32[4,128]{1,0:T(4,128)S(1)}, u32[]{:S(2)}, u32[]{:S(2)}) collective-permute-start(s32[4,128]{1,0:T(4,128)} %cells.1), channel_id=1, source_target_pairs={{0,1},{1,0},{2,3},{3,2},{4,5},{5,4},{6,7},{7,6},{8,9},{9,8},{10,11... | collective-permute-start | bytes 6152 | tf_op jit(solution)/shard_map/ppermute | solution.py:37
  1.4 0.1 collective-permute-start
  1.4 1.2 %pack.1 = (f32[61,4,128]{2,1,0:T(4,128)S(1)}, f32[2,128]{1,0:T(2,128)S(1)}) custom-call(f32[32,1920]{1,0:T(8,128)} %depth_in.1, f32[32,1920]{1,0:T(8,128)} %bed_in.1, s32[32,1920]{1,0:T(8,128)} %rough_in.1, f32[32,1920]{1,0:T(8,128)} %east_in.1, f32[32,1920]{1,0:T(8,128)} %south_in.1, f32[1,128]{1,0:T(1,128)} %bitcast.15, s32[4,128]{1,0:T(4,128)} %cells.1, ...), custom_call_target="tpu_custom_call" | custom-call | tf_op jit(solution)/shard_map/pack/pallas_call | solution.py:722
  2.7 0.0 collective-permute-done
  2.7 0.0 collective-permute-done.1.cells.partner_cells
  2.7 3.5 %collective-permute-start.2 = (f32[61,4,128]{2,1,0:T(4,128)S(1)}, f32[61,4,128]{2,1,0:T(4,128)S(1)}, u32[]{:S(2)}, u32[]{:S(2)}) collective-permute-start(f32[61,4,128]{2,1,0:T(4,128)S(1)} %join.1), channel_id=1, source_target_pairs={{1,2},{2,1},{3,4},{4,3},{5,6},{6,5},{7,8},{8,7},{9,10},{10,9},{11,... | collective-permute-start | bytes 374792 | tf_op jit(solution)/shard_map/ppermute | solution.py:37
  6.2 1.4 %load.1 = (f32[40,1920]{1,0:T(8,128)S(1)}, f32[40,1920]{1,0:T(8,128)S(1)}, f32[40,1920]{1,0:T(8,128)S(1)}, f32[40,1920]{1,0:T(8,128)S(1)}, s32[32,1920]{1,0:T(8,128)S(1)}, /*index=5*/f32[8,128]{1,0:T(8,128)S(1)}) custom-call(f32[32,1920]{1,0:T(8,128)} %depth_in.1, f32[32,1920]{1,0:T(8,128)} %east_in.1, f32[32,1920]{1,0:T(8,128)} %south_in.1, ...), custom_call_target="tpu_custom_call" | custom-call | tf_op jit(solution)/shard_map/load/pallas_call | solution.py:750
  7.7 0.7 %prepare.1 = (f32[40,1920]{1,0:T(8,128)S(1)}, f32[40,1920]{1,0:T(8,128)S(1)}, f32[40,1920]{1,0:T(8,128)S(1)}, f32[40,1920]{1,0:T(8,128)S(1)}, f32[40,1920]{1,0:T...) custom-call(f32[8,128]{1,0:T(8,128)S(1)} %get-tuple-element.68.table, ...), custom_call_target="tpu_custom_call", output_to_operand_aliasing={{0}: (2, {}), {1}: (3, {}), {2}: (4, {}), {3}: (5, {})} | custom-call | tf_op jit(solution)/shard_map/prepare/pallas_call | solution.py:702
  8.3 0.1 collective-permute-start.4
  8.4 0.5 %nodes.1 = (f32[40,1920]{1,0:T(8,128)S(1)}, f32[40,1920]{1,0:T(8,128)S(1)}, bf16[2,256,512]{2,1,0:T(8,128)(2,1)S(1)}, f32[2,256,128]{2,1,0:T(8,128)S(1)}, f32[32...) custom-call(f32[40,1920]{1,0:T(8,128)S(1)} %get-tuple-element.74.surf.refs_0_, f32[2,128]{1,0:T(2,128)S(1)} %get-tuple-element.75.own.refs_7_, ...), custom_call_target="tpu_custom_call" | custom-call | tf_op jit(solution)/shard_map/nodes/pallas_call | solution.py:702
  9.0 1.0 %collective-permute-done.2.by_other = f32[61,4,128]{2,1,0:T(4,128)S(1)} collective-permute-done((f32[61,4,128]{2,1,0:T(4,128)S(1)}, f32[61,4,128]{2,1,0:T(4,128)S(1)}, u32[]{:S(2)}, u32[]{:S(2)}) %collective-permute-start.2) | collective-permute-done | bytes 124960 | tf_op jit(solution)/shard_map/ppermute | solution.py:37
  10.0 0.8 %collective-permute-start.3 = (f32[2,128]{1,0:T(2,128)S(1)}, f32[2,128]{1,0:T(2,128)S(1)}, u32[]{:S(2)}, u32[]{:S(2)}) collective-permute-start(f32[2,128]{1,0:T(2,128)S(1)} %get-tuple-element.77.near), channel_id=1, source_target_pairs={{0,1},{1,0},{2,3},{3,2},{4,5},{5,4},{6,7},{7,6},{8,9},{9,8},{10,11... | collective-permute-start | bytes 3080 | tf_op jit(solution)/shard_map/ppermute | solution.py:37
  10.7 0.0 collective-permute-done.4.by_partner
  10.7 0.5 %border.1 = (f32[40,1920]{1,0:T(8,128)S(1)}, f32[40,1920]{1,0:T(8,128)S(1)}, f32[40,1920]{1,0:T(8,128)S(1)}, f32[40,1920]{1,0:T(8,128)S(1)}, f32[40,1920]{1,0:T(...) custom-call(f32[60,4,128]{2,1,0:T(4,128)S(1)} %collective-permute-do, ...), custom_call_target="tpu_custom_call", output_to_operand_aliasing={{0}: (4, {}), {1}: (5, {}), {2}: (6, {}), {3}: (7, {}), {4}... | custom-call | tf_op jit(solution)/shard_map/border/pallas_call | solution.py:702
  11.3 0.6 %first.1 = (f32[40,1920]{1,0:T(8,128)S(1)}, f32[40,1920]{1,0:T(8,128)S(1)}, f32[40,1920]{1,0:T(8,128)S(1)}, f32[40,1920]{1,0:T(8,128)S(1)}, f32[40,1920]{1,0:T(8...) custom-call(f32[40,1920]{1,0:T(8,128)S(1)} %get-tuple-element.90.surf, f32[40,1920]{1,0:T(8,128)S(1)} %get-tuple-element.91.east, ...), custom_call_target="tpu_custom_call" | custom-call | tf_op jit(solution)/shard_map/first/pallas_call | solution.py:702
  11.9 0.0 collective-permute-done.3.far
  11.9 0.9 %second.1 = (f32[40,1920]{1,0:T(8,128)S(1)}, f32[40,1920]{1,0:T(8,128)S(1)}, f32[40,1920]{1,0:T(8,128)S(1)}, f32[40,1920]{1,0:T(8,128)S(1)}, f32[40,1920]{1,0:T(...) custom-call(f32[2,128]{1,0:T(2,128)S(1)} %collective-permute-done.3., ...), custom_call_target="tpu_custom_call", output_to_operand_aliasing={{0}: (12, {}), {1}: (13, {}), {2}: (14, {}), {3}: (15, {}),... | custom-call | tf_op jit(solution)/shard_map/second/pallas_call | solution.py:702
  12.8 1.2 %third.1 = (f32[40,1920]{1,0:T(8,128)S(1)}, f32[40,1920]{1,0:T(8,128)S(1)}, f32[40,1920]{1,0:T(8,128)S(1)}, f32[1,128]{1,0:T(1,128)S(1)}, f32[1,128]{1,0:T(1,128...) custom-call(f32[40,1920]{1,0:T(8,128)S(1)} %get-tuple-element.107.surf.refs_0_, ...), custom_call_target="tpu_custom_call" | custom-call | tf_op jit(solution)/shard_map/third/pallas_call | solution.py:702
  14.0 3.1 %collective-permute-start.5 = (f32[128]{0:T(128)S(1)}, f32[128]{0:T(128)S(1)}, u32[]{:S(2)}, u32[]{:S(2)}) collective-permute-start(f32[128]{0:T(128)S(1)} %bitcast.12), channel_id=1, source_target_pairs={{1,2},{2,1},{3,4},{4,3},{5,6},{6,5},{7,8},{8,7},{9,10},{10,9},{11,... | collective-permute-start | bytes 1544 | tf_op jit(solution)/shard_map/ppermute | solution.py:37
  17.1 0.1 collective-permute-start.6
  17.2 1.6 %last.1 = (f32[40,1920]{1,0:T(8,128)S(1)}, f32[32,1920]{1,0:T(8,128)}, f32[32,1920]{1,0:T(8,128)}, f32[32,1920]{1,0:T(8,128)}) custom-call(f32[40,1920]{1,0:T(8,128)S(1)} %get-tuple-element.107.surf.refs_0_, f32[40,1920]{1,0:T(8,128)S(1)} %get-tuple-element.108.east.refs_1_, ...), custom_call_target="tpu_custom_call", output_to_operand_aliasing={{0}: (11, {}), {1}: (13, {}), {2}: (14, {}), {3}: (15, {})} | custom-call | tf_op jit(solution)/shard_map/last/pallas_call | solution.py:820
  18.8 1.0 %collective-permute-done.5 = f32[128]{0:T(128)S(1)} collective-permute-done((f32[128]{0:T(128)S(1)}, f32[128]{0:T(128)S(1)}, u32[]{:S(2)}, u32[]{:S(2)}) %collective-permute-start.5) | collective-permute-done | bytes 544 | tf_op jit(solution)/shard_map/ppermute | solution.py:37
  19.8 0.0 collective-permute-done.6
  19.8 0.5 %fusion = f32[128]{0:T(128)} fusion(f32[128]{0:T(128)S(1)} %collective-permute-done.6, f32[128]{0:T(128)S(1)} %collective-permute-done.5, f32[1,128]{1,0:T(1,128)S(1)} %get-tuple-element.127), kind=kLoop, calls=%fused_computation.1 | loop fusion | flops 256 | bytes 2048 | tf_op jit(solution)/shard_map/add | solution.py:830
  (2 shorter events, 0.0 us)
Async XLA Ops:
  0.6 2.1 %collective-permute-start.1 = (s32[4,128]{1,0:T(4,128)}, s32[4,128]{1,0:T(4,128)S(1)}, u32[]{:S(2)}, u32[]{:S(2)}) collective-permute-start(s32[4,128]{1,0:T(4,128)} %cells.1), channel_id=1, source_target_pairs={{0,1},{1,0},{2,3},{3,2},{4,5},{5,4},{6,7},{7,6},{8,9},{9,8},{10,11... | collective-permute-start | bytes 6152 | tf_op jit(solution)/shard_map/ppermute | solution.py:37
  1.4 1.3 %collective-permute-start = (f32[128]{0:T(128)}, f32[128]{0:T(128)S(1)}, u32[]{:S(2)}, u32[]{:S(2)}) collective-permute-start(f32[128]{0:T(128)} %param.11), channel_id=1, source_target_pairs={{0,1},{1,0},{2,3},{3,2},{4,5},{5,4},{6,7},{7,6},{8,9},{9,8},{10,11... | collective-permute-start | bytes 1544 | tf_op jit(solution)/shard_map/ppermute | solution.py:37
  2.7 7.2 %collective-permute-start.2 = (f32[61,4,128]{2,1,0:T(4,128)S(1)}, f32[61,4,128]{2,1,0:T(4,128)S(1)}, u32[]{:S(2)}, u32[]{:S(2)}) collective-permute-start(f32[61,4,128]{2,1,0:T(4,128)S(1)} %join.1), channel_id=1, source_target_pairs={{1,2},{2,1},{3,4},{4,3},{5,6},{6,5},{7,8},{8,7},{9,10},{10,9},{11,... | collective-permute-start | bytes 374792 | tf_op jit(solution)/shard_map/ppermute | solution.py:37
  8.3 2.4 %collective-permute-start.4 = (f32[60,4,128]{2,1,0:T(4,128)S(1)}, f32[60,4,128]{2,1,0:T(4,128)S(1)}, u32[]{:S(2)}, u32[]{:S(2)}) collective-permute-start(f32[60,4,128]{2,1,0:T(4,128)S(1)} %get-tuple-element.79), channel_id=1, source_target_pairs={{0,1},{1,0},{2,3},{3,2},{4,5},{5,4},{6,7},{7,6},{8,9},{9,8},{10,11... | collective-permute-start | bytes 368648 | tf_op jit(solution)/shard_map/ppermute | solution.py:37
  10.0 1.9 %collective-permute-start.3 = (f32[2,128]{1,0:T(2,128)S(1)}, f32[2,128]{1,0:T(2,128)S(1)}, u32[]{:S(2)}, u32[]{:S(2)}) collective-permute-start(f32[2,128]{1,0:T(2,128)S(1)} %get-tuple-element.77.near), channel_id=1, source_target_pairs={{0,1},{1,0},{2,3},{3,2},{4,5},{5,4},{6,7},{7,6},{8,9},{9,8},{10,11... | collective-permute-start | bytes 3080 | tf_op jit(solution)/shard_map/ppermute | solution.py:37
  14.0 5.8 %collective-permute-start.5 = (f32[128]{0:T(128)S(1)}, f32[128]{0:T(128)S(1)}, u32[]{:S(2)}, u32[]{:S(2)}) collective-permute-start(f32[128]{0:T(128)S(1)} %bitcast.12), channel_id=1, source_target_pairs={{1,2},{2,1},{3,4},{4,3},{5,6},{6,5},{7,8},{8,7},{9,10},{10,9},{11,... | collective-permute-start | bytes 1544 | tf_op jit(solution)/shard_map/ppermute | solution.py:37
  17.1 2.6 %collective-permute-start.6 = (f32[128]{0:T(128)S(1)}, f32[128]{0:T(128)S(1)}, u32[]{:S(2)}, u32[]{:S(2)}) collective-permute-start(f32[128]{0:T(128)S(1)} %bitcast.11), channel_id=1, source_target_pairs={{0,1},{1,0},{2,3},{3,2},{4,5},{5,4},{6,7},{7,6},{8,9},{9,8},{10,11... | collective-permute-start | bytes 1544 | tf_op jit(solution)/shard_map/ppermute | solution.py:37

commit v8 on v7

--- a/solution.py
+++ b/solution.py
@@ -360,17 +360,36 @@
     return ((row == ext - 1) & (position == 0)) | ((row == rows - 1) & (position == tiles - 1))
 
 
-def border_kernel(reach, tiles, by_partner, by_other, table_rows, near, *refs):
-    surf, east, south, bed, mann, bed_e, bed_s, drag_e, drag_s, number, total, takes, masks = refs[11:]
+def near_kernel(reach, early, near, *refs):
+    number, total, takes, masks = refs[-4:]
+    ext, columns = number.shape
+    rows = ext - 2 * HALO
+    chunks = columns // LANES
+    position = lax.axis_index("gy")
+    if early:
+        refs[2][...] = near[...]
+
+    @pl.when((position % 4 == 3) if early else (position % 4 != 3))
+    def _():
+        cell = near[1:2, :]
+        valid, node_row, node_chunk, node_lane = located(cell, position, rows, ext, columns)
+        key = jnp.where(valid, node_chunk * ext + node_row, -1)
+        starts, levels = scattered(near[0:1, :], key, node_lane, chunks * ext)
+        for chunk in range(chunks):
+            at = cols(chunk)
+            number[:, at] += starts[chunk * ext : (chunk + 1) * ext]
+            total[:, at] += levels[chunk * ext : (chunk + 1) * ext]
+        key = jnp.where(valid & (node_row < rows), node_chunk * rows + node_row, -1)
+        picking(reach, rows, key, node_lane, takes, masks)
+
+
+def border_kernel(tiles, by_partner, by_other, table_rows, *refs):
+    surf, east, south, bed, mann, bed_e, bed_s, drag_e, drag_s = refs[9:]
     ext, columns = surf.shape
     rows = ext - 2 * HALO
     chunks = columns // LANES
     position = lax.axis_index("gy")
     even = position % 2 == 0
-    valid, node_row, node_chunk, node_lane = located(near[1:2, :], position, rows, ext, columns)
-    key = jnp.where(valid, node_chunk * ext + node_row, -1)
-    starts, levels = scattered(near[0:1, :], key, node_lane, chunks * ext)
-
     entries = [table_rows[k : k + 1, :] for k in range(table_rows.shape[0])]
     row = lax.broadcasted_iota(jnp.int32, (2 * HALO, LANES), 0)
     for chunk in range(chunks):
@@ -390,15 +409,10 @@
         east[rows:, at] = halos[3]
         south[rows:, at] = flux
 
-    key = jnp.where(valid & (node_row < rows), node_chunk * rows + node_row, -1)
-    picking(reach, rows, key, node_lane, takes, masks)
-
     wall = wall_of(ext, tiles)
     kept = lax.broadcasted_iota(jnp.int32, (16, LANES), 0) % 8 < 7
     for chunk in range(chunks):
         at, then = cols(chunk), cols(min(chunk + 1, chunks - 1))
-        number[:, at] += starts[chunk * ext : (chunk + 1) * ext]
-        total[:, at] += levels[chunk * ext : (chunk + 1) * ext]
         b0, m0 = bed[rows:, at], mann[rows:, at]
         bed_e[rows:, at] = jnp.maximum(b0, moved_left(b0, bed[rows:, then], 1))
         drag_e[rows:, at] = drag_of(m0, moved_left(m0, mann[rows:, then], 1))
@@ -775,15 +789,29 @@
         (fields[0], own, partner_section, partner_cells),
     )
     near, beyond = call(relay_kernel, "relay", [pair, pair], (by_other, masks))
+    near, number, total, takes_near, masks_near = call(
+        functools.partial(near_kernel, corridor, True),
+        "near_early",
+        [pair, field, field] + picks(owned),
+        (near, number, total),
+        aliases={1: 1, 2: 2},
+    )
     from_far = swapped(near, 0)
-    *fields, takes_near, masks_near = call(
-        functools.partial(border_kernel, corridor, tiles),
+    number, total, takes_near, masks_near = call(
+        functools.partial(near_kernel, corridor, False),
+        "near",
+        [field] * 2 + picks(owned),
+        (near, number, total, takes_near, masks_near),
+        aliases={1 + slot: slot for slot in range(4)},
+    )
+    fields = call(
+        functools.partial(border_kernel, tiles),
         "border",
-        [field] * 11 + picks(owned),
-        (by_partner, by_other, table_rows, near, *fields, number, total),
-        aliases={4 + slot: slot for slot in range(11)},
-    )
-    surf, east, south, bed, _, *faces, number, total = fields
+        [field] * 9,
+        (by_partner, by_other, table_rows, *fields),
+        aliases={3 + slot: slot for slot in range(9)},
+    )
+    surf, east, south, bed, _, *faces = fields
     surf_1, total_1, count, keep, total_2, sums_2, given_2 = call(
         functools.partial(first_kernel, corridor),
         "first",

time: 20.5 us -> 20.6 us (level)
  the two profiles are of different devices: /device:TPU:7 before, /device:TPU:1 now
where the time goes in v8:
time: 20.6 us; the launch traced here: 20.4 us
  starting transfers between devices  10.2 us (50%)
  Pallas kernels  8.84 us (43%)
  between operations  0.81 us (4%)
  other arithmetic  0.52 us (3%)
    ppermute x7, starting transfers between devices, swapped(): return lax.ppermute(value, 'gy', pairs)  10.2 us
    pallas_call x10, Pallas kernels, call(): pl.pallas_call(kernel, out_shape=outs, in_specs=[VMEM_SPEC] * len(values)...  4.61 us
    pallas_call x1, Pallas kernels, local(): pl.pallas_call(functools.partial(last_kernel, corridor, tiles), out_shape...  1.55 us
    pallas_call x1, Pallas kernels, local(): pl.pallas_call(load_kernel, out_shape=[field] * 4 + [pltpu.VMEM((rows, co...  1.44 us
    pallas_call x1, Pallas kernels, local(): pl.pallas_call(pack_kernel, out_shape=[wide, pair], in_specs=[HBM_SPEC] *...  1.24 us
    add x1, other arithmetic, local(): river_section = own_term.reshape(owned) + from_other + from_partner  0.52 us
  transfers between devices with their start and end apart: 7, of which 0 were waited for; matrix products, arithmetic and copies ran while one was open for 0% of the time, Pallas kernels for 33%

profile of v8, /device:TPU:1, one launch (start us, length us, event | category | flops | bytes accessed | tf_op | source)
XLA Modules:
  0.0 20.4 jit_solution(7591379259201139160)
XLA Ops:
  0.6 0.1 collective-permute-start.1
  0.8 0.5 %collective-permute-start = (f32[128]{0:T(128)}, f32[128]{0:T(128)S(1)}, u32[]{:S(2)}, u32[]{:S(2)}) collective-permute-start(f32[128]{0:T(128)} %param.11), channel_id=1, source_target_pairs={{0,1},{1,0},{2,3},{3,2},{4,5},{5,4},{6,7},{7,6},{8,9},{9,8},{10,11... | collective-permute-start | bytes 1544 | tf_op jit(solution)/shard_map/ppermute | solution.py:37
  1.2 1.2 %pack.1 = (f32[61,4,128]{2,1,0:T(4,128)S(1)}, f32[2,128]{1,0:T(2,128)S(1)}) custom-call(f32[32,1920]{1,0:T(8,128)} %depth_in.1, f32[32,1920]{1,0:T(8,128)} %bed_in.1, s32[32,1920]{1,0:T(8,128)} %rough_in.1, f32[32,1920]{1,0:T(8,128)} %east_in.1, f32[32,1920]{1,0:T(8,128)} %south_in.1, f32[1,128]{1,0:T(1,128)} %bitcast.15, s32[4,128]{1,0:T(4,128)} %cells.1, ...), custom_call_target="tpu_custom_call" | custom-call | tf_op jit(solution)/shard_map/pack/pallas_call | solution.py:736
  2.5 0.0 collective-permute-done
  2.5 0.0 collective-permute-done.1.cells.partner_cells
  2.5 4.5 %collective-permute-start.2 = (f32[61,4,128]{2,1,0:T(4,128)S(1)}, f32[61,4,128]{2,1,0:T(4,128)S(1)}, u32[]{:S(2)}, u32[]{:S(2)}) collective-permute-start(f32[61,4,128]{2,1,0:T(4,128)S(1)} %join.1), channel_id=1, source_target_pairs={{1,2},{2,1},{3,4},{4,3},{5,6},{6,5},{7,8},{8,7},{9,10},{10,9},{11,... | collective-permute-start | bytes 374792 | tf_op jit(solution)/shard_map/ppermute | solution.py:37
  7.0 1.4 %load.1 = (f32[40,1920]{1,0:T(8,128)S(1)}, f32[40,1920]{1,0:T(8,128)S(1)}, f32[40,1920]{1,0:T(8,128)S(1)}, f32[40,1920]{1,0:T(8,128)S(1)}, s32[32,1920]{1,0:T(8,128)S(1)}, /*index=5*/f32[8,128]{1,0:T(8,128)S(1)}) custom-call(f32[32,1920]{1,0:T(8,128)} %depth_in.1, f32[32,1920]{1,0:T(8,128)} %east_in.1, f32[32,1920]{1,0:T(8,128)} %south_in.1, ...), custom_call_target="tpu_custom_call" | custom-call | tf_op jit(solution)/shard_map/load/pallas_call | solution.py:764
  8.5 0.7 %prepare.1 = (f32[40,1920]{1,0:T(8,128)S(1)}, f32[40,1920]{1,0:T(8,128)S(1)}, f32[40,1920]{1,0:T(8,128)S(1)}, f32[40,1920]{1,0:T(8,128)S(1)}, f32[40,1920]{1,0:T...) custom-call(f32[8,128]{1,0:T(8,128)S(1)} %get-tuple-element.73.table, ...), custom_call_target="tpu_custom_call", output_to_operand_aliasing={{0}: (2, {}), {1}: (3, {}), {2}: (4, {}), {3}: (5, {})} | custom-call | tf_op jit(solution)/shard_map/prepare/pallas_call | solution.py:716
  9.2 0.1 collective-permute-start.4
  9.2 0.5 %nodes.1 = (f32[40,1920]{1,0:T(8,128)S(1)}, f32[40,1920]{1,0:T(8,128)S(1)}, bf16[2,256,512]{2,1,0:T(8,128)(2,1)S(1)}, f32[2,256,128]{2,1,0:T(8,128)S(1)}, f32[32...) custom-call(f32[40,1920]{1,0:T(8,128)S(1)} %get-tuple-element.79.surf.refs_0_, f32[2,128]{1,0:T(2,128)S(1)} %get-tuple-element.80.own.refs_7_, ...), custom_call_target="tpu_custom_call" | custom-call | tf_op jit(solution)/shard_map/nodes/pallas_call | solution.py:716
  9.8 0.0 collective-permute-done.2.by_other
  9.8 0.6 %collective-permute-start.3 = (f32[2,128]{1,0:T(2,128)S(1)}, f32[2,128]{1,0:T(2,128)S(1)}, u32[]{:S(2)}, u32[]{:S(2)}) collective-permute-start(f32[2,128]{1,0:T(2,128)S(1)} %get-tuple-element.85.near), channel_id=1, source_target_pairs={{0,1},{1,0},{2,3},{3,2},{4,5},{5,4},{6,7},{7,6},{8,9},{9,8},{10,11... | collective-permute-start | bytes 3080 | tf_op jit(solution)/shard_map/ppermute | solution.py:37
  10.4 0.3 %near.1 = (f32[40,1920]{1,0:T(8,128)S(1)}, f32[40,1920]{1,0:T(8,128)S(1)}, bf16[2,128,512]{2,1,0:T(8,128)(2,1)S(1)}, f32[2,128,128]{2,1,0:T(8,128)S(1)}) custom-call(f32[2,128]{1,0:T(2,128)S(1)} %get-tuple-element.85.near, f32[40,1920]{1,0:T(8,128)S(1)} %get-tuple-element.103.refs_0_, ...), custom_call_target="tpu_custom_call", output_to_operand_aliasing={{0}: (1, {}), {1}: (2, {}), {2}: (3, {}), {3}: (4, {})} | custom-call | tf_op jit(solution)/shard_map/near/pallas_call | solution.py:716
  10.8 0.0 collective-permute-done.4.by_partner
  10.8 0.3 %border.1 = (f32[40,1920]{1,0:T(8,128)S(1)}, f32[40,1920]{1,0:T(8,128)S(1)}, f32[40,1920]{1,0:T(8,128)S(1)}, f32[40,1920]{1,0:T(8,128)S(1)}, f32[40,1920]{1,0:T(...) custom-call(f32[60,4,128]{2,1,0:T(4,128)S(1)} %collective-permute-do, ...), custom_call_target="tpu_custom_call", output_to_operand_aliasing={{0}: (3, {}), {1}: (4, {}), {2}: (5, {}), {3}: (6, {}), {4}... | custom-call | tf_op jit(solution)/shard_map/border/pallas_call | solution.py:716
  11.1 0.6 %first.1 = (f32[40,1920]{1,0:T(8,128)S(1)}, f32[40,1920]{1,0:T(8,128)S(1)}, f32[40,1920]{1,0:T(8,128)S(1)}, f32[40,1920]{1,0:T(8,128)S(1)}, f32[40,1920]{1,0:T(8...) custom-call(f32[40,1920]{1,0:T(8,128)S(1)} %get-tuple-element.96.surf, f32[40,1920]{1,0:T(8,128)S(1)} %get-tuple-element.97.east, ...), custom_call_target="tpu_custom_call" | custom-call | tf_op jit(solution)/shard_map/first/pallas_call | solution.py:716
  11.6 0.0 collective-permute-done.3.far
  11.6 0.9 %second.1 = (f32[40,1920]{1,0:T(8,128)S(1)}, f32[40,1920]{1,0:T(8,128)S(1)}, f32[40,1920]{1,0:T(8,128)S(1)}, f32[40,1920]{1,0:T(8,128)S(1)}, f32[40,1920]{1,0:T(...) custom-call(f32[2,128]{1,0:T(2,128)S(1)} %collective-permute-done.3., ...), custom_call_target="tpu_custom_call", output_to_operand_aliasing={{0}: (12, {}), {1}: (13, {}), {2}: (14, {}), {3}: (15, {}),... | custom-call | tf_op jit(solution)/shard_map/second/pallas_call | solution.py:716
  12.6 1.2 %third.1 = (f32[40,1920]{1,0:T(8,128)S(1)}, f32[40,1920]{1,0:T(8,128)S(1)}, f32[40,1920]{1,0:T(8,128)S(1)}, f32[1,128]{1,0:T(1,128)S(1)}, f32[1,128]{1,0:T(1,128...) custom-call(f32[40,1920]{1,0:T(8,128)S(1)} %get-tuple-element.117.surf.refs_0_, ...), custom_call_target="tpu_custom_call" | custom-call | tf_op jit(solution)/shard_map/third/pallas_call | solution.py:716
  13.8 4.4 %collective-permute-start.5 = (f32[128]{0:T(128)S(1)}, f32[128]{0:T(128)S(1)}, u32[]{:S(2)}, u32[]{:S(2)}) collective-permute-start(f32[128]{0:T(128)S(1)} %bitcast.12), channel_id=1, source_target_pairs={{1,2},{2,1},{3,4},{4,3},{5,6},{6,5},{7,8},{8,7},{9,10},{10,9},{11,... | collective-permute-start | bytes 1544 | tf_op jit(solution)/shard_map/ppermute | solution.py:37
  18.2 0.1 collective-permute-start.6
  18.3 1.5 %last.1 = (f32[40,1920]{1,0:T(8,128)S(1)}, f32[32,1920]{1,0:T(8,128)}, f32[32,1920]{1,0:T(8,128)}, f32[32,1920]{1,0:T(8,128)}) custom-call(f32[40,1920]{1,0:T(8,128)S(1)} %get-tuple-element.117.surf.refs_0_, f32[40,1920]{1,0:T(8,128)S(1)} %get-tuple-element.118.east.refs_1_, ...), custom_call_target="tpu_custom_call", output_to_operand_aliasing={{0}: (11, {}), {1}: (13, {}), {2}: (14, {}), {3}: (15, {})} | custom-call | tf_op jit(solution)/shard_map/last/pallas_call | solution.py:848
  19.8 0.0 collective-permute-done.5
  19.8 0.0 collective-permute-done.6
  19.8 0.5 %fusion = f32[128]{0:T(128)} fusion(f32[128]{0:T(128)S(1)} %collective-permute-done.6, f32[128]{0:T(128)S(1)} %collective-permute-done.5, f32[1,128]{1,0:T(1,128)S(1)} %get-tuple-element.137), kind=kLoop, calls=%fused_computation.1 | loop fusion | flops 256 | bytes 2048 | tf_op jit(solution)/shard_map/add | solution.py:858
  (3 shorter events, 0.0 us)
Async XLA Ops:
  0.6 1.8 %collective-permute-start.1 = (s32[4,128]{1,0:T(4,128)}, s32[4,128]{1,0:T(4,128)S(1)}, u32[]{:S(2)}, u32[]{:S(2)}) collective-permute-start(s32[4,128]{1,0:T(4,128)} %cells.1), channel_id=1, source_target_pairs={{0,1},{1,0},{2,3},{3,2},{4,5},{5,4},{6,7},{7,6},{8,9},{9,8},{10,11... | collective-permute-start | bytes 6152 | tf_op jit(solution)/shard_map/ppermute | solution.py:37
  0.8 1.7 %collective-permute-start = (f32[128]{0:T(128)}, f32[128]{0:T(128)S(1)}, u32[]{:S(2)}, u32[]{:S(2)}) collective-permute-start(f32[128]{0:T(128)} %param.11), channel_id=1, source_target_pairs={{0,1},{1,0},{2,3},{3,2},{4,5},{5,4},{6,7},{7,6},{8,9},{9,8},{10,11... | collective-permute-start | bytes 1544 | tf_op jit(solution)/shard_map/ppermute | solution.py:37
  2.5 7.3 %collective-permute-start.2 = (f32[61,4,128]{2,1,0:T(4,128)S(1)}, f32[61,4,128]{2,1,0:T(4,128)S(1)}, u32[]{:S(2)}, u32[]{:S(2)}) collective-permute-start(f32[61,4,128]{2,1,0:T(4,128)S(1)} %join.1), channel_id=1, source_target_pairs={{1,2},{2,1},{3,4},{4,3},{5,6},{6,5},{7,8},{8,7},{9,10},{10,9},{11,... | collective-permute-start | bytes 374792 | tf_op jit(solution)/shard_map/ppermute | solution.py:37
  9.2 1.6 %collective-permute-start.4 = (f32[60,4,128]{2,1,0:T(4,128)S(1)}, f32[60,4,128]{2,1,0:T(4,128)S(1)}, u32[]{:S(2)}, u32[]{:S(2)}) collective-permute-start(f32[60,4,128]{2,1,0:T(4,128)S(1)} %get-tuple-element.87), channel_id=1, source_target_pairs={{0,1},{1,0},{2,3},{3,2},{4,5},{5,4},{6,7},{7,6},{8,9},{9,8},{10,11... | collective-permute-start | bytes 368648 | tf_op jit(solution)/shard_map/ppermute | solution.py:37
  9.8 1.8 %collective-permute-start.3 = (f32[2,128]{1,0:T(2,128)S(1)}, f32[2,128]{1,0:T(2,128)S(1)}, u32[]{:S(2)}, u32[]{:S(2)}) collective-permute-start(f32[2,128]{1,0:T(2,128)S(1)} %get-tuple-element.85.near), channel_id=1, source_target_pairs={{0,1},{1,0},{2,3},{3,2},{4,5},{5,4},{6,7},{7,6},{8,9},{9,8},{10,11... | collective-permute-start | bytes 3080 | tf_op jit(solution)/shard_map/ppermute | solution.py:37
  13.8 6.0 %collective-permute-start.5 = (f32[128]{0:T(128)S(1)}, f32[128]{0:T(128)S(1)}, u32[]{:S(2)}, u32[]{:S(2)}) collective-permute-start(f32[128]{0:T(128)S(1)} %bitcast.12), channel_id=1, source_target_pairs={{1,2},{2,1},{3,4},{4,3},{5,6},{6,5},{7,8},{8,7},{9,10},{10,9},{11,... | collective-permute-start | bytes 1544 | tf_op jit(solution)/shard_map/ppermute | solution.py:37
  18.2 1.6 %collective-permute-start.6 = (f32[128]{0:T(128)S(1)}, f32[128]{0:T(128)S(1)}, u32[]{:S(2)}, u32[]{:S(2)}) collective-permute-start(f32[128]{0:T(128)S(1)} %bitcast.11), channel_id=1, source_target_pairs={{0,1},{1,0},{2,3},{3,2},{4,5},{5,4},{6,7},{7,6},{8,9},{9,8},{10,11... | collective-permute-start | bytes 1544 | tf_op jit(solution)/shard_map/ppermute | solution.py:37

commit v9 on v8

--- a/solution.py
+++ b/solution.py
@@ -653,32 +653,34 @@
     chunks = columns // LANES
     own, tail = slice(0, rows), slice(rows, ext)
 
-    def copy(slot, source, target, first, last):
+    def copy(slot, source, target, first=0, last=chunks, top=0, bottom=rows):
         part = pl.ds(first * LANES, (last - first) * LANES)
+        lines = pl.ds(top, bottom - top)
         return pltpu.make_async_copy(
-            source.at[pl.ds(0, rows), part], target.at[:, part], sems.at[slot]
+            source.at[lines, part], target.at[lines, part], sems.at[slot]
         )
 
     before = (surf_3, east_3, south_3)
     tail_sums = summed(corridor, tail, total_2)
     refill(corridor, own, surf_2, total_2, count, total_3)
     fluxes(own, rows - 8, None, before, faces, east_4, south_4, scale=SLOPE)
-    copies = [copy(0, east_4, east_out, 0, chunks)]
+    copies = [copy(0, east_4, east_out), copy(1, south_4, south_out, bottom=rows - 8)]
     copies[0].start()
+    copies[1].start()
     fluxes(tail, 0, None, (surf_2, east_2, None), faces, east_tail, None)
     for chunk, new_surf in settled(tail, surf_2, east_tail, south_3, keep, tail_sums):
         surf_3[tail, cols(chunk)] = new_surf
     sums = summed(corridor, own, total_3)
     fluxes(slice(0, 0), 0, wall_of(ext, tiles), before, faces, None, south_4, scale=SLOPE)
-    copies.append(copy(1, south_4, south_out, 0, chunks))
-    copies[1].start()
-    group = 5
+    copies.append(copy(2, south_4, south_out, top=rows - 8))
+    copies[2].start()
+    group = 3
     for chunk, new_surf in settled(own, surf_3, east_4, south_4, keep, sums, spread=SPREAD):
         at = cols(chunk)
         depth_4[:, at] = new_surf - bed[own, at]
         if (chunk + 1) % group == 0 or chunk + 1 == chunks:
             first = chunk // group
-            copies.append(copy(2 + first, depth_4, depth_out, first * group, chunk + 1))
+            copies.append(copy(3 + first, depth_4, depth_out, first * group, chunk + 1))
             copies[-1].start()
     for one in copies:
         one.wait()
@@ -831,7 +833,7 @@
         aliases={12 + slot: slot for slot in range(5)},
     )
     last_scratch = [small, small, field, field, small]
-    last_scratch.append(pltpu.SemaphoreType.DMA((2 + -(-chunks // 5),)))
+    last_scratch.append(pltpu.SemaphoreType.DMA((3 + -(-chunks // 3),)))
     surf_3, east_3, south_3, own_term, partner_term, other_term, *results = call(
         functools.partial(third_kernel, corridor, tiles),
         "third",

time: 20.6 us -> 20.6 us (level)
  no operation moved by 1% of the time
where the time goes in v9:
time: 20.6 us; the launch traced here: 20.4 us
  starting transfers between devices  10.2 us (50%)
  Pallas kernels  8.85 us (43%)
  between operations  0.81 us (4%)
  other arithmetic  0.52 us (3%)
    ppermute x7, starting transfers between devices, swapped(): return lax.ppermute(value, 'gy', pairs)  10.2 us
    pallas_call x10, Pallas kernels, call(): pl.pallas_call(kernel, out_shape=outs, in_specs=[VMEM_SPEC] * len(values)...  4.64 us
    pallas_call x1, Pallas kernels, local(): pl.pallas_call(functools.partial(last_kernel, corridor, tiles), out_shape...  1.54 us
    pallas_call x1, Pallas kernels, local(): pl.pallas_call(load_kernel, out_shape=[field] * 4 + [pltpu.VMEM((rows, co...  1.44 us
    pallas_call x1, Pallas kernels, local(): pl.pallas_call(pack_kernel, out_shape=[wide, pair], in_specs=[HBM_SPEC] *...  1.24 us
    add x1, other arithmetic, local(): river_section = own_term.reshape(owned) + from_other + from_partner  0.52 us
  transfers between devices with their start and end apart: 7, of which 0 were waited for; matrix products, arithmetic and copies ran while one was open for 0% of the time, Pallas kernels for 33%

profile of v9, /device:TPU:1, one launch (start us, length us, event | category | flops | bytes accessed | tf_op | source)
XLA Modules:
  0.0 20.4 jit_solution(3112720213990467963)
XLA Ops:
  0.6 0.1 collective-permute-start.1
  0.8 0.5 %collective-permute-start = (f32[128]{0:T(128)}, f32[128]{0:T(128)S(1)}, u32[]{:S(2)}, u32[]{:S(2)}) collective-permute-start(f32[128]{0:T(128)} %param.11), channel_id=1, source_target_pairs={{0,1},{1,0},{2,3},{3,2},{4,5},{5,4},{6,7},{7,6},{8,9},{9,8},{10,11... | collective-permute-start | bytes 1544 | tf_op jit(solution)/shard_map/ppermute | solution.py:37
  1.2 1.2 %pack.1 = (f32[61,4,128]{2,1,0:T(4,128)S(1)}, f32[2,128]{1,0:T(2,128)S(1)}) custom-call(f32[32,1920]{1,0:T(8,128)} %depth_in.1, f32[32,1920]{1,0:T(8,128)} %bed_in.1, s32[32,1920]{1,0:T(8,128)} %rough_in.1, f32[32,1920]{1,0:T(8,128)} %east_in.1, f32[32,1920]{1,0:T(8,128)} %south_in.1, f32[1,128]{1,0:T(1,128)} %bitcast.15, s32[4,128]{1,0:T(4,128)} %cells.1, ...), custom_call_target="tpu_custom_call" | custom-call | tf_op jit(solution)/shard_map/pack/pallas_call | solution.py:738
  2.5 0.0 collective-permute-done
  2.5 0.0 collective-permute-done.1.cells.partner_cells
  2.5 4.5 %collective-permute-start.2 = (f32[61,4,128]{2,1,0:T(4,128)S(1)}, f32[61,4,128]{2,1,0:T(4,128)S(1)}, u32[]{:S(2)}, u32[]{:S(2)}) collective-permute-start(f32[61,4,128]{2,1,0:T(4,128)S(1)} %join.1), channel_id=1, source_target_pairs={{1,2},{2,1},{3,4},{4,3},{5,6},{6,5},{7,8},{8,7},{9,10},{10,9},{11,... | collective-permute-start | bytes 374792 | tf_op jit(solution)/shard_map/ppermute | solution.py:37
  7.0 1.4 %load.1 = (f32[40,1920]{1,0:T(8,128)S(1)}, f32[40,1920]{1,0:T(8,128)S(1)}, f32[40,1920]{1,0:T(8,128)S(1)}, f32[40,1920]{1,0:T(8,128)S(1)}, s32[32,1920]{1,0:T(8,128)S(1)}, /*index=5*/f32[8,128]{1,0:T(8,128)S(1)}) custom-call(f32[32,1920]{1,0:T(8,128)} %depth_in.1, f32[32,1920]{1,0:T(8,128)} %east_in.1, f32[32,1920]{1,0:T(8,128)} %south_in.1, ...), custom_call_target="tpu_custom_call" | custom-call | tf_op jit(solution)/shard_map/load/pallas_call | solution.py:766
  8.5 0.7 %prepare.1 = (f32[40,1920]{1,0:T(8,128)S(1)}, f32[40,1920]{1,0:T(8,128)S(1)}, f32[40,1920]{1,0:T(8,128)S(1)}, f32[40,1920]{1,0:T(8,128)S(1)}, f32[40,1920]{1,0:T...) custom-call(f32[8,128]{1,0:T(8,128)S(1)} %get-tuple-element.73.table, ...), custom_call_target="tpu_custom_call", output_to_operand_aliasing={{0}: (2, {}), {1}: (3, {}), {2}: (4, {}), {3}: (5, {})} | custom-call | tf_op jit(solution)/shard_map/prepare/pallas_call | solution.py:718
  9.2 0.1 collective-permute-start.4
  9.2 0.5 %nodes.1 = (f32[40,1920]{1,0:T(8,128)S(1)}, f32[40,1920]{1,0:T(8,128)S(1)}, bf16[2,256,512]{2,1,0:T(8,128)(2,1)S(1)}, f32[2,256,128]{2,1,0:T(8,128)S(1)}, f32[32...) custom-call(f32[40,1920]{1,0:T(8,128)S(1)} %get-tuple-element.79.surf.refs_0_, f32[2,128]{1,0:T(2,128)S(1)} %get-tuple-element.80.own.refs_7_, ...), custom_call_target="tpu_custom_call" | custom-call | tf_op jit(solution)/shard_map/nodes/pallas_call | solution.py:718
  9.8 0.0 collective-permute-done.2.by_other
  9.8 0.6 %collective-permute-start.3 = (f32[2,128]{1,0:T(2,128)S(1)}, f32[2,128]{1,0:T(2,128)S(1)}, u32[]{:S(2)}, u32[]{:S(2)}) collective-permute-start(f32[2,128]{1,0:T(2,128)S(1)} %get-tuple-element.85.near), channel_id=1, source_target_pairs={{0,1},{1,0},{2,3},{3,2},{4,5},{5,4},{6,7},{7,6},{8,9},{9,8},{10,11... | collective-permute-start | bytes 3080 | tf_op jit(solution)/shard_map/ppermute | solution.py:37
  10.4 0.3 %near.1 = (f32[40,1920]{1,0:T(8,128)S(1)}, f32[40,1920]{1,0:T(8,128)S(1)}, bf16[2,128,512]{2,1,0:T(8,128)(2,1)S(1)}, f32[2,128,128]{2,1,0:T(8,128)S(1)}) custom-call(f32[2,128]{1,0:T(2,128)S(1)} %get-tuple-element.85.near, f32[40,1920]{1,0:T(8,128)S(1)} %get-tuple-element.103.refs_0_, ...), custom_call_target="tpu_custom_call", output_to_operand_aliasing={{0}: (1, {}), {1}: (2, {}), {2}: (3, {}), {3}: (4, {})} | custom-call | tf_op jit(solution)/shard_map/near/pallas_call | solution.py:718
  10.8 0.0 collective-permute-done.4.by_partner
  10.8 0.3 %border.1 = (f32[40,1920]{1,0:T(8,128)S(1)}, f32[40,1920]{1,0:T(8,128)S(1)}, f32[40,1920]{1,0:T(8,128)S(1)}, f32[40,1920]{1,0:T(8,128)S(1)}, f32[40,1920]{1,0:T(...) custom-call(f32[60,4,128]{2,1,0:T(4,128)S(1)} %collective-permute-do, ...), custom_call_target="tpu_custom_call", output_to_operand_aliasing={{0}: (3, {}), {1}: (4, {}), {2}: (5, {}), {3}: (6, {}), {4}... | custom-call | tf_op jit(solution)/shard_map/border/pallas_call | solution.py:718
  11.1 0.6 %first.1 = (f32[40,1920]{1,0:T(8,128)S(1)}, f32[40,1920]{1,0:T(8,128)S(1)}, f32[40,1920]{1,0:T(8,128)S(1)}, f32[40,1920]{1,0:T(8,128)S(1)}, f32[40,1920]{1,0:T(8...) custom-call(f32[40,1920]{1,0:T(8,128)S(1)} %get-tuple-element.96.surf, f32[40,1920]{1,0:T(8,128)S(1)} %get-tuple-element.97.east, ...), custom_call_target="tpu_custom_call" | custom-call | tf_op jit(solution)/shard_map/first/pallas_call | solution.py:718
  11.6 0.0 collective-permute-done.3.far
  11.6 0.9 %second.1 = (f32[40,1920]{1,0:T(8,128)S(1)}, f32[40,1920]{1,0:T(8,128)S(1)}, f32[40,1920]{1,0:T(8,128)S(1)}, f32[40,1920]{1,0:T(8,128)S(1)}, f32[40,1920]{1,0:T(...) custom-call(f32[2,128]{1,0:T(2,128)S(1)} %collective-permute-done.3., ...), custom_call_target="tpu_custom_call", output_to_operand_aliasing={{0}: (12, {}), {1}: (13, {}), {2}: (14, {}), {3}: (15, {}),... | custom-call | tf_op jit(solution)/shard_map/second/pallas_call | solution.py:718
  12.6 1.3 %third.1 = (f32[40,1920]{1,0:T(8,128)S(1)}, f32[40,1920]{1,0:T(8,128)S(1)}, f32[40,1920]{1,0:T(8,128)S(1)}, f32[1,128]{1,0:T(1,128)S(1)}, f32[1,128]{1,0:T(1,128...) custom-call(f32[40,1920]{1,0:T(8,128)S(1)} %get-tuple-element.117.surf.refs_0_, ...), custom_call_target="tpu_custom_call" | custom-call | tf_op jit(solution)/shard_map/third/pallas_call | solution.py:718
  13.8 4.4 %collective-permute-start.5 = (f32[128]{0:T(128)S(1)}, f32[128]{0:T(128)S(1)}, u32[]{:S(2)}, u32[]{:S(2)}) collective-permute-start(f32[128]{0:T(128)S(1)} %bitcast.12), channel_id=1, source_target_pairs={{1,2},{2,1},{3,4},{4,3},{5,6},{6,5},{7,8},{8,7},{9,10},{10,9},{11,... | collective-permute-start | bytes 1544 | tf_op jit(solution)/shard_map/ppermute | solution.py:37
  18.2 0.1 collective-permute-start.6
  18.3 1.5 %last.1 = (f32[40,1920]{1,0:T(8,128)S(1)}, f32[32,1920]{1,0:T(8,128)}, f32[32,1920]{1,0:T(8,128)}, f32[32,1920]{1,0:T(8,128)}) custom-call(f32[40,1920]{1,0:T(8,128)S(1)} %get-tuple-element.117.surf.refs_0_, f32[40,1920]{1,0:T(8,128)S(1)} %get-tuple-element.118.east.refs_1_, ...), custom_call_target="tpu_custom_call", output_to_operand_aliasing={{0}: (11, {}), {1}: (13, {}), {2}: (14, {}), {3}: (15, {})} | custom-call | tf_op jit(solution)/shard_map/last/pallas_call | solution.py:850
  19.8 0.0 collective-permute-done.5
  19.8 0.0 collective-permute-done.6
  19.9 0.5 %fusion = f32[128]{0:T(128)} fusion(f32[128]{0:T(128)S(1)} %collective-permute-done.6, f32[128]{0:T(128)S(1)} %collective-permute-done.5, f32[1,128]{1,0:T(1,128)S(1)} %get-tuple-element.137), kind=kLoop, calls=%fused_computation.1 | loop fusion | flops 256 | bytes 2048 | tf_op jit(solution)/shard_map/add | solution.py:860
  (3 shorter events, 0.0 us)
Async XLA Ops:
  0.6 1.8 %collective-permute-start.1 = (s32[4,128]{1,0:T(4,128)}, s32[4,128]{1,0:T(4,128)S(1)}, u32[]{:S(2)}, u32[]{:S(2)}) collective-permute-start(s32[4,128]{1,0:T(4,128)} %cells.1), channel_id=1, source_target_pairs={{0,1},{1,0},{2,3},{3,2},{4,5},{5,4},{6,7},{7,6},{8,9},{9,8},{10,11... | collective-permute-start | bytes 6152 | tf_op jit(solution)/shard_map/ppermute | solution.py:37
  0.8 1.7 %collective-permute-start = (f32[128]{0:T(128)}, f32[128]{0:T(128)S(1)}, u32[]{:S(2)}, u32[]{:S(2)}) collective-permute-start(f32[128]{0:T(128)} %param.11), channel_id=1, source_target_pairs={{0,1},{1,0},{2,3},{3,2},{4,5},{5,4},{6,7},{7,6},{8,9},{9,8},{10,11... | collective-permute-start | bytes 1544 | tf_op jit(solution)/shard_map/ppermute | solution.py:37
  2.5 7.3 %collective-permute-start.2 = (f32[61,4,128]{2,1,0:T(4,128)S(1)}, f32[61,4,128]{2,1,0:T(4,128)S(1)}, u32[]{:S(2)}, u32[]{:S(2)}) collective-permute-start(f32[61,4,128]{2,1,0:T(4,128)S(1)} %join.1), channel_id=1, source_target_pairs={{1,2},{2,1},{3,4},{4,3},{5,6},{6,5},{7,8},{8,7},{9,10},{10,9},{11,... | collective-permute-start | bytes 374792 | tf_op jit(solution)/shard_map/ppermute | solution.py:37
  9.2 1.6 %collective-permute-start.4 = (f32[60,4,128]{2,1,0:T(4,128)S(1)}, f32[60,4,128]{2,1,0:T(4,128)S(1)}, u32[]{:S(2)}, u32[]{:S(2)}) collective-permute-start(f32[60,4,128]{2,1,0:T(4,128)S(1)} %get-tuple-element.87), channel_id=1, source_target_pairs={{0,1},{1,0},{2,3},{3,2},{4,5},{5,4},{6,7},{7,6},{8,9},{9,8},{10,11... | collective-permute-start | bytes 368648 | tf_op jit(solution)/shard_map/ppermute | solution.py:37
  9.8 1.8 %collective-permute-start.3 = (f32[2,128]{1,0:T(2,128)S(1)}, f32[2,128]{1,0:T(2,128)S(1)}, u32[]{:S(2)}, u32[]{:S(2)}) collective-permute-start(f32[2,128]{1,0:T(2,128)S(1)} %get-tuple-element.85.near), channel_id=1, source_target_pairs={{0,1},{1,0},{2,3},{3,2},{4,5},{5,4},{6,7},{7,6},{8,9},{9,8},{10,11... | collective-permute-start | bytes 3080 | tf_op jit(solution)/shard_map/ppermute | solution.py:37
  13.8 6.0 %collective-permute-start.5 = (f32[128]{0:T(128)S(1)}, f32[128]{0:T(128)S(1)}, u32[]{:S(2)}, u32[]{:S(2)}) collective-permute-start(f32[128]{0:T(128)S(1)} %bitcast.12), channel_id=1, source_target_pairs={{1,2},{2,1},{3,4},{4,3},{5,6},{6,5},{7,8},{8,7},{9,10},{10,9},{11,... | collective-permute-start | bytes 1544 | tf_op jit(solution)/shard_map/ppermute | solution.py:37
  18.2 1.6 %collective-permute-start.6 = (f32[128]{0:T(128)S(1)}, f32[128]{0:T(128)S(1)}, u32[]{:S(2)}, u32[]{:S(2)}) collective-permute-start(f32[128]{0:T(128)S(1)} %bitcast.11), channel_id=1, source_target_pairs={{0,1},{1,0},{2,3},{3,2},{4,5},{5,4},{6,7},{7,6},{8,9},{9,8},{10,11... | collective-permute-start | bytes 1544 | tf_op jit(solution)/shard_map/ppermute | solution.py:37
